TPU v7x, 32 devices: a whole 2x2x4 slice. The times are simulated.
32 devices in a mesh: groups: 2 (over x), seq: 16 (over z, y, core).
Axes of the slice: x: 2, y: 2, z: 4, core: 2. Of those that a mesh axis runs over, the one named last changes fastest.
Arguments:
- queries: bfloat16 [16384, 2048], P(('groups', 'seq')), parts along dimension 0, may hold values from -10 to 10
- keys: bfloat16 [16384, 2048], P(('groups', 'seq')), parts along dimension 0, may hold values from -10 to 10
- values: bfloat16 [16384, 2048], P(('groups', 'seq')), parts along dimension 0, may hold values from -6 to 6
- ssd_input: bfloat16 [16384, 2048], P(('groups', 'seq')), parts along dimension 0, may hold values from -6 to 6
- bmat: bfloat16 [16384, 128], P(('groups', 'seq')), parts along dimension 0, may hold values from -0.5 to 0.5
- cmat: bfloat16 [16384, 128], P(('groups', 'seq')), parts along dimension 0, may hold values from -6 to 6
- expo: int32 [16384, 32], P(('groups', 'seq')), parts along dimension 0, may hold values from 1 to 16384
- rate: float32 [32], replicated, may hold values from 1.2207031e-05 to 0.06
- skip: float32 [32], replicated, may hold values from 0.5 to 1.5
Outputs:
- attn_out: bfloat16 [16384, 2048], P(('groups', 'seq')), parts along dimension 0
- normed_recurrence_output: bfloat16 [16384, 2048], P(('groups', 'seq')), parts along dimension 0
There are 2 independent parts, one for each index of `groups`. A program takes and returns all parts, laid end to end along the dimension named above; an argument that names none is the same for every part. Nothing has to cross between parts.
All inputs are finite; a program needn't handle non-finite values.
Results may differ from a plain program's by a relative error of at most 0.0049.
Values may be sent and summed in bfloat16 or wider, within the bound.
No kernel may reach another device: no remote copies, remote signals or barrier semaphores. Data moves between devices by JAX's collectives and lax.ppermute only.
A program may use at most 192 MiB of HBM per device.

v0:
```python
import math

import jax
import jax.numpy as jnp
from jax import lax
from jax.sharding import PartitionSpec as P

E = 128
W = 2048
Q = 256


def passed_along(block, axis, distance):
    devices = range(lax.axis_size(axis))
    route = [(i - distance, i) for i in devices if i - distance in devices]
    return lax.ppermute(block, axis, route)


def entering_2(shard, axis, combine, identity):
    peers, here = (lax.axis_size(axis), lax.axis_index(axis))
    everything = jax.tree.map(lambda part: lax.all_gather(part, axis), shard)
    start = jax.tree.map(
        lambda part, zero: jnp.broadcast_to(jnp.asarray(zero, part.dtype), part.shape),
        shard,
        identity,
    )

    def hop(k, before):
        reached = k < here
        new = combine(before, jax.tree.map(lambda part: part[k], everything))
        return jax.tree.map(lambda a, b: jnp.where(reached, a, b), new, before)

    return lax.fori_loop(0, peers, hop, start)


def block_local(piece_x, piece_b, piece_c, piece_loga):
    cumulative = jnp.cumsum(piece_loga, axis=0).T
    block_len = cumulative.shape[1]
    lower_mask = jnp.arange(block_len)[:, None] >= jnp.arange(block_len)[None, :]
    log_gaps = cumulative[:, :, None] - cumulative[:, None, :]
    decay_grid = jnp.where(
        lower_mask[None], jnp.exp(jnp.where(lower_mask[None], log_gaps, 0.0)), 0.0
    )
    cross_term = jnp.dot(piece_c, piece_b.T, preferred_element_type=jnp.float32)
    inner_term = (cross_term[None] * decay_grid).astype(jnp.bfloat16)
    intra_term = jnp.einsum("hts,shp->thp", inner_term, piece_x, preferred_element_type=jnp.float32)
    end_weights = jnp.exp(cumulative[:, -1:] - cumulative)
    weighted = (end_weights.T[:, :, None] * piece_b.astype(jnp.float32)[:, None, :]).astype(
        jnp.bfloat16
    )
    local_state = jnp.einsum("shp,shn->hpn", piece_x, weighted, preferred_element_type=jnp.float32)
    end_decay = jnp.exp(cumulative[:, -1])
    return (intra_term, cumulative, end_decay, local_state)


def block_output(intra_term, cumulative, piece_x, piece_c, skip, carried):
    inter_term = jnp.einsum(
        "tn,hpn->thp",
        piece_c.astype(jnp.float32),
        carried,
        precision=lax.Precision.HIGHEST,
        preferred_element_type=jnp.float32,
    )
    mixed = (
        intra_term
        + inter_term * jnp.exp(cumulative.T)[:, :, None]
        + skip[None, :, None] * piece_x.astype(jnp.float32)
    )
    inv_rms = lax.rsqrt(jnp.mean(mixed * mixed, axis=2, keepdims=True) + 1e-05)
    return (
        (mixed * inv_rms)
        .astype(jnp.bfloat16)
        .reshape(mixed.shape[0], mixed.shape[1] * mixed.shape[2])
    )


def window_attention(queries, keys_all, values_all, first_pos):
    length = queries.shape[0]
    row_width = queries.shape[1]
    head_count = row_width // E
    group_size = math.gcd(head_count, 4)
    group_cols = group_size * E
    block_rows = min(length, 512)
    query_pos = first_pos + 0 + jnp.arange(block_rows, dtype=jnp.int32)
    key_pos = first_pos - W + 0 + jnp.arange(block_rows + W, dtype=jnp.int32)
    visible = (
        (key_pos[None, :] <= query_pos[:, None])
        & (key_pos[None, :] > query_pos[:, None] - W)
        & (key_pos[None, :] >= 0)
    )

    def one_group(group_index, result):
        column = group_index * group_cols
        query_group = lax.dynamic_slice_in_dim(queries, column, group_cols, 1).reshape(
            block_rows, group_size, E
        )
        key_group = lax.dynamic_slice_in_dim(keys_all, column, group_cols, 1).reshape(
            block_rows + W, group_size, E
        )
        value_group = lax.dynamic_slice_in_dim(values_all, column, group_cols, 1).reshape(
            block_rows + W, group_size, E
        )
        scores = jnp.einsum(
            "rge,kge->grk", query_group, key_group, preferred_element_type=jnp.float32
        ) / math.sqrt(E)
        scores = jnp.where(visible[None], scores, -1e30)
        row_max = jnp.max(scores, axis=2, keepdims=True)
        exp_scores = jnp.exp(scores - row_max)
        attn_probs = (exp_scores / jnp.sum(exp_scores, axis=2, keepdims=True)).astype(jnp.bfloat16)
        group_out = jnp.einsum(
            "grk,kge->rge", attn_probs, value_group, preferred_element_type=jnp.float32
        )
        group_out = group_out.reshape(block_rows, group_cols).astype(jnp.bfloat16)
        return lax.dynamic_update_slice_in_dim(result, group_out, column, 1)

    results = lax.fori_loop(
        0, head_count // group_size, one_group, jnp.zeros((block_rows, row_width), jnp.bfloat16)
    )
    return results


def on_device(queries, keys, values, ssd_input, bmat, cmat, expo, rate, skip):
    length = queries.shape[0]
    first_pos = lax.axis_index("seq") * length
    kv_pair = jnp.stack([keys, values])
    span_shards = W // length
    relayed = kv_pair
    earlier = []
    for distance in range(span_shards):
        relayed = passed_along(relayed, "seq", 1)
        earlier.insert(0, relayed)
    joined = jnp.concatenate(earlier + [kv_pair], axis=1)
    attn_out = window_attention(queries, joined[0], joined[1], first_pos)
    head_count = rate.shape[0]
    head_dim = ssd_input.shape[1] // head_count
    state_size = cmat.shape[1]
    block_count = length // Q
    all_x = ssd_input.reshape(length, head_count, head_dim)
    all_loga = -rate[None, :] * expo.astype(jnp.float32)
    locals_list = []
    dev_decay = jnp.ones((head_count,), jnp.float32)
    dev_state = jnp.zeros((head_count, head_dim, state_size), jnp.float32)
    for block_index in range(block_count):
        lower = block_index * Q
        parts_now = block_local(
            all_x[lower : lower + Q],
            bmat[lower : lower + Q],
            cmat[lower : lower + Q],
            all_loga[lower : lower + Q],
        )
        locals_list.append(parts_now)
        dev_state = parts_now[2][:, None, None] * dev_state + parts_now[3]
        dev_decay = dev_decay * parts_now[2]

    def link(earlier_pair, later_pair):
        return (
            earlier_pair[0] * later_pair[0],
            later_pair[0][:, None, None] * earlier_pair[1] + later_pair[1],
        )

    identity = (
        jnp.ones((head_count,), jnp.float32),
        jnp.zeros((head_count, head_dim, state_size), jnp.float32),
    )
    entering = entering_2((dev_decay, dev_state), "seq", link, identity)
    carried = entering[1]
    outputs = []
    for block_index in range(block_count):
        lower = block_index * Q
        intra_term, cumulative, end_decay, local_state = locals_list[block_index]
        outputs.append(
            block_output(
                intra_term,
                cumulative,
                all_x[lower : lower + Q],
                cmat[lower : lower + Q],
                skip,
                carried,
            )
        )
        carried = end_decay[:, None, None] * carried + local_state
    normed_recurrence_output = jnp.concatenate(outputs, axis=0)
    return (attn_out, normed_recurrence_output)


def solution(mesh):
    placed = (
        P(("groups", "seq"), None),
        P(("groups", "seq"), None),
        P(("groups", "seq"), None),
        P(("groups", "seq"), None),
        P(("groups", "seq"), None),
        P(("groups", "seq"), None),
        P(("groups", "seq"), None),
        P(),
        P(),
    )
    return jax.shard_map(
        on_device,
        mesh=mesh,
        in_specs=placed,
        out_specs=(P(("groups", "seq"), None), P(("groups", "seq"), None)),
        check_vma=False,
    )
```

profile of v0, /device:TPU:17, one launch (start us, length us, event | category | flops | bytes accessed | tf_op | source)
XLA Modules:
  0.0 587.4 jit_solution(17286876546489918469)
XLA Ops:
  9.9 3.7 collective-permute-start
  13.6 45.4 %collective-permute-done = bf16[2,512,2048]{2,1,0:T(8,128)(2,1)S(1)} collective-permute-done((bf16[2,512,2048]{2,1,0:T(8,128)(2,1)S(1)}, bf16[2,512,2048]{2,1,0:T(8,128)(2,1)S(1)}, u32[]{:S(2)}, u32[]{:S(2)}) %collective-permute-start) | collective-permute-done | bytes 4194336 | tf_op jit(solution)/shard_map/ppermute | solution.py:16
  61.0 4.4 collective-permute-start.1
  65.3 45.4 %collective-permute-done.1 = bf16[2,512,2048]{2,1,0:T(8,128)(2,1)} collective-permute-done((bf16[2,512,2048]{2,1,0:T(8,128)(2,1)S(1)}, bf16[2,512,2048]{2,1,0:T(8,128)(2,1)}, u32[]{:S(2)}, u32[]{:S(2)}) %collective-permute-start.1) | collective-permute-done | bytes 4194336 | tf_op jit(solution)/shard_map/ppermute | solution.py:16
  110.8 4.5 collective-permute-start.2
  124.1 36.9 %collective-permute-done.2 = bf16[2,512,2048]{2,1,0:T(8,128)(2,1)} collective-permute-done((bf16[2,512,2048]{2,1,0:T(8,128)(2,1)}, bf16[2,512,2048]{2,1,0:T(8,128)(2,1)}, u32[]{:S(2)}, u32[]{:S(2)}) %collective-permute-start.2) | collective-permute-done | bytes 4194336 | tf_op jit(solution)/shard_map/ppermute | solution.py:16
  161.0 4.4 collective-permute-start.3
  169.5 141.4 %all-reduce = f32[512]{0:T(512)S(1)} all-reduce(f32[512]{0:T(512)S(1)} %dynamic-update-slice), channel_id=2, replica_groups=mesh['groups'=2,'seq'=16] {'seq'}, use_global_device_ids=true, to_apply=%add | all-reduce | flops 512 | bytes 4096
  314.0 2.8 constant_dynamic-update-slice_fusion.5
  319.3 2.9 constant_dynamic-update-slice_fusion.3
  325.7 7.4 %slice_bitcast_fusion = (bf16[2560,2048]{1,0:T(8,128)(2,1)}, bf16[2560,2048]{1,0:T(8,128)(2,1)}) fusion(bf16[2,2560,2048]{2,1,0:T(8,128)(2,1)S(1)} %constant_dynamic-update-slice_fusion.1), kind=kLoop, calls=%fused_computation.22 | loop fusion | bytes 41943040 | tf_op jit(solution)/shard_map/squeeze | solution.py:133
  334.7 174.4 %while.28 = (s32[]{:T(128)}, bf16[512,2048]{1,0:T(8,128)(2,1)}, bf16[2560,2048]{1,0:T(8,128)(2,1)}, bf16[512,2048]{1,0:T(8,128)(2,1)}, bf16[2560,2048]{1,0:T(8,1...) while((s32[]{:T(128)}, bf16[512,2048]{1,0:T(8,128)(2,1)}, ...), condition=%wide.region_3.4_spmd.clone, body=%wide.region_0.3_spmd.clone.sunk | while | flops 2721319424 | bytes 76055216 | solution.py:116
  334.7 4.4 constant_dynamic-slice_fusion.5
  339.1 4.4 copy.97
  345.6 3.6 and_and_fusion.2
  349.2 13.8 %fusion.78 = (f32[4,512]{1,0:T(4,128)S(1)}, f32[4,512,2560]{2,1,0:T(8,128)}) fusion(pred[512,2560]{1,0:T(8,128)(4,1)} %and_and_fusion.2, bf16[512,4,128]{0,2,1:T(8,128)(2,1)} %bitcast.120, bf16[2560,4,128]{0,2,1:T(8,128)(2,1)} %bitcast.118), kind=kOutput, calls=%fused_computation.111.clone.1 | convolution fusion | flops 1363151360 | bytes 25436160 | tf_op jit(solution)/shard_map/while/body/eval_jaxpr/sub | solution.py:108
  363.0 2.8 copy.95
  365.8 11.4 %fusion.79 = bf16[4,128,512]{2,1,0:T(8,128)(2,1)S(1)} fusion(bf16[2560,4,128]{0,2,1:T(8,128)(2,1)} %bitcast.119, f32[4,512,2560]{2,1,0:T(8,128)} %get-tuple-element.428, f32[4,512]{1,0:T(4,128)S(1)} %get-tuple-element.429), kind=kOutput, calls=%fused_computation.12.clone.1 | convolution fusion | flops 1352925184 | bytes 24125440 | tf_op jit(solution)/shard_map/while/body/eval_jaxpr/grk,kge->rge/dot_general | solution.py:110
  378.3 4.4 constant_dynamic-slice_fusion.5
  382.7 4.4 copy.97
  389.2 3.6 and_and_fusion.2
  392.8 13.8 %fusion.78 = (f32[4,512]{1,0:T(4,128)S(1)}, f32[4,512,2560]{2,1,0:T(8,128)}) fusion(pred[512,2560]{1,0:T(8,128)(4,1)} %and_and_fusion.2, bf16[512,4,128]{0,2,1:T(8,128)(2,1)} %bitcast.120, bf16[2560,4,128]{0,2,1:T(8,128)(2,1)} %bitcast.118), kind=kOutput, calls=%fused_computation.111.clone.1 | convolution fusion | flops 1363151360 | bytes 25436160 | tf_op jit(solution)/shard_map/while/body/eval_jaxpr/sub | solution.py:108
  406.6 2.8 copy.95
  409.4 11.4 %fusion.79 = bf16[4,128,512]{2,1,0:T(8,128)(2,1)S(1)} fusion(bf16[2560,4,128]{0,2,1:T(8,128)(2,1)} %bitcast.119, f32[4,512,2560]{2,1,0:T(8,128)} %get-tuple-element.428, f32[4,512]{1,0:T(4,128)S(1)} %get-tuple-element.429), kind=kOutput, calls=%fused_computation.12.clone.1 | convolution fusion | flops 1352925184 | bytes 24125440 | tf_op jit(solution)/shard_map/while/body/eval_jaxpr/grk,kge->rge/dot_general | solution.py:110
  421.9 4.4 constant_dynamic-slice_fusion.5
  426.3 4.4 copy.97
  432.8 3.6 and_and_fusion.2
  436.4 13.8 %fusion.78 = (f32[4,512]{1,0:T(4,128)S(1)}, f32[4,512,2560]{2,1,0:T(8,128)}) fusion(pred[512,2560]{1,0:T(8,128)(4,1)} %and_and_fusion.2, bf16[512,4,128]{0,2,1:T(8,128)(2,1)} %bitcast.120, bf16[2560,4,128]{0,2,1:T(8,128)(2,1)} %bitcast.118), kind=kOutput, calls=%fused_computation.111.clone.1 | convolution fusion | flops 1363151360 | bytes 25436160 | tf_op jit(solution)/shard_map/while/body/eval_jaxpr/sub | solution.py:108
  450.2 2.8 copy.95
  453.0 11.4 %fusion.79 = bf16[4,128,512]{2,1,0:T(8,128)(2,1)S(1)} fusion(bf16[2560,4,128]{0,2,1:T(8,128)(2,1)} %bitcast.119, f32[4,512,2560]{2,1,0:T(8,128)} %get-tuple-element.428, f32[4,512]{1,0:T(4,128)S(1)} %get-tuple-element.429), kind=kOutput, calls=%fused_computation.12.clone.1 | convolution fusion | flops 1352925184 | bytes 24125440 | tf_op jit(solution)/shard_map/while/body/eval_jaxpr/grk,kge->rge/dot_general | solution.py:110
  465.5 4.4 constant_dynamic-slice_fusion.5
  469.9 4.4 copy.97
  476.4 3.6 and_and_fusion.2
  480.0 13.8 %fusion.78 = (f32[4,512]{1,0:T(4,128)S(1)}, f32[4,512,2560]{2,1,0:T(8,128)}) fusion(pred[512,2560]{1,0:T(8,128)(4,1)} %and_and_fusion.2, bf16[512,4,128]{0,2,1:T(8,128)(2,1)} %bitcast.120, bf16[2560,4,128]{0,2,1:T(8,128)(2,1)} %bitcast.118), kind=kOutput, calls=%fused_computation.111.clone.1 | convolution fusion | flops 1363151360 | bytes 25436160 | tf_op jit(solution)/shard_map/while/body/eval_jaxpr/sub | solution.py:108
  493.8 2.8 copy.95
  496.6 11.4 %fusion.79 = bf16[4,128,512]{2,1,0:T(8,128)(2,1)S(1)} fusion(bf16[2560,4,128]{0,2,1:T(8,128)(2,1)} %bitcast.119, f32[4,512,2560]{2,1,0:T(8,128)} %get-tuple-element.428, f32[4,512]{1,0:T(4,128)S(1)} %get-tuple-element.429), kind=kOutput, calls=%fused_computation.12.clone.1 | convolution fusion | flops 1352925184 | bytes 24125440 | tf_op jit(solution)/shard_map/while/body/eval_jaxpr/grk,kge->rge/dot_general | solution.py:110
  509.1 54.3 %while.29 = (s32[]{:T(128)}, f32[32,64,128]{2,1,0:T(8,128)}, s32[]{:T(128)}, f32[16,32]{1,0:T(8,128)}, f32[16,32,64,128]{3,2,1,0:T(8,128)}, /*index=5*/s32[]{:T(128)}, s32[]{:T(128)}) while((s32[]{:T(128)}, f32[32,64,128]{2,1,0:T(8,128)}, s32[]{:T(128)}, f32[16,32]{1,0:T(8,128)}, f32[16,32,64,128]{3,2,1,0:T(8,128)}, ...), condition=%wide.region_9.10_spmd.clone, body=%wide.region_8.9_spmd.clone.sunk | while | flops 1048580 | bytes 3146217 | solution.py:33
  513.2 2.7 fusion.80
  516.6 2.7 fusion.80
  520.0 2.7 fusion.80
  523.4 2.7 fusion.80
  526.8 2.7 fusion.80
  536.9 2.7 fusion.80
  543.7 2.7 fusion.80
  547.1 2.7 fusion.80
  563.5 3.6 fusion.44
  569.4 2.7 multiply_reduce_fusion
  573.5 4.6 multiply_reduce_fusion.1
  (147 shorter events, 78.4 us)
Async XLA Ops:
  7.2 501.9 %all-gather.4.cloned.1.call-start = ((), (), s32[]{:S(2)}) async-start(), calls=%async_computation | async-start | bytes 17825792 | tf_op jit(solution)/shard_map/all_gather | solution.py:21
  7.2 108.0 %copy-start.24 = (f32[32]{0:T(128)S(1)}, f32[32]{0:T(128)}, u32[]{:S(2)}) copy-start(f32[32]{0:T(128)} %param.20) | copy-start | bytes 388
  7.2 108.1 %copy-start.19 = (s32[512,32]{0,1:T(8,128)S(1)}, s32[512,32]{0,1:T(8,128)}, u32[]{:S(2)}) copy-start(s32[512,32]{0,1:T(8,128)} %param.19) | copy-start | bytes 196612
  9.9 49.1 %collective-permute-start = (bf16[2,512,2048]{2,1,0:T(8,128)(2,1)S(1)}, bf16[2,512,2048]{2,1,0:T(8,128)(2,1)S(1)}, u32[]{:S(2)}, u32[]{:S(2)}) collective-permute-start(bf16[2,512,2048]{2,1,0:T(8,128)(2,1)S(1)} %pad_maximum_fusion), channel_id=1, source_target_pairs={{0,1},{1,2},{2,3},{3,4},{4,5},{5,6},{6,7},{7,8},{8,9},{9,10},{10,1... | collective-permute-start | bytes 12582920 | tf_op jit(solution)/shard_map/ppermute | solution.py:16
  59.0 1.9 copy-start.2
  61.0 49.8 %collective-permute-start.1 = (bf16[2,512,2048]{2,1,0:T(8,128)(2,1)S(1)}, bf16[2,512,2048]{2,1,0:T(8,128)(2,1)}, u32[]{:S(2)}, u32[]{:S(2)}) collective-permute-start(bf16[2,512,2048]{2,1,0:T(8,128)(2,1)S(1)} %collective-permute-done), channel_id=1, source_target_pairs={{0,1},{1,2},{2,3},{3,4},{4,5},{5,6},{6,7},{7,8},{8,9},{9,10},{10,1... | collective-permute-start | bytes 12582920 | tf_op jit(solution)/shard_map/ppermute | solution.py:16
  110.8 50.2 %collective-permute-start.2 = (bf16[2,512,2048]{2,1,0:T(8,128)(2,1)}, bf16[2,512,2048]{2,1,0:T(8,128)(2,1)}, u32[]{:S(2)}, u32[]{:S(2)}) collective-permute-start(bf16[2,512,2048]{2,1,0:T(8,128)(2,1)} %collective-permute-done.1), channel_id=1, source_target_pairs={{0,1},{1,2},{2,3},{3,4},{4,5},{5,6},{6,7},{7,8},{8,9},{9,10},{10,1... | collective-permute-start | bytes 12582920 | tf_op jit(solution)/shard_map/ppermute | solution.py:16
  117.0 5.6 copy-start.12
  119.2 48.7 %copy-start.6 = (bf16[256,2048]{0,1:T(8,128)(2,1)}, bf16[256,2048]{0,1:T(8,128)(2,1)S(1)}, u32[]{:S(2)}) copy-start(bf16[256,2048]{0,1:T(8,128)(2,1)S(1)} %copy.61) | copy-start | bytes 3145732
  119.3 0.7 copy-start.17
  119.4 0.8 copy-start.15
  120.7 193.3 %copy-start.8 = (bf16[256,2048]{0,1:T(8,128)(2,1)}, bf16[256,2048]{0,1:T(8,128)(2,1)S(1)}, u32[]{:S(2)}) copy-start(bf16[256,2048]{0,1:T(8,128)(2,1)S(1)} %copy.64) | copy-start | bytes 3145732
  120.7 47.3 %copy-start.26 = (u32[32]{0:T(128)S(1)}, u32[32]{0:T(128)}, u32[]{:S(2)}) copy-start(u32[32]{0:T(128)} %constant.106) | copy-start | bytes 388
  120.7 191.5 %copy-start.10 = (bf16[512,128]{1,0:T(8,128)(2,1)S(1)}, bf16[512,128]{1,0:T(8,128)(2,1)}, u32[]{:S(2)}) copy-start(bf16[512,128]{1,0:T(8,128)(2,1)} %param.18) | copy-start | bytes 393220
  124.1 41.3 %copy-start.4 = (f32[32,64,128]{2,1,0:T(8,128)}, f32[32,64,128]{2,1,0:T(8,128)S(1)}, u32[]{:S(2)}) copy-start(f32[32,64,128]{2,1,0:T(8,128)S(1)} %fusion.38) | copy-start | bytes 3145732
  161.0 153.0 %collective-permute-start.3 = (bf16[2,512,2048]{2,1,0:T(8,128)(2,1)}, bf16[2,512,2048]{2,1,0:T(8,128)(2,1)}, u32[]{:S(2)}, u32[]{:S(2)}) collective-permute-start(bf16[2,512,2048]{2,1,0:T(8,128)(2,1)} %collective-permute-done.2), channel_id=1, source_target_pairs={{0,1},{1,2},{2,3},{3,4},{4,5},{5,6},{6,7},{7,8},{8,9},{9,10},{10,1... | collective-permute-start | bytes 12582920 | tf_op jit(solution)/shard_map/ppermute | solution.py:16
  319.3 3.7 copy-start.3
  322.9 1.6 copy-start
  322.9 2.2 copy-start.1
  509.1 54.4 %copy-start.11 = (bf16[512,128]{1,0:T(8,128)(2,1)S(1)}, bf16[512,128]{1,0:T(8,128)(2,1)}, u32[]{:S(2)}) copy-start(bf16[512,128]{1,0:T(8,128)(2,1)} %param.18) | copy-start | bytes 393220
  509.1 58.0 %copy-start.5 = (f32[32,64,128]{2,1,0:T(8,128)S(1)}, f32[32,64,128]{2,1,0:T(8,128)}, u32[]{:S(2)}) copy-start(f32[32,64,128]{2,1,0:T(8,128)} %copy-done.4) | copy-start | bytes 3145732
  509.1 58.0 %copy-start.23 = (f32[32]{0:T(128)S(1)}, f32[32]{0:T(128)}, u32[]{:S(2)}) copy-start(f32[32]{0:T(128)} %get-tuple-element.331) | copy-start | bytes 388
  563.4 6.0 %copy-start.9 = (bf16[256,2048]{0,1:T(8,128)(2,1)S(1)}, bf16[256,2048]{0,1:T(8,128)(2,1)}, u32[]{:S(2)}) copy-start(bf16[256,2048]{0,1:T(8,128)(2,1)} %copy-done.8) | copy-start | bytes 3145732
  563.4 6.0 %copy-start.14 = (f32[256,256]{1,0:T(8,128)S(1)}, f32[256,256]{1,0:T(8,128)}, u32[]{:S(2)}) copy-start(f32[256,256]{1,0:T(8,128)} %fusion.47) | copy-start | bytes 786436
  563.4 6.0 %copy-start.18 = (f32[32,256]{1,0:T(8,128)S(1)}, f32[32,256]{1,0:T(8,128)}, u32[]{:S(2)}) copy-start(f32[32,256]{1,0:T(8,128)} %copy-done.17) | copy-start | bytes 98308
  563.4 6.0 %copy-start.20 = (pred[256,256]{1,0:T(8,128)(4,1)S(1)}, pred[256,256]{1,0:T(8,128)(4,1)}, u32[]{:S(2)}) copy-start(pred[256,256]{1,0:T(8,128)(4,1)} %iota_compare_fusion) | copy-start | bytes 196612
  563.4 6.0 %copy-start.22 = (f32[256,32]{0,1:T(8,128)S(1)}, f32[256,32]{0,1:T(8,128)}, u32[]{:S(2)}) copy-start(f32[256,32]{0,1:T(8,128)} %get-tuple-element.329) | copy-start | bytes 98308
  563.4 6.0 %copy-start.25 = (f32[32]{0:T(128)S(1)}, f32[32]{0:T(128)}, u32[]{:S(2)}) copy-start(f32[32]{0:T(128)} %param.21) | copy-start | bytes 388
  572.2 1.2 copy-start.7
  572.2 1.3 copy-start.13
  572.2 1.2 copy-start.16
  572.2 1.2 copy-start.21
Sparse Core Ops, SparseCore 0:
  168.1 154.6 all-gather.3
where the time goes:
time: 589 us; the launch traced here: 587 us
  blocking collectives  141 us (24%)
  waiting for transfers between devices  128 us (22%)
  matrix products  120 us (20%)
  local copies, waits for them, and re-layouts  98.8 us (17%)
  other arithmetic  67.1 us (11%)
  starting transfers between devices  17 us (3%)
  between operations  15.1 us (3%)
    unnamed x1, blocking collectives  141 us
    ppermute x4, waiting for transfers between devices, passed_along(): return lax.ppermute(block, axis, route)  128 us
    sub x4, matrix products, one_group(): exp_scores = jnp.exp(scores - row_max)  55.1 us
    dot_general x4, matrix products, one_group(): jnp.einsum('grk,kge->rge', attn_probs, value_group, preferred_element_typ...  45.7 us
    select_n x16, other arithmetic, hop(): return jax.tree.map(lambda a, b: jnp.where(reached, a, b), new, before)  43 us
    dynamic_slice x8, local copies, waits for them, and re-layouts, one_group(): lax.dynamic_slice_in_dim(keys_all, column, group_cols, 1)  35.2 us
    ppermute x4, starting transfers between devices, passed_along(): return lax.ppermute(block, axis, route)  16.9 us
    unnamed x62, local copies, waits for them, and re-layouts  14.8 us
  transfers between devices with their start and end apart: 5, of which 3 were waited for; matrix products, arithmetic and copies ran while one was open for 35% of the time, Pallas kernels for 0%

commit v1 on v0

v1 whole, which is shorter than its diff:
```python
import functools
import math

import jax
import jax.numpy as jnp
from jax import lax
from jax.experimental import pallas as pl
from jax.experimental.pallas import tpu as pltpu
from jax.sharding import PartitionSpec as P

E = 128
W = 2048
Q = 256
EPS = 1e-05
NEG = -1e30
CHUNK_HEADS = 2
VMEM = 48 * 1024 * 1024


def contract(a, b, dims):
    return lax.dot_general(a, b, (dims, ((), ())), preferred_element_type=jnp.float32)


def split_bf16(v, terms):
    parts = []
    for _ in range(terms):
        part = v.astype(jnp.bfloat16)
        parts.append(part)
        v = v - part.astype(jnp.float32)
    return parts


def attention_kernel(ok_ref, q_ref, ok0, ov0, zk, zv, yk, yv, ak, av, bk, bv, *rest):
    o_ref = rest[-1]
    rows = q_ref.shape[0]
    half = rows // 2
    scale = math.log2(math.e) / math.sqrt(E)
    row = lax.broadcasted_iota(jnp.int32, (half, half), 0)
    col = lax.broadcasted_iota(jnp.int32, (half, half), 1)
    lo, hi, whole = slice(0, half), slice(half, rows), slice(0, rows)
    for r in range(2):
        q = q_ref[r * half : (r + 1) * half, :]
        if r == 0:
            pieces = [
                (zk, zv, lo, col > row, 0),
                (zk, zv, hi, None, 0),
                (ok0, ov0, lo, col <= row, None),
            ]
        else:
            pieces = [
                (zk, zv, hi, col > row, 0),
                (ok0, ov0, lo, None, None),
                (ok0, ov0, hi, col <= row, None),
            ]
        pieces += [
            (ak, av, whole, None, 1),
            (yk, yv, whole, None, 2),
            (bk, bv, whole, None, 3),
        ]
        scores = []
        top = None
        for k_ref, _, part, mask, flag in pieces:
            s = contract(q, k_ref[part, :], ((1,), (1,)))
            if mask is not None:
                s = jnp.where(mask, s, NEG)
            m = jnp.max(s, axis=1, keepdims=True)
            if flag is not None:
                m = jnp.where(ok_ref[flag] > 0, m, NEG)
            top = m if top is None else jnp.maximum(top, m)
            scores.append(s)
        shift = top * (-scale)
        total = jnp.zeros((half, 1), jnp.float32)
        acc = jnp.zeros((half, E), jnp.float32)
        for s, (_, v_ref, part, mask, flag) in zip(scores, pieces):
            offset = shift
            if flag is not None:
                offset = jnp.where(ok_ref[flag] > 0, shift, NEG)
            p = jnp.exp2(s * scale + offset)
            total += jnp.sum(p, axis=1, keepdims=True)
            acc += contract(p.astype(jnp.bfloat16), v_ref[part, :], ((1,), (0,)))
        o_ref[r * half : (r + 1) * half, :] = (acc / total).astype(o_ref.dtype)


def attention_chunk(chunk, heads, flags, queries, keys, values, z, y, a, b, result):
    rows, width = queries.shape
    first = chunk * heads
    own = pl.BlockSpec((rows, E), lambda h: (0, first + h))
    key = pl.BlockSpec((rows, E), lambda h: (0, h))
    value = pl.BlockSpec((rows, E), lambda h: (0, heads + h))
    args = [flags, queries, keys, values, z, z, y, y, a, a, b, b]
    specs = [pl.BlockSpec(memory_space=pltpu.SMEM), own, own, own] + [key, value] * 4
    aliases = {}
    if result is not None:
        aliases = {len(args): 0}
        args.append(result)
        specs.append(pl.BlockSpec(memory_space=pl.ANY))
    seen = rows + W
    return pl.pallas_call(
        attention_kernel,
        grid=(heads,),
        in_specs=specs,
        out_specs=own,
        out_shape=jax.ShapeDtypeStruct((rows, width), jnp.bfloat16),
        input_output_aliases=aliases,
        compiler_params=pltpu.CompilerParams(vmem_limit_bytes=VMEM),
        cost_estimate=pl.CostEstimate(
            flops=heads * rows * seen * E * 8,
            bytes_accessed=heads * (2 * seen + 2 * rows) * E * 2,
            transcendentals=heads * rows * seen,
        ),
        name="attention",
    )(*args)


def running_expo(expo_ref):
    size = expo_ref.shape[0]
    expo = expo_ref[...]
    high = (expo >> 8).astype(jnp.float32).astype(jnp.bfloat16)
    low = (expo & 255).astype(jnp.float32).astype(jnp.bfloat16)
    row = lax.broadcasted_iota(jnp.int32, (size, size), 0)
    col = lax.broadcasted_iota(jnp.int32, (size, size), 1)
    lower = jnp.where(row >= col, 1.0, 0.0).astype(jnp.bfloat16)
    upper = jnp.where(row <= col, 1.0, 0.0).astype(jnp.bfloat16)
    down = contract(lower, high, ((1,), (0,))) * 256.0 + contract(lower, low, ((1,), (0,)))
    across = contract(high, upper, ((0,), (0,))) * 256.0 + contract(low, upper, ((0,), (0,)))
    return down, across


def pair_lanes(left, right, rows, dim):
    lane = lax.broadcasted_iota(jnp.int32, (rows, 2 * dim), 1)
    return jnp.where(lane < dim, left, right)


def states_kernel(dim, expo_ref, rate_ref, x_ref, b_ref, local_ref, total_ref, decay_ref):
    heads = expo_ref.shape[1]
    state = b_ref.shape[1]
    first = pl.program_id(0) == 0

    @pl.when(first)
    def _():
        total_ref[...] = jnp.zeros_like(total_ref)
        decay_ref[...] = jnp.ones_like(decay_ref)

    down, _ = running_expo(expo_ref)
    rate = rate_ref[...]
    end = down[-1:, :]
    weights = jnp.exp(rate * (down - end))
    end_decay = jnp.exp(-rate * end)
    b = b_ref[...].astype(jnp.float32)
    for pair in range(heads // 2):
        columns = slice(pair * 2 * dim, (pair + 1) * 2 * dim)
        x = x_ref[:, columns]
        made = []
        for h in (2 * pair, 2 * pair + 1):
            weighted = (weights[:, h : h + 1] * b).astype(jnp.bfloat16)
            made.append(contract(weighted, x, ((0,), (0,))))
        new = pair_lanes(made[0], made[1], state, dim)
        decay = pair_lanes(
            end_decay[:, 2 * pair : 2 * pair + 1],
            end_decay[:, 2 * pair + 1 : 2 * pair + 2],
            1,
            dim,
        )
        before = total_ref[:, columns]
        local_ref[:, columns] = before
        total_ref[:, columns] = before * decay + new
        decay_ref[:, columns] = decay_ref[:, columns] * decay


def intra_kernel(
    dim, expo_ref, rate_ref, rates_ref, skip_ref, x_ref, b_ref, c_ref, local_ref, pre_ref, factor_ref, past
):
    heads = expo_ref.shape[1]
    size = expo_ref.shape[0]
    half = size // 2

    @pl.when(pl.program_id(0) == 0)
    def _():
        past[...] = jnp.zeros_like(past)

    down, across = running_expo(expo_ref)
    rate = rate_ref[...]
    within = jnp.exp(-rate * down)
    factor_ref[...] = jnp.exp(-rate * (down + past[...]))
    past[...] = past[...] + down[-1:, :]
    c = c_ref[...]
    cross = contract(c, b_ref[...], ((1,), (1,)))
    row = lax.broadcasted_iota(jnp.int32, (half, half), 0)
    col = lax.broadcasted_iota(jnp.int32, (half, half), 1)
    seen = row >= col
    for pair in range(heads // 2):
        columns = slice(pair * 2 * dim, (pair + 1) * 2 * dim)
        x = x_ref[:, columns]
        xf = x.astype(jnp.float32)
        upper, lower = [], []
        for h in (2 * pair, 2 * pair + 1):
            r = rates_ref[h]
            here, there = down[:, h : h + 1], across[h : h + 1, :]
            gap = jnp.where(seen, (there[:, :half] - here[:half]) * r, NEG)
            inner = (cross[:half, :half] * jnp.exp(gap)).astype(jnp.bfloat16)
            upper.append(contract(inner, x[:half], ((1,), (0,))))
            gap = (there[:, :half] - here[half:]) * r
            inner_left = (cross[half:, :half] * jnp.exp(gap)).astype(jnp.bfloat16)
            gap = jnp.where(seen, (there[:, half:] - here[half:]) * r, NEG)
            inner_right = (cross[half:, half:] * jnp.exp(gap)).astype(jnp.bfloat16)
            inner = jnp.concatenate([inner_left, inner_right], axis=1)
            lower.append(contract(inner, x, ((1,), (0,))))
        intra = jnp.concatenate(
            [
                pair_lanes(upper[0], upper[1], half, dim),
                pair_lanes(lower[0], lower[1], half, dim),
            ],
            axis=0,
        )
        high, low = split_bf16(local_ref[:, columns], 2)
        carried = contract(c, high, ((1,), (0,))) + contract(c, low, ((1,), (0,)))
        decay = pair_lanes(
            within[:, 2 * pair : 2 * pair + 1], within[:, 2 * pair + 1 : 2 * pair + 2], size, dim
        )
        skip = pair_lanes(skip_ref[2 * pair], skip_ref[2 * pair + 1], 1, dim)
        pre_ref[:, columns] = intra + carried * decay + skip * xf


def final_kernel(dim, pre_ref, factor_ref, c_ref, entering_ref, o_ref):
    heads = factor_ref.shape[1]
    size = pre_ref.shape[0]
    c = c_ref[...]
    row = lax.broadcasted_iota(jnp.int32, (2 * dim, 2 * dim), 0) // dim
    col = lax.broadcasted_iota(jnp.int32, (2 * dim, 2 * dim), 1) // dim
    same = jnp.where(row == col, 1.0, 0.0).astype(jnp.bfloat16)
    for pair in range(heads // 2):
        columns = slice(pair * 2 * dim, (pair + 1) * 2 * dim)
        high, low = split_bf16(entering_ref[:, columns], 2)
        carried = contract(c, high, ((1,), (0,))) + contract(c, low, ((1,), (0,)))
        decay = pair_lanes(
            factor_ref[:, 2 * pair : 2 * pair + 1],
            factor_ref[:, 2 * pair + 1 : 2 * pair + 2],
            size,
            dim,
        )
        mixed = pre_ref[:, columns] + carried * decay
        high, low = split_bf16(mixed * mixed, 2)
        power = contract(high, same, ((1,), (0,))) + contract(low, same, ((1,), (0,)))
        o_ref[:, columns] = (mixed * lax.rsqrt(power * (1.0 / dim) + EPS)).astype(o_ref.dtype)


def recurrence_states(expo, rate, ssd_input, bmat):
    length, heads = expo.shape
    width, state = ssd_input.shape[1], bmat.shape[1]
    blocks = length // Q
    by_block = lambda n: pl.BlockSpec((Q, n), lambda b: (b, 0))
    once = lambda r, n: pl.BlockSpec((r, n), lambda b: (0, 0))
    return pl.pallas_call(
        functools.partial(states_kernel, width // heads),
        grid=(blocks,),
        in_specs=[by_block(heads), once(1, heads), by_block(width), by_block(state)],
        out_specs=[pl.BlockSpec((state, width), lambda b: (b, 0)), once(state, width), once(8, width)],
        out_shape=[
            jax.ShapeDtypeStruct((blocks * state, width), jnp.float32),
            jax.ShapeDtypeStruct((state, width), jnp.float32),
            jax.ShapeDtypeStruct((8, width), jnp.float32),
        ],
        compiler_params=pltpu.CompilerParams(vmem_limit_bytes=VMEM),
        cost_estimate=pl.CostEstimate(
            flops=length * width * state * 8, bytes_accessed=8 << 20, transcendentals=length * heads
        ),
        name="states",
    )(expo, rate[None], ssd_input, bmat)


def recurrence_intra(expo, rate, skip, ssd_input, bmat, cmat, local):
    length, heads = expo.shape
    width, state = ssd_input.shape[1], bmat.shape[1]
    blocks = length // Q
    by_block = lambda n: pl.BlockSpec((Q, n), lambda b: (b, 0))
    once = lambda r, n: pl.BlockSpec((r, n), lambda b: (0, 0))
    scalars = pl.BlockSpec(memory_space=pltpu.SMEM)
    return pl.pallas_call(
        functools.partial(intra_kernel, width // heads),
        grid=(blocks,),
        in_specs=[
            by_block(heads),
            once(1, heads),
            scalars,
            scalars,
            by_block(width),
            by_block(state),
            by_block(state),
            pl.BlockSpec((state, width), lambda b: (b, 0)),
        ],
        out_specs=[by_block(width), by_block(heads)],
        out_shape=[
            jax.ShapeDtypeStruct((length, width), jnp.float32),
            jax.ShapeDtypeStruct((length, heads), jnp.float32),
        ],
        scratch_shapes=[pltpu.VMEM((1, heads), jnp.float32)],
        compiler_params=pltpu.CompilerParams(vmem_limit_bytes=VMEM),
        cost_estimate=pl.CostEstimate(
            flops=length * width * Q * 8, bytes_accessed=12 << 20, transcendentals=length * heads * Q
        ),
        name="intra",
    )(expo, rate[None], rate, skip, ssd_input, bmat, cmat, local)


def recurrence_final(pre, factor, cmat, entering):
    length, width = pre.shape
    heads, state = factor.shape[1], cmat.shape[1]
    by_block = lambda n: pl.BlockSpec((Q, n), lambda b: (b, 0))
    return pl.pallas_call(
        functools.partial(final_kernel, width // heads),
        grid=(length // Q,),
        in_specs=[
            by_block(width),
            by_block(heads),
            by_block(state),
            pl.BlockSpec((state, width), lambda b: (0, 0)),
        ],
        out_specs=by_block(width),
        out_shape=jax.ShapeDtypeStruct((length, width), jnp.bfloat16),
        compiler_params=pltpu.CompilerParams(vmem_limit_bytes=VMEM),
        cost_estimate=pl.CostEstimate(
            flops=length * width * state * 8, bytes_accessed=8 << 20, transcendentals=length * heads
        ),
        name="final",
    )(pre, factor, cmat, entering)


def on_device(queries, keys, values, ssd_input, bmat, cmat, expo, rate, skip):
    length, width = queries.shape
    devices = lax.axis_size("seq")
    here = lax.axis_index("seq")
    span = W // length
    assert span == 4 and devices % span == 0 and length % (2 * Q) == 0
    planes = devices // span
    core, column = here % 2, (here // 2) % 2
    forward = [(i, i + span) for i in range(devices - span)]
    across = [(i, i ^ 2) for i in range(devices)]
    partner = [(i, i ^ 1) for i in range(devices)]
    send = lambda array, route: lax.ppermute(array, "seq", route)

    heads = width // E
    per = math.gcd(heads, CHUNK_HEADS)
    chunks = heads // per

    def packed(chunk):
        part = slice(chunk * per * E, (chunk + 1) * per * E)
        return jnp.concatenate([keys[:, part], values[:, part]], axis=1)

    near = jnp.where(core == 0, 3, 1)
    distance = jnp.stack([jnp.int32(4), near, jnp.int32(2), 4 - near])
    flags = (here >= distance).astype(jnp.int32)

    own = [packed(i) for i in range(chunks)]
    by_z = [send(part, forward) for part in own]
    by_y = [send(jnp.where(column == 0, o, z), across) for o, z in zip(own, by_z)]
    by_a = [send(jnp.where(core == 0, o, z), partner) for o, z in zip(own, by_z)]
    by_b = [send(y, partner) for y in by_y]

    local, total, decay = recurrence_states(expo, rate, ssd_input, bmat)
    pre, factor = recurrence_intra(expo, rate, skip, ssd_input, bmat, cmat, local)
    state = total.shape[0]
    both = jnp.concatenate([total, decay], axis=0)
    other = send(both, partner)
    first = jnp.where(core == 0, both, other)
    second = jnp.where(core == 0, other, both)
    first_total, first_decay = first[:state], first[state : state + 1]
    second_total, second_decay = second[:state], second[state : state + 1]
    wide = total.shape[1] // 2
    mine = lambda array: lax.dynamic_slice_in_dim(array, core * wide, wide, 1)
    chip_total = mine(second_decay * first_total + second_total)
    chip_decay = mine(first_decay * second_decay)
    rows = jnp.concatenate(
        [chip_total.astype(jnp.bfloat16)] + split_bf16(chip_decay, 3) + [jnp.zeros((13, wide), jnp.bfloat16)],
        axis=0,
    )
    got = send(rows, across).astype(jnp.float32)
    got_total = got[:state]
    got_decay = got[state : state + 1] + got[state + 1 : state + 2] + got[state + 2 : state + 3]
    plane_decay = chip_decay * got_decay
    plane_total = jnp.where(
        column == 0, got_decay * chip_total + got_total, chip_decay * got_total + chip_total
    )
    entering = jnp.zeros((state, wide), jnp.float32)
    for plane in range(planes - 1):
        route = [(plane * span + j, (plane + 1) * span + j) for j in range(span)]
        leaving = (plane_decay * entering + plane_total).astype(jnp.bfloat16)
        entering = entering + send(leaving, route).astype(jnp.float32)
    entering = jnp.where(column == 0, entering, got_decay * entering + got_total)
    theirs = send(entering, partner)
    entering = jnp.concatenate(
        [jnp.where(core == 0, entering, theirs), jnp.where(core == 0, theirs, entering)], axis=1
    )
    entering = jnp.where(core == 0, entering, first_decay * entering + first_total)

    attn_out = None
    for i in range(chunks):
        attn_out = attention_chunk(
            i, per, flags, queries, keys, values, by_z[i], by_y[i], by_a[i], by_b[i], attn_out
        )
    normed_recurrence_output = recurrence_final(pre, factor, cmat, entering)
    return (attn_out, normed_recurrence_output)


def solution(mesh):
    placed = P(("groups", "seq"), None)
    return jax.shard_map(
        on_device,
        mesh=mesh,
        in_specs=(placed,) * 7 + (P(), P()),
        out_specs=(placed, placed),
        check_vma=False,
    )
```

time: 589 us -> 215 us (0.37)
  the two profiles are of different devices: /device:TPU:17 before, /device:TPU:13 now
where the time goes in v1:
time: 215 us; the launch traced here: 214 us
  Pallas kernels  68.1 us (32%)
  waiting for transfers between devices  53.6 us (25%)
  starting transfers between devices  50.8 us (24%)
  other arithmetic  21.6 us (10%)
  local copies, waits for them, and re-layouts  18.4 us (9%)
    ppermute x38, waiting for transfers between devices, on_device(): send = lambda array, route: lax.ppermute(array, 'seq', route)  53.6 us
    ppermute x38, starting transfers between devices, on_device(): send = lambda array, route: lax.ppermute(array, 'seq', route)  50.8 us
    pallas_call x8, Pallas kernels, attention_chunk(): pl.pallas_call(attention_kernel, grid=(heads,), in_specs=specs, out_specs...  48.1 us
    unnamed x124, local copies, waits for them, and re-layouts  12.4 us
    select_n x8, other arithmetic, on_device(): jnp.where(core == 0, o, z)  9.65 us
    pallas_call x1, Pallas kernels, recurrence_intra(): pl.pallas_call(functools.partial(intra_kernel, width // heads), grid=(blo...  8.42 us
    pallas_call x1, Pallas kernels, recurrence_states(): pl.pallas_call(functools.partial(states_kernel, width // heads), grid=(bl...  7.44 us
    concatenate x8, other arithmetic, packed(): return jnp.concatenate([keys[:, part], values[:, part]], axis=1)  7.27 us
  transfers between devices with their start and end apart: 38, of which 9 were waited for; matrix products, arithmetic and copies ran while one was open for 13% of the time, Pallas kernels for 26%

profile of v1, /device:TPU:13, one launch (start us, length us, event | category | flops | bytes accessed | tf_op | source)
XLA Modules:
  0.0 214.0 jit_solution(9986149422214602496)
XLA Ops:
  1.6 1.6 copy-done.5
  4.8 7.4 %states.1 = (f32[256,2048]{1,0:T(8,128)S(1)}, f32[128,2048]{1,0:T(8,128)S(1)}, f32[8,2048]{1,0:T(8,128)S(1)}) custom-call(s32[512,32]{1,0:T(8,128)S(1)} %copy.19.expo_ref, f32[1,32]{1,0:T(1,128)S(1)} %bitcast.8, bf16[512,2048]{1,0:T(8,128)(2,1)S(1)} %copy-done.5, bf16[512,128]{1,0:T(8,128)(2,1)S(1)} %copy-done.7), custom_call_target="tpu_custom_call" | custom-call | flops 1073741824 | bytes 8388608 | tf_op jit(solution)/shard_map/states/pallas_call | solution.py:253
  16.1 1.3 pad_maximum_fusion.8
  17.4 3.2 %collective-permute-start.28 = (bf16[512,512]{1,0:T(8,128)(2,1)}, bf16[512,512]{1,0:T(8,128)(2,1)S(1)}, u32[]{:S(2)}, u32[]{:S(2)}) collective-permute-start(bf16[512,512]{1,0:T(8,128)(2,1)} %pad_maximum_fusion.8), channel_id=1, source_target_pairs={{0,4},{1,5},{2,6},{3,7},{4,8},{5,9},{6,10},{7,11},{8,12},{9,13},{1... | collective-permute-start | bytes 1572872 | tf_op jit(solution)/shard_map/ppermute | solution.py:339
  21.4 3.2 %collective-permute-start.24 = (bf16[512,512]{1,0:T(8,128)(2,1)}, bf16[512,512]{1,0:T(8,128)(2,1)S(1)}, u32[]{:S(2)}, u32[]{:S(2)}) collective-permute-start(bf16[512,512]{1,0:T(8,128)(2,1)} %pad_maximum_fusion.7), channel_id=1, source_target_pairs={{0,4},{1,5},{2,6},{3,7},{4,8},{5,9},{6,10},{7,11},{8,12},{9,13},{1... | collective-permute-start | bytes 1572872 | tf_op jit(solution)/shard_map/ppermute | solution.py:339
  25.5 1.9 collective-permute-start.20
  28.2 1.9 collective-permute-start.16
  33.8 1.6 copy-done.6
  35.4 1.6 copy-done.13
  37.0 8.4 %intra.1 = (f32[512,2048]{1,0:T(8,128)}, f32[512,32]{1,0:T(8,128)S(1)}) custom-call(s32[512,32]{1,0:T(8,128)S(1)} %copy.19.expo_ref, f32[1,32]{1,0:T(1,128)S(1)} %bitcast.9, f32[32]{0:T(128)S(1)} %copy-done.10, f32[32]{0:T(128)S(1)} %copy-done.11, bf16[512,2048]{1,0:T(8,128)(2,1)S(1)} %copy-done.6, bf16[512,128]{1,0:T(8,128)(2,1)S(1)} %copy-done.8, ...), custom_call_target="tpu_custom_call" | custom-call | flops 2147483648 | bytes 12582912 | tf_op jit(solution)/shard_map/intra/pallas_call | solution.py:278
  45.5 2.1 collective-permute-start.12
  47.6 1.2 broadcast_select_fusion.2
  48.8 1.9 collective-permute-start.8
  50.7 1.2 broadcast_select_fusion.3
  51.9 2.8 %collective-permute-done.20.zk.zv = bf16[512,512]{1,0:T(8,128)(2,1)S(1)} collective-permute-done((bf16[512,512]{1,0:T(8,128)(2,1)}, bf16[512,512]{1,0:T(8,128)(2,1)S(1)}, u32[]{:S(2)}, u32[]{:S(2)}) %collective-permute-start.20) | collective-permute-done | bytes 524320 | tf_op jit(solution)/shard_map/ppermute | solution.py:339
  54.7 3.2 %collective-permute-start.4 = (bf16[512,512]{1,0:T(8,128)(2,1)}, bf16[512,512]{1,0:T(8,128)(2,1)S(1)}, u32[]{:S(2)}, u32[]{:S(2)}) collective-permute-start(bf16[512,512]{1,0:T(8,128)(2,1)} %pad_maximum_fusion.2), channel_id=1, source_target_pairs={{0,4},{1,5},{2,6},{3,7},{4,8},{5,9},{6,10},{7,11},{8,12},{9,13},{1... | collective-permute-start | bytes 1572872 | tf_op jit(solution)/shard_map/ppermute | solution.py:339
  59.1 3.2 %collective-permute-start = (bf16[512,512]{1,0:T(8,128)(2,1)}, bf16[512,512]{1,0:T(8,128)(2,1)S(1)}, u32[]{:S(2)}, u32[]{:S(2)}) collective-permute-start(bf16[512,512]{1,0:T(8,128)(2,1)} %pad_maximum_fusion.1), channel_id=1, source_target_pairs={{0,4},{1,5},{2,6},{3,7},{4,8},{5,9},{6,10},{7,11},{8,12},{9,13},{1... | collective-permute-start | bytes 1572872 | tf_op jit(solution)/shard_map/ppermute | solution.py:339
  62.3 1.8 broadcast_select_fusion.1
  67.8 4.3 %concatenate.42 = bf16[144,1024]{1,0:T(8,128)(2,1)} concatenate(bf16[128,1024]{1,0:T(8,128)(2,1)} %fusion.2, bf16[1,1024]{1,0:T(2,128)(2,1)} %get-tuple-element.55, bf16[1,1024]{1,0:T(2,128)(2,1)} %get-tuple-element.54, bf16[1,1024]{1,0:T(2,128)(2,1)} %get-tuple-element.16, bf16[13,1024]{1,0:T(8,128)(2,1)} %broadcast_in_dim.11), dimensions={0} | concatenate | bytes 589824 | tf_op jit(solution)/shard_map/concatenate | solution.py:372
  72.5 1.4 broadcast_select_fusion.5
  73.9 3.4 %collective-permute-done.12.zk.zv = bf16[512,512]{1,0:T(8,128)(2,1)} collective-permute-done((bf16[512,512]{1,0:T(8,128)(2,1)}, bf16[512,512]{1,0:T(8,128)(2,1)}, u32[]{:S(2)}, u32[]{:S(2)}) %collective-permute-start.12) | collective-permute-done | bytes 524320 | tf_op jit(solution)/shard_map/ppermute | solution.py:339
  77.5 2.2 %broadcast_select_fusion.6 = (bf16[512,512]{1,0:T(8,128)(2,1)}, bf16[512,512]{1,0:T(8,128)(2,1)}) fusion(bf16[512,512]{1,0:T(8,128)(2,1)} %collective-permute-done.12.zk.zv, pred[]{:T(512)S(6)} %eq.7, bf16[512,256]{1,0:T(8,128)(2,1)S(1)} %copy-done.37, bf16[512,256]{1,0:T(8,128)(2,1)S(1)} %copy-done.35, pred[]{:T(512)S(6)} %eq.8), kind=kLoop, calls=%fused_computation.26 | loop fusion | flops 1572864 | bytes 2097154 | tf_op jit(solution)/shard_map/jit(_where)/select_n | solution.py:356
  79.7 8.7 %collective-permute-done.8.zk.zv = bf16[512,512]{1,0:T(8,128)(2,1)S(1)} collective-permute-done((bf16[512,512]{1,0:T(8,128)(2,1)}, bf16[512,512]{1,0:T(8,128)(2,1)S(1)}, u32[]{:S(2)}, u32[]{:S(2)}) %collective-permute-start.8) | collective-permute-done | bytes 524320 | tf_op jit(solution)/shard_map/ppermute | solution.py:339
  88.4 2.7 %collective-permute-start.30 = (bf16[512,512]{1,0:T(8,128)(2,1)S(1)}, bf16[512,512]{1,0:T(8,128)(2,1)S(1)}, u32[]{:S(2)}, u32[]{:S(2)}) collective-permute-start(bf16[512,512]{1,0:T(8,128)(2,1)S(1)} %copy-done.56), channel_id=1, source_target_pairs={{0,1},{1,0},{2,3},{3,2},{4,5},{5,4},{6,7},{7,6},{8,9},{9,8},{10,11... | collective-permute-start | bytes 1572872 | tf_op jit(solution)/shard_map/ppermute | solution.py:339
  91.1 8.5 %collective-permute-done.4.zk.zv = bf16[512,512]{1,0:T(8,128)(2,1)S(1)} collective-permute-done((bf16[512,512]{1,0:T(8,128)(2,1)}, bf16[512,512]{1,0:T(8,128)(2,1)S(1)}, u32[]{:S(2)}, u32[]{:S(2)}) %collective-permute-start.4) | collective-permute-done | bytes 524320 | tf_op jit(solution)/shard_map/ppermute | solution.py:339
  99.9 3.0 %collective-permute-start.26 = (bf16[512,512]{1,0:T(8,128)(2,1)S(1)}, bf16[512,512]{1,0:T(8,128)(2,1)S(1)}, u32[]{:S(2)}, u32[]{:S(2)}) collective-permute-start(bf16[512,512]{1,0:T(8,128)(2,1)S(1)} %copy-done.55), channel_id=1, source_target_pairs={{0,1},{1,0},{2,3},{3,2},{4,5},{5,4},{6,7},{7,6},{8,9},{9,8},{10,11... | collective-permute-start | bytes 1572872 | tf_op jit(solution)/shard_map/ppermute | solution.py:339
  104.4 6.6 %collective-permute-done.zk.zv = bf16[512,512]{1,0:T(8,128)(2,1)S(1)} collective-permute-done((bf16[512,512]{1,0:T(8,128)(2,1)}, bf16[512,512]{1,0:T(8,128)(2,1)S(1)}, u32[]{:S(2)}, u32[]{:S(2)}) %collective-permute-start) | collective-permute-done | bytes 524320 | tf_op jit(solution)/shard_map/ppermute | solution.py:339
  111.1 1.8 collective-permute-start.22
  113.0 1.3 collective-permute-start.17
  115.1 7.7 %collective-permute-done.21.yk.yv = bf16[512,512]{1,0:T(8,128)(2,1)S(1)} collective-permute-done((bf16[512,512]{1,0:T(8,128)(2,1)S(1)}, bf16[512,512]{1,0:T(8,128)(2,1)S(1)}, u32[]{:S(2)}, u32[]{:S(2)}) %collective-permute-start.21) | collective-permute-done | bytes 524320 | tf_op jit(solution)/shard_map/ppermute | solution.py:339
  123.0 4.8 %collective-permute-start.14 = (bf16[512,512]{1,0:T(8,128)(2,1)}, bf16[512,512]{1,0:T(8,128)(2,1)S(1)}, u32[]{:S(2)}, u32[]{:S(2)}) collective-permute-start(bf16[512,512]{1,0:T(8,128)(2,1)} %get-tuple-element.46), channel_id=1, source_target_pairs={{0,1},{1,0},{2,3},{3,2},{4,5},{5,4},{6,7},{7,6},{8,9},{9,8},{10,11... | collective-permute-start | bytes 1572872 | tf_op jit(solution)/shard_map/ppermute | solution.py:339
  127.8 6.2 %collective-permute-done.17.yk.yv = bf16[512,512]{1,0:T(8,128)(2,1)S(1)} collective-permute-done((bf16[512,512]{1,0:T(8,128)(2,1)S(1)}, bf16[512,512]{1,0:T(8,128)(2,1)S(1)}, u32[]{:S(2)}, u32[]{:S(2)}) %collective-permute-start.17) | collective-permute-done | bytes 524320 | tf_op jit(solution)/shard_map/ppermute | solution.py:339
  134.0 4.5 %collective-permute-start.27 = (bf16[512,512]{1,0:T(8,128)(2,1)S(1)}, bf16[512,512]{1,0:T(8,128)(2,1)S(1)}, u32[]{:S(2)}, u32[]{:S(2)}) collective-permute-start(bf16[512,512]{1,0:T(8,128)(2,1)S(1)} %collective-permute-done.25.yk.yv), channel_id=1, source_target_pairs={{0,1},{1,0},{2,3},{3,2},{4,5},{5,4},{6,7},{7,6},{8,9},{9,8},{10,11... | collective-permute-start | bytes 1572872 | tf_op jit(solution)/shard_map/ppermute | solution.py:339
  138.6 1.5 collective-permute-start.34
  141.5 6.9 %collective-permute-done.34 = bf16[128,1024]{1,0:T(8,128)(2,1)S(1)} collective-permute-done((bf16[128,1024]{1,0:T(8,128)(2,1)S(1)}, bf16[128,1024]{1,0:T(8,128)(2,1)S(1)}, u32[]{:S(2)}, u32[]{:S(2)}) %collective-permute-start.34) | collective-permute-done | bytes 262176 | tf_op jit(solution)/shard_map/ppermute | solution.py:339
  149.2 6.0 %attention.8.rest_0_ = bf16[512,2048]{1,0:T(8,128)(2,1)} custom-call(s32[4]{0:T(128)S(1)} %compare_convert_fusion.ok_ref, bf16[512,2048]{1,0:T(8,128)(2,1)S(1)} %copy-done, bf16[512,2048]{1,0:T(8,128)(2,1)} %ok0.15, bf16[512,2048]{1,0:T(8,128)(2,1)} %ov0.15, bf16[512,512]{1,0:T(8,128)(2,1)S(1)} %copy-done.2, bf16[512,512]{1,0:T(8,128)(2,1)S(1)} %copy-done.2, ...), custom_call_target="tpu_custom_call" | custom-call | flops 2684354560 | bytes 3145728 | tf_op jit(solution)/shard_map/attention/pallas_call | solution.py:98
  155.8 1.3 collective-permute-start.35
  157.1 6.0 %attention.9.rest_0_ = bf16[512,2048]{1,0:T(8,128)(2,1)} custom-call(s32[4]{0:T(128)S(1)} %compare_convert_fusion.ok_ref, bf16[512,2048]{1,0:T(8,128)(2,1)S(1)} %copy-done, bf16[512,2048]{1,0:T(8,128)(2,1)} %ok0.15, bf16[512,2048]{1,0:T(8,128)(2,1)} %ov0.15, bf16[512,512]{1,0:T(8,128)(2,1)S(1)} %collective-permute-done.24.zk.zv, ...), custom_call_target="tpu_custom_call", output_to_operand_aliasing={{}: (12, {})} | custom-call | flops 2684354560 | bytes 3145728 | tf_op jit(solution)/shard_map/attention/pallas_call | solution.py:98
  163.7 5.9 %attention.10.rest_0_ = bf16[512,2048]{1,0:T(8,128)(2,1)} custom-call(s32[4]{0:T(128)S(1)} %compare_convert_fusion.ok_ref, bf16[512,2048]{1,0:T(8,128)(2,1)S(1)} %copy-done, bf16[512,2048]{1,0:T(8,128)(2,1)} %ok0.15, bf16[512,2048]{1,0:T(8,128)(2,1)} %ov0.15, bf16[512,512]{1,0:T(8,128)(2,1)S(1)} %collective-permute-done.20.zk.zv, ...), custom_call_target="tpu_custom_call", output_to_operand_aliasing={{}: (12, {})} | custom-call | flops 2684354560 | bytes 3145728 | tf_op jit(solution)/shard_map/attention/pallas_call | solution.py:98
  169.7 1.3 collective-permute-start.1
  172.5 6.0 %attention.11.rest_0_ = bf16[512,2048]{1,0:T(8,128)(2,1)} custom-call(s32[4]{0:T(128)S(1)} %compare_convert_fusion.ok_ref, bf16[512,2048]{1,0:T(8,128)(2,1)S(1)} %copy-done, bf16[512,2048]{1,0:T(8,128)(2,1)} %ok0.15, bf16[512,2048]{1,0:T(8,128)(2,1)} %ov0.15, bf16[512,512]{1,0:T(8,128)(2,1)S(1)} %collective-permute-done.16.zk.zv, ...), custom_call_target="tpu_custom_call", output_to_operand_aliasing={{}: (12, {})} | custom-call | flops 2684354560 | bytes 3145728 | tf_op jit(solution)/shard_map/attention/pallas_call | solution.py:98
  179.1 6.1 %attention.12.rest_0_ = bf16[512,2048]{1,0:T(8,128)(2,1)} custom-call(s32[4]{0:T(128)S(1)} %compare_convert_fusion.ok_ref, bf16[512,2048]{1,0:T(8,128)(2,1)S(1)} %copy-done, bf16[512,2048]{1,0:T(8,128)(2,1)} %ok0.15, bf16[512,2048]{1,0:T(8,128)(2,1)} %ov0.15, bf16[512,512]{1,0:T(8,128)(2,1)} %collective-permute-done.12.zk.zv, ...), custom_call_target="tpu_custom_call", output_to_operand_aliasing={{}: (12, {})} | custom-call | flops 2684354560 | bytes 3145728 | tf_op jit(solution)/shard_map/attention/pallas_call | solution.py:98
  185.2 2.7 %collective-permute-done.1.yk.yv = bf16[512,512]{1,0:T(8,128)(2,1)S(1)} collective-permute-done((bf16[512,512]{1,0:T(8,128)(2,1)S(1)}, bf16[512,512]{1,0:T(8,128)(2,1)S(1)}, u32[]{:S(2)}, u32[]{:S(2)}) %collective-permute-start.1) | collective-permute-done | bytes 524320 | tf_op jit(solution)/shard_map/ppermute | solution.py:339
  189.5 5.9 %attention.13.rest_0_ = bf16[512,2048]{1,0:T(8,128)(2,1)} custom-call(s32[4]{0:T(128)S(1)} %compare_convert_fusion.ok_ref, bf16[512,2048]{1,0:T(8,128)(2,1)S(1)} %copy-done, bf16[512,2048]{1,0:T(8,128)(2,1)} %ok0.15, bf16[512,2048]{1,0:T(8,128)(2,1)} %ov0.15, bf16[512,512]{1,0:T(8,128)(2,1)S(1)} %collective-permute-done.8.zk.zv, ...), custom_call_target="tpu_custom_call", output_to_operand_aliasing={{}: (12, {})} | custom-call | flops 2684354560 | bytes 3145728 | tf_op jit(solution)/shard_map/attention/pallas_call | solution.py:98
  195.4 6.0 %attention.14.rest_0_ = bf16[512,2048]{1,0:T(8,128)(2,1)} custom-call(s32[4]{0:T(128)S(1)} %compare_convert_fusion.ok_ref, bf16[512,2048]{1,0:T(8,128)(2,1)S(1)} %copy-done, bf16[512,2048]{1,0:T(8,128)(2,1)} %ok0.15, bf16[512,2048]{1,0:T(8,128)(2,1)} %ov0.15, bf16[512,512]{1,0:T(8,128)(2,1)S(1)} %collective-permute-done.4.zk.zv, ...), custom_call_target="tpu_custom_call", output_to_operand_aliasing={{}: (12, {})} | custom-call | flops 2684354560 | bytes 3145728 | tf_op jit(solution)/shard_map/attention/pallas_call | solution.py:98
  201.4 6.2 %attention.15 = bf16[512,2048]{1,0:T(8,128)(2,1)} custom-call(s32[4]{0:T(128)S(1)} %compare_convert_fusion.ok_ref, bf16[512,2048]{1,0:T(8,128)(2,1)S(1)} %copy-done, bf16[512,2048]{1,0:T(8,128)(2,1)} %ok0.15, bf16[512,2048]{1,0:T(8,128)(2,1)} %ov0.15, bf16[512,512]{1,0:T(8,128)(2,1)S(1)} %collective-permute-done.zk.zv, ...), custom_call_target="tpu_custom_call", output_to_operand_aliasing={{}: (12, {})} | custom-call | flops 2684354560 | bytes 3145728 | tf_op jit(solution)/shard_map/attention/pallas_call | solution.py:98
  208.0 1.9 copy-done.3
  209.9 4.1 %final.1 = bf16[512,2048]{1,0:T(8,128)(2,1)} custom-call(f32[512,2048]{1,0:T(8,128)S(1)} %copy-done.3, f32[512,32]{1,0:T(8,128)S(1)} %get-tuple-element.9.factor_ref, bf16[512,128]{1,0:T(8,128)(2,1)S(1)} %copy-done.4, f32[128,2048]{1,0:T(8,128)S(1)} %add_select_fusion.entering_ref), custom_call_target="tpu_custom_call" | custom-call | flops 1073741824 | bytes 8388608 | tf_op jit(solution)/shard_map/final/pallas_call | solution.py:309
  (202 shorter events, 28.1 us)
Async XLA Ops:
  13.9 45.2 %collective-permute-start.32 = (f32[136,2048]{1,0:T(8,128)}, f32[136,2048]{1,0:T(8,128)}, u32[]{:S(2)}, u32[]{:S(2)}) collective-permute-start(f32[136,2048]{1,0:T(8,128)} %constant_dynamic-update-slice_fusion), channel_id=1, source_target_pairs={{0,1},{1,0},{2,3},{3,2},{4,5},{5,4},{6,7},{7,6},{8,9},{9,8},{10,11... | collective-permute-start | bytes 3342344 | tf_op jit(solution)/shard_map/ppermute | solution.py:339
  17.4 28.1 %collective-permute-start.28 = (bf16[512,512]{1,0:T(8,128)(2,1)}, bf16[512,512]{1,0:T(8,128)(2,1)S(1)}, u32[]{:S(2)}, u32[]{:S(2)}) collective-permute-start(bf16[512,512]{1,0:T(8,128)(2,1)} %pad_maximum_fusion.8), channel_id=1, source_target_pairs={{0,4},{1,5},{2,6},{3,7},{4,8},{5,9},{6,10},{7,11},{8,12},{9,13},{1... | collective-permute-start | bytes 1572872 | tf_op jit(solution)/shard_map/ppermute | solution.py:339
  21.4 27.3 %collective-permute-start.24 = (bf16[512,512]{1,0:T(8,128)(2,1)}, bf16[512,512]{1,0:T(8,128)(2,1)S(1)}, u32[]{:S(2)}, u32[]{:S(2)}) collective-permute-start(bf16[512,512]{1,0:T(8,128)(2,1)} %pad_maximum_fusion.7), channel_id=1, source_target_pairs={{0,4},{1,5},{2,6},{3,7},{4,8},{5,9},{6,10},{7,11},{8,12},{9,13},{1... | collective-permute-start | bytes 1572872 | tf_op jit(solution)/shard_map/ppermute | solution.py:339
  25.5 29.3 %collective-permute-start.20 = (bf16[512,512]{1,0:T(8,128)(2,1)}, bf16[512,512]{1,0:T(8,128)(2,1)S(1)}, u32[]{:S(2)}, u32[]{:S(2)}) collective-permute-start(bf16[512,512]{1,0:T(8,128)(2,1)} %pad_maximum_fusion.6), channel_id=1, source_target_pairs={{0,4},{1,5},{2,6},{3,7},{4,8},{5,9},{6,10},{7,11},{8,12},{9,13},{1... | collective-permute-start | bytes 1572872 | tf_op jit(solution)/shard_map/ppermute | solution.py:339
  28.2 44.0 %collective-permute-start.16 = (bf16[512,512]{1,0:T(8,128)(2,1)}, bf16[512,512]{1,0:T(8,128)(2,1)S(1)}, u32[]{:S(2)}, u32[]{:S(2)}) collective-permute-start(bf16[512,512]{1,0:T(8,128)(2,1)} %pad_maximum_fusion.5), channel_id=1, source_target_pairs={{0,4},{1,5},{2,6},{3,7},{4,8},{5,9},{6,10},{7,11},{8,12},{9,13},{1... | collective-permute-start | bytes 1572872 | tf_op jit(solution)/shard_map/ppermute | solution.py:339
  45.5 31.8 %collective-permute-start.12 = (bf16[512,512]{1,0:T(8,128)(2,1)}, bf16[512,512]{1,0:T(8,128)(2,1)}, u32[]{:S(2)}, u32[]{:S(2)}) collective-permute-start(bf16[512,512]{1,0:T(8,128)(2,1)} %pad_maximum_fusion.4), channel_id=1, source_target_pairs={{0,4},{1,5},{2,6},{3,7},{4,8},{5,9},{6,10},{7,11},{8,12},{9,13},{1... | collective-permute-start | bytes 1572872 | tf_op jit(solution)/shard_map/ppermute | solution.py:339
  48.8 39.7 %collective-permute-start.8 = (bf16[512,512]{1,0:T(8,128)(2,1)}, bf16[512,512]{1,0:T(8,128)(2,1)S(1)}, u32[]{:S(2)}, u32[]{:S(2)}) collective-permute-start(bf16[512,512]{1,0:T(8,128)(2,1)} %pad_maximum_fusion.3), channel_id=1, source_target_pairs={{0,4},{1,5},{2,6},{3,7},{4,8},{5,9},{6,10},{7,11},{8,12},{9,13},{1... | collective-permute-start | bytes 1572872 | tf_op jit(solution)/shard_map/ppermute | solution.py:339
  54.7 44.9 %collective-permute-start.4 = (bf16[512,512]{1,0:T(8,128)(2,1)}, bf16[512,512]{1,0:T(8,128)(2,1)S(1)}, u32[]{:S(2)}, u32[]{:S(2)}) collective-permute-start(bf16[512,512]{1,0:T(8,128)(2,1)} %pad_maximum_fusion.2), channel_id=1, source_target_pairs={{0,4},{1,5},{2,6},{3,7},{4,8},{5,9},{6,10},{7,11},{8,12},{9,13},{1... | collective-permute-start | bytes 1572872 | tf_op jit(solution)/shard_map/ppermute | solution.py:339
  59.1 51.8 %collective-permute-start = (bf16[512,512]{1,0:T(8,128)(2,1)}, bf16[512,512]{1,0:T(8,128)(2,1)S(1)}, u32[]{:S(2)}, u32[]{:S(2)}) collective-permute-start(bf16[512,512]{1,0:T(8,128)(2,1)} %pad_maximum_fusion.1), channel_id=1, source_target_pairs={{0,4},{1,5},{2,6},{3,7},{4,8},{5,9},{6,10},{7,11},{8,12},{9,13},{1... | collective-permute-start | bytes 1572872 | tf_op jit(solution)/shard_map/ppermute | solution.py:339
  72.2 27.5 %copy-start.57 = (bf16[512,512]{1,0:T(8,128)(2,1)S(1)}, bf16[512,512]{1,0:T(8,128)(2,1)}, u32[]{:S(2)}) copy-start(bf16[512,512]{1,0:T(8,128)(2,1)} %get-tuple-element.41) | copy-start | bytes 1572868
  72.2 27.7 %copy-start.55 = (bf16[512,512]{1,0:T(8,128)(2,1)S(1)}, bf16[512,512]{1,0:T(8,128)(2,1)}, u32[]{:S(2)}) copy-start(bf16[512,512]{1,0:T(8,128)(2,1)} %get-tuple-element.40) | copy-start | bytes 1572868
  72.2 30.8 %copy-start.31 = (bf16[512,256]{1,0:T(8,128)(2,1)S(1)}, bf16[512,256]{1,0:T(8,128)(2,1)}, u32[]{:S(2)}) copy-start(bf16[512,256]{1,0:T(8,128)(2,1)} %copy-done.30) | copy-start | bytes 786436
  72.2 30.8 %copy-start.33 = (bf16[512,256]{1,0:T(8,128)(2,1)S(1)}, bf16[512,256]{1,0:T(8,128)(2,1)}, u32[]{:S(2)}) copy-start(bf16[512,256]{1,0:T(8,128)(2,1)} %copy-done.32) | copy-start | bytes 786436
  72.2 27.6 %collective-permute-start.33 = (bf16[144,1024]{1,0:T(8,128)(2,1)}, bf16[144,1024]{1,0:T(8,128)(2,1)S(1)}, u32[]{:S(2)}, u32[]{:S(2)}) collective-permute-start(bf16[144,1024]{1,0:T(8,128)(2,1)} %concatenate.42), channel_id=1, source_target_pairs={{0,2},{1,3},{2,0},{3,1},{4,6},{5,7},{6,4},{7,5},{8,10},{9,11},{10,... | collective-permute-start | bytes 884744 | tf_op jit(solution)/shard_map/ppermute | solution.py:339
  77.3 26.7 %copy-start.27 = (bf16[512,256]{1,0:T(8,128)(2,1)S(1)}, bf16[512,256]{1,0:T(8,128)(2,1)}, u32[]{:S(2)}) copy-start(bf16[512,256]{1,0:T(8,128)(2,1)} %copy-done.26) | copy-start | bytes 786436
  77.3 26.7 %copy-start.29 = (bf16[512,256]{1,0:T(8,128)(2,1)S(1)}, bf16[512,256]{1,0:T(8,128)(2,1)}, u32[]{:S(2)}) copy-start(bf16[512,256]{1,0:T(8,128)(2,1)} %copy-done.28) | copy-start | bytes 786436
  77.3 33.8 %collective-permute-start.29 = (bf16[512,512]{1,0:T(8,128)(2,1)}, bf16[512,512]{1,0:T(8,128)(2,1)S(1)}, u32[]{:S(2)}, u32[]{:S(2)}) collective-permute-start(bf16[512,512]{1,0:T(8,128)(2,1)} %get-tuple-element.39), channel_id=1, source_target_pairs={{0,2},{1,3},{2,0},{3,1},{4,6},{5,7},{6,4},{7,5},{8,10},{9,11},{10,... | collective-permute-start | bytes 1572872 | tf_op jit(solution)/shard_map/ppermute | solution.py:339
  88.4 24.5 %collective-permute-start.30 = (bf16[512,512]{1,0:T(8,128)(2,1)S(1)}, bf16[512,512]{1,0:T(8,128)(2,1)S(1)}, u32[]{:S(2)}, u32[]{:S(2)}) collective-permute-start(bf16[512,512]{1,0:T(8,128)(2,1)S(1)} %copy-done.56), channel_id=1, source_target_pairs={{0,1},{1,0},{2,3},{3,2},{4,5},{5,4},{6,7},{7,6},{8,9},{9,8},{10,11... | collective-permute-start | bytes 1572872 | tf_op jit(solution)/shard_map/ppermute | solution.py:339
  99.7 14.6 %collective-permute-start.25 = (bf16[512,512]{1,0:T(8,128)(2,1)S(1)}, bf16[512,512]{1,0:T(8,128)(2,1)S(1)}, u32[]{:S(2)}, u32[]{:S(2)}) collective-permute-start(bf16[512,512]{1,0:T(8,128)(2,1)S(1)} %copy-done.57), channel_id=1, source_target_pairs={{0,2},{1,3},{2,0},{3,1},{4,6},{5,7},{6,4},{7,5},{8,10},{9,11},{10,... | collective-permute-start | bytes 1572872 | tf_op jit(solution)/shard_map/ppermute | solution.py:339
  99.9 14.7 %collective-permute-start.26 = (bf16[512,512]{1,0:T(8,128)(2,1)S(1)}, bf16[512,512]{1,0:T(8,128)(2,1)S(1)}, u32[]{:S(2)}, u32[]{:S(2)}) collective-permute-start(bf16[512,512]{1,0:T(8,128)(2,1)S(1)} %copy-done.55), channel_id=1, source_target_pairs={{0,1},{1,0},{2,3},{3,2},{4,5},{5,4},{6,7},{7,6},{8,9},{9,8},{10,11... | collective-permute-start | bytes 1572872 | tf_op jit(solution)/shard_map/ppermute | solution.py:339
  104.3 35.8 %copy-start.23 = (bf16[512,256]{1,0:T(8,128)(2,1)S(1)}, bf16[512,256]{1,0:T(8,128)(2,1)}, u32[]{:S(2)}) copy-start(bf16[512,256]{1,0:T(8,128)(2,1)} %copy-done.22) | copy-start | bytes 786436
  104.3 35.8 %copy-start.25 = (bf16[512,256]{1,0:T(8,128)(2,1)S(1)}, bf16[512,256]{1,0:T(8,128)(2,1)}, u32[]{:S(2)}) copy-start(bf16[512,256]{1,0:T(8,128)(2,1)} %copy-done.24) | copy-start | bytes 786436
  110.9 11.9 %collective-permute-start.21 = (bf16[512,512]{1,0:T(8,128)(2,1)S(1)}, bf16[512,512]{1,0:T(8,128)(2,1)S(1)}, u32[]{:S(2)}, u32[]{:S(2)}) collective-permute-start(bf16[512,512]{1,0:T(8,128)(2,1)S(1)} %copy-done.54), channel_id=1, source_target_pairs={{0,2},{1,3},{2,0},{3,1},{4,6},{5,7},{6,4},{7,5},{8,10},{9,11},{10,... | collective-permute-start | bytes 1572872 | tf_op jit(solution)/shard_map/ppermute | solution.py:339
  111.1 11.9 %collective-permute-start.22 = (bf16[512,512]{1,0:T(8,128)(2,1)S(1)}, bf16[512,512]{1,0:T(8,128)(2,1)S(1)}, u32[]{:S(2)}, u32[]{:S(2)}) collective-permute-start(bf16[512,512]{1,0:T(8,128)(2,1)S(1)} %copy-done.53), channel_id=1, source_target_pairs={{0,1},{1,0},{2,3},{3,2},{4,5},{5,4},{6,7},{7,6},{8,9},{9,8},{10,11... | collective-permute-start | bytes 1572872 | tf_op jit(solution)/shard_map/ppermute | solution.py:339
  113.0 21.1 %collective-permute-start.17 = (bf16[512,512]{1,0:T(8,128)(2,1)S(1)}, bf16[512,512]{1,0:T(8,128)(2,1)S(1)}, u32[]{:S(2)}, u32[]{:S(2)}) collective-permute-start(bf16[512,512]{1,0:T(8,128)(2,1)S(1)} %get-tuple-element.45), channel_id=1, source_target_pairs={{0,2},{1,3},{2,0},{3,1},{4,6},{5,7},{6,4},{7,5},{8,10},{9,11},{10,... | collective-permute-start | bytes 1572872 | tf_op jit(solution)/shard_map/ppermute | solution.py:339
  114.2 24.3 %collective-permute-start.18 = (bf16[512,512]{1,0:T(8,128)(2,1)S(1)}, bf16[512,512]{1,0:T(8,128)(2,1)S(1)}, u32[]{:S(2)}, u32[]{:S(2)}) collective-permute-start(bf16[512,512]{1,0:T(8,128)(2,1)S(1)} %get-tuple-element.44), channel_id=1, source_target_pairs={{0,1},{1,0},{2,3},{3,2},{4,5},{5,4},{6,7},{7,6},{8,9},{9,8},{10,11... | collective-permute-start | bytes 1572872 | tf_op jit(solution)/shard_map/ppermute | solution.py:339
  114.6 26.6 %collective-permute-start.31 = (bf16[512,512]{1,0:T(8,128)(2,1)S(1)}, bf16[512,512]{1,0:T(8,128)(2,1)S(1)}, u32[]{:S(2)}, u32[]{:S(2)}) collective-permute-start(bf16[512,512]{1,0:T(8,128)(2,1)S(1)} %collective-permute-done.29.yk.yv), channel_id=1, source_target_pairs={{0,1},{1,0},{2,3},{3,2},{4,5},{5,4},{6,7},{7,6},{8,9},{9,8},{10,11... | collective-permute-start | bytes 1572872 | tf_op jit(solution)/shard_map/ppermute | solution.py:339
  114.8 34.3 %copy-start = (bf16[512,2048]{1,0:T(8,128)(2,1)S(1)}, bf16[512,2048]{1,0:T(8,128)(2,1)}, u32[]{:S(2)}) copy-start(bf16[512,2048]{1,0:T(8,128)(2,1)} %q_ref.15) | copy-start | bytes 6291460
  114.9 34.3 %copy-start.2 = (bf16[512,512]{1,0:T(8,128)(2,1)S(1)}, bf16[512,512]{1,0:T(8,128)(2,1)}, u32[]{:S(2)}) copy-start(bf16[512,512]{1,0:T(8,128)(2,1)} %copy-done.1) | copy-start | bytes 1572868
  122.8 32.4 %collective-permute-start.13 = (bf16[512,512]{1,0:T(8,128)(2,1)}, bf16[512,512]{1,0:T(8,128)(2,1)S(1)}, u32[]{:S(2)}, u32[]{:S(2)}) collective-permute-start(bf16[512,512]{1,0:T(8,128)(2,1)} %get-tuple-element.47), channel_id=1, source_target_pairs={{0,2},{1,3},{2,0},{3,1},{4,6},{5,7},{6,4},{7,5},{8,10},{9,11},{10,... | collective-permute-start | bytes 1572872 | tf_op jit(solution)/shard_map/ppermute | solution.py:339
  123.0 32.3 %collective-permute-start.14 = (bf16[512,512]{1,0:T(8,128)(2,1)}, bf16[512,512]{1,0:T(8,128)(2,1)S(1)}, u32[]{:S(2)}, u32[]{:S(2)}) collective-permute-start(bf16[512,512]{1,0:T(8,128)(2,1)} %get-tuple-element.46), channel_id=1, source_target_pairs={{0,1},{1,0},{2,3},{3,2},{4,5},{5,4},{6,7},{7,6},{8,9},{9,8},{10,11... | collective-permute-start | bytes 1572872 | tf_op jit(solution)/shard_map/ppermute | solution.py:339
  134.0 21.8 %collective-permute-start.27 = (bf16[512,512]{1,0:T(8,128)(2,1)S(1)}, bf16[512,512]{1,0:T(8,128)(2,1)S(1)}, u32[]{:S(2)}, u32[]{:S(2)}) collective-permute-start(bf16[512,512]{1,0:T(8,128)(2,1)S(1)} %collective-permute-done.25.yk.yv), channel_id=1, source_target_pairs={{0,1},{1,0},{2,3},{3,2},{4,5},{5,4},{6,7},{7,6},{8,9},{9,8},{10,11... | collective-permute-start | bytes 1572872 | tf_op jit(solution)/shard_map/ppermute | solution.py:339
  138.6 9.8 %collective-permute-start.34 = (bf16[128,1024]{1,0:T(8,128)(2,1)S(1)}, bf16[128,1024]{1,0:T(8,128)(2,1)S(1)}, u32[]{:S(2)}, u32[]{:S(2)}) collective-permute-start(bf16[128,1024]{1,0:T(8,128)(2,1)S(1)} %get-tuple-element.12), channel_id=1, source_target_pairs={{0,4},{1,5},{2,6},{3,7},{16,20},{17,21},{18,22},{19,23}} | collective-permute-start | bytes 786440 | tf_op jit(solution)/shard_map/ppermute | solution.py:339
  141.2 21.8 %collective-permute-start.9 = (bf16[512,512]{1,0:T(8,128)(2,1)}, bf16[512,512]{1,0:T(8,128)(2,1)S(1)}, u32[]{:S(2)}, u32[]{:S(2)}) collective-permute-start(bf16[512,512]{1,0:T(8,128)(2,1)} %get-tuple-element.49), channel_id=1, source_target_pairs={{0,2},{1,3},{2,0},{3,1},{4,6},{5,7},{6,4},{7,5},{8,10},{9,11},{10,... | collective-permute-start | bytes 1572872 | tf_op jit(solution)/shard_map/ppermute | solution.py:339
  148.4 15.0 %collective-permute-start.23 = (bf16[512,512]{1,0:T(8,128)(2,1)S(1)}, bf16[512,512]{1,0:T(8,128)(2,1)S(1)}, u32[]{:S(2)}, u32[]{:S(2)}) collective-permute-start(bf16[512,512]{1,0:T(8,128)(2,1)S(1)} %collective-permute-done.21.yk.yv), channel_id=1, source_target_pairs={{0,1},{1,0},{2,3},{3,2},{4,5},{5,4},{6,7},{7,6},{8,9},{9,8},{10,11... | collective-permute-start | bytes 1572872 | tf_op jit(solution)/shard_map/ppermute | solution.py:339
  155.2 15.9 %collective-permute-start.10 = (bf16[512,512]{1,0:T(8,128)(2,1)S(1)}, bf16[512,512]{1,0:T(8,128)(2,1)S(1)}, u32[]{:S(2)}, u32[]{:S(2)}) collective-permute-start(bf16[512,512]{1,0:T(8,128)(2,1)S(1)} %get-tuple-element.48), channel_id=1, source_target_pairs={{0,1},{1,0},{2,3},{3,2},{4,5},{5,4},{6,7},{7,6},{8,9},{9,8},{10,11... | collective-permute-start | bytes 1572872 | tf_op jit(solution)/shard_map/ppermute | solution.py:339
  155.3 16.3 %collective-permute-start.19 = (bf16[512,512]{1,0:T(8,128)(2,1)S(1)}, bf16[512,512]{1,0:T(8,128)(2,1)S(1)}, u32[]{:S(2)}, u32[]{:S(2)}) collective-permute-start(bf16[512,512]{1,0:T(8,128)(2,1)S(1)} %collective-permute-done.17.yk.yv), channel_id=1, source_target_pairs={{0,1},{1,0},{2,3},{3,2},{4,5},{5,4},{6,7},{7,6},{8,9},{9,8},{10,11... | collective-permute-start | bytes 1572872 | tf_op jit(solution)/shard_map/ppermute | solution.py:339
  155.8 13.9 %collective-permute-start.35 = (bf16[128,1024]{1,0:T(8,128)(2,1)S(1)}, bf16[128,1024]{1,0:T(8,128)(2,1)S(1)}, u32[]{:S(2)}, u32[]{:S(2)}) collective-permute-start(bf16[128,1024]{1,0:T(8,128)(2,1)S(1)} %fusion.1), channel_id=1, source_target_pairs={{4,8},{5,9},{6,10},{7,11},{20,24},{21,25},{22,26},{23,27}} | collective-permute-start | bytes 786440 | tf_op jit(solution)/shard_map/ppermute | solution.py:339
  163.1 15.4 %collective-permute-start.5 = (bf16[512,512]{1,0:T(8,128)(2,1)S(1)}, bf16[512,512]{1,0:T(8,128)(2,1)S(1)}, u32[]{:S(2)}, u32[]{:S(2)}) collective-permute-start(bf16[512,512]{1,0:T(8,128)(2,1)S(1)} %get-tuple-element.51), channel_id=1, source_target_pairs={{0,2},{1,3},{2,0},{3,1},{4,6},{5,7},{6,4},{7,5},{8,10},{9,11},{10,... | collective-permute-start | bytes 1572872 | tf_op jit(solution)/shard_map/ppermute | solution.py:339
  163.4 15.3 %collective-permute-start.15 = (bf16[512,512]{1,0:T(8,128)(2,1)S(1)}, bf16[512,512]{1,0:T(8,128)(2,1)S(1)}, u32[]{:S(2)}, u32[]{:S(2)}) collective-permute-start(bf16[512,512]{1,0:T(8,128)(2,1)S(1)} %collective-permute-done.13.yk.yv), channel_id=1, source_target_pairs={{0,1},{1,0},{2,3},{3,2},{4,5},{5,4},{6,7},{7,6},{8,9},{9,8},{10,11... | collective-permute-start | bytes 1572872 | tf_op jit(solution)/shard_map/ppermute | solution.py:339
  169.7 18.2 %collective-permute-start.1 = (bf16[512,512]{1,0:T(8,128)(2,1)S(1)}, bf16[512,512]{1,0:T(8,128)(2,1)S(1)}, u32[]{:S(2)}, u32[]{:S(2)}) collective-permute-start(bf16[512,512]{1,0:T(8,128)(2,1)S(1)} %copy-done.58), channel_id=1, source_target_pairs={{0,2},{1,3},{2,0},{3,1},{4,6},{5,7},{6,4},{7,5},{8,10},{9,11},{10,... | collective-permute-start | bytes 1572872 | tf_op jit(solution)/shard_map/ppermute | solution.py:339
  171.1 17.8 %collective-permute-start.11 = (bf16[512,512]{1,0:T(8,128)(2,1)S(1)}, bf16[512,512]{1,0:T(8,128)(2,1)S(1)}, u32[]{:S(2)}, u32[]{:S(2)}) collective-permute-start(bf16[512,512]{1,0:T(8,128)(2,1)S(1)} %collective-permute-done.9.yk.yv), channel_id=1, source_target_pairs={{0,1},{1,0},{2,3},{3,2},{4,5},{5,4},{6,7},{7,6},{8,9},{9,8},{10,11... | collective-permute-start | bytes 1572872 | tf_op jit(solution)/shard_map/ppermute | solution.py:339
  171.6 17.1 %collective-permute-start.36 = (bf16[128,1024]{1,0:T(8,128)(2,1)S(1)}, bf16[128,1024]{1,0:T(8,128)(2,1)S(1)}, u32[]{:S(2)}, u32[]{:S(2)}) collective-permute-start(bf16[128,1024]{1,0:T(8,128)(2,1)S(1)} %add_convert_fusion), channel_id=1, source_target_pairs={{8,12},{9,13},{10,14},{11,15},{24,28},{25,29},{26,30},{27,31}} | collective-permute-start | bytes 786440 | tf_op jit(solution)/shard_map/ppermute | solution.py:339
  178.5 16.9 %collective-permute-start.6 = (bf16[512,512]{1,0:T(8,128)(2,1)S(1)}, bf16[512,512]{1,0:T(8,128)(2,1)S(1)}, u32[]{:S(2)}, u32[]{:S(2)}) collective-permute-start(bf16[512,512]{1,0:T(8,128)(2,1)S(1)} %get-tuple-element.50), channel_id=1, source_target_pairs={{0,1},{1,0},{2,3},{3,2},{4,5},{5,4},{6,7},{7,6},{8,9},{9,8},{10,11... | collective-permute-start | bytes 1572872 | tf_op jit(solution)/shard_map/ppermute | solution.py:339
  178.7 16.8 %collective-permute-start.7 = (bf16[512,512]{1,0:T(8,128)(2,1)S(1)}, bf16[512,512]{1,0:T(8,128)(2,1)S(1)}, u32[]{:S(2)}, u32[]{:S(2)}) collective-permute-start(bf16[512,512]{1,0:T(8,128)(2,1)S(1)} %collective-permute-done.5.yk.yv), channel_id=1, source_target_pairs={{0,1},{1,0},{2,3},{3,2},{4,5},{5,4},{6,7},{7,6},{8,9},{9,8},{10,11... | collective-permute-start | bytes 1572872 | tf_op jit(solution)/shard_map/ppermute | solution.py:339
  187.9 13.6 %collective-permute-start.2 = (bf16[512,512]{1,0:T(8,128)(2,1)S(1)}, bf16[512,512]{1,0:T(8,128)(2,1)S(1)}, u32[]{:S(2)}, u32[]{:S(2)}) collective-permute-start(bf16[512,512]{1,0:T(8,128)(2,1)S(1)} %copy-done.52), channel_id=1, source_target_pairs={{0,1},{1,0},{2,3},{3,2},{4,5},{5,4},{6,7},{7,6},{8,9},{9,8},{10,11... | collective-permute-start | bytes 1572872 | tf_op jit(solution)/shard_map/ppermute | solution.py:339
  188.7 12.7 %collective-permute-start.3 = (bf16[512,512]{1,0:T(8,128)(2,1)S(1)}, bf16[512,512]{1,0:T(8,128)(2,1)S(1)}, u32[]{:S(2)}, u32[]{:S(2)}) collective-permute-start(bf16[512,512]{1,0:T(8,128)(2,1)S(1)} %collective-permute-done.1.yk.yv), channel_id=1, source_target_pairs={{0,1},{1,0},{2,3},{3,2},{4,5},{5,4},{6,7},{7,6},{8,9},{9,8},{10,11... | collective-permute-start | bytes 1572872 | tf_op jit(solution)/shard_map/ppermute | solution.py:339
  189.0 18.7 %collective-permute-start.37 = (f32[128,1024]{1,0:T(8,128)S(1)}, f32[128,1024]{1,0:T(8,128)S(1)}, u32[]{:S(2)}, u32[]{:S(2)}) collective-permute-start(f32[128,1024]{1,0:T(8,128)S(1)} %add_select_fusion.1), channel_id=1, source_target_pairs={{0,1},{1,0},{2,3},{3,2},{4,5},{5,4},{6,7},{7,6},{8,9},{9,8},{10,11... | collective-permute-start | bytes 1572872 | tf_op jit(solution)/shard_map/ppermute | solution.py:339
  (51 other events, 406.7 us)

commit v2 on v1

v2 whole, which is shorter than its diff:
```python
import functools
import math

import jax
import jax.numpy as jnp
from jax import lax
from jax.experimental import pallas as pl
from jax.experimental.pallas import tpu as pltpu
from jax.sharding import PartitionSpec as P

E = 128
W = 2048
Q = 256
EPS = 1e-05
NEG = -1e30
SCALE = math.log2(math.e) / math.sqrt(E)
PAIR = 2
LENT = (2, 4, 4)
RELAYED = (2, 2, 2)
MIB = 1024 * 1024
HBM = pl.BlockSpec(memory_space=pl.ANY)
ON_CHIP = pl.BlockSpec(memory_space=pltpu.VMEM)
SCALARS = pl.BlockSpec(memory_space=pltpu.SMEM)


def params(mib):
    return pltpu.CompilerParams(vmem_limit_bytes=mib * MIB)


def contract(a, b, dims=((1,), (0,))):
    return lax.dot_general(a, b, (dims, ((), ())), preferred_element_type=jnp.float32)


def split_bf16(v, terms):
    parts = []
    for _ in range(terms):
        part = v.astype(jnp.bfloat16)
        parts.append(part)
        v = v - part.astype(jnp.float32)
    return parts


def split_contract(a, b, terms=2):
    return sum(contract(part, b) for part in split_bf16(a, terms))


def scaled(q):
    high, low = split_bf16(q.astype(jnp.float32) * SCALE, 2)
    return jnp.concatenate([high, low], axis=1)


def score(q, k, mask):
    s = contract(q, jnp.concatenate([k, k], axis=1), ((1,), (1,)))
    return s if mask is None else jnp.where(mask, s, NEG)


def weigh(s, top, v):
    p = jnp.exp2(s - top).astype(jnp.bfloat16)
    return contract(p, jnp.concatenate([v, jnp.ones_like(v)], axis=1))


def alternate(steps):
    steps = list(steps)
    while steps:
        for step in list(steps):
            try:
                next(step)
            except StopIteration:
                steps.remove(step)


def in_stages(tiles, first, second):
    kept = [{} for _ in tiles]
    alternate([first(*tiles[0], kept[0])])
    for i, tile in enumerate(tiles):
        ahead = [first(*tiles[i + 1], kept[i + 1])] if i + 1 < len(tiles) else []
        alternate(ahead + [second(*tile, kept[i])])
        kept[i].clear()


def lent_kernel(heads, side, q_ref, n_ref, ok, ov, pk, pv, yk, yv, bk, bv, _, o_ref, l_ref, m_ref):
    rows = q_ref.shape[0]
    half = rows // 2
    before = pl.program_id(0) * PAIR
    row = lax.broadcasted_iota(jnp.int32, (half, half), 0)
    col = lax.broadcasted_iota(jnp.int32, (half, half), 1)
    lane = lax.broadcasted_iota(jnp.int32, (half, E), 1)
    by_core, by_column = side[0] > 0, side[1] > 0
    causal, later = col <= row, col > row
    lo, hi = slice(0, half), slice(half, rows)

    @pl.when(before == 0)
    def _():
        l_ref[...] = jnp.zeros_like(l_ref)
        m_ref[:, heads * E :] = jnp.zeros((rows, E), m_ref.dtype)

    def first(h, r, kept):
        rr = (lo, hi)[r]
        cols = slice(h * E, (h + 1) * E)
        mine, lent = scaled(q_ref[rr, cols]), scaled(n_ref[rr, cols])
        core_q = jnp.where(by_core, mine, lent)
        column_q = jnp.where(by_column, mine, lent)
        own = (ok, ov)
        if r == 0:
            todo = [("mine", mine, own, lo, causal), ("lent", lent, own, lo, later), ("lent", lent, own, hi, None)]
        else:
            todo = [("mine", mine, own, lo, None), ("mine", mine, own, hi, causal), ("lent", lent, own, hi, later)]
        for name, q, shard in (
            ("core", core_q, (pk, pv)),
            ("column", column_q, (yk, yv)),
            ("column", column_q, (bk, bv)),
        ):
            todo += [(name, q, shard, part, None) for part in (lo, hi)]
        kept["top"], kept["scores"] = {}, []
        for name, q, (k_ref, v_ref), part, mask in todo:
            s = score(q, k_ref[part, cols], mask)
            m = jnp.max(s, axis=1, keepdims=True)
            tops = kept["top"]
            tops[name] = jnp.maximum(tops[name], m) if name in tops else m
            kept["scores"].append((name, s, v_ref, part))
            yield

    def second(h, r, kept):
        rr = (lo, hi)[r]
        cols = slice(h * E, (h + 1) * E)
        top = kept["top"]
        mine = jnp.maximum(top["mine"], jnp.maximum(jnp.where(by_core, top["core"], NEG), jnp.where(by_column, top["column"], NEG)))
        lent = jnp.maximum(top["lent"], jnp.maximum(jnp.where(by_core, NEG, top["core"]), jnp.where(by_column, NEG, top["column"])))
        limit = {
            "mine": mine,
            "lent": lent,
            "core": jnp.where(by_core, mine, lent),
            "column": jnp.where(by_column, mine, lent),
        }
        acc = {}
        for name, s, v_ref, part in kept["scores"]:
            a = weigh(s, limit[name], v_ref[part, cols])
            acc[name] = acc[name] + a if name in acc else a
            yield
        acc_mine = acc["mine"] + jnp.where(by_core, acc["core"], 0.0) + jnp.where(by_column, acc["column"], 0.0)
        acc_lent = acc["lent"] + jnp.where(by_core, 0.0, acc["core"]) + jnp.where(by_column, 0.0, acc["column"])
        o_ref[rr, cols] = acc_mine[:, :E] / acc_mine[:, E:]
        head = before + h
        at = pl.ds(pl.multiple_of(head * E, E), E)
        m_ref[rr, at] = (acc_lent[:, :E] / acc_lent[:, E:]).astype(m_ref.dtype)
        l_ref[rr, :] = jnp.where(lane == head, mine + jnp.log2(acc_mine[:, E:]), l_ref[rr, :])
        tail = slice(heads * E, (heads + 1) * E)
        stat = m_ref[rr, tail]
        for t, part in enumerate(split_bf16(lent + jnp.log2(acc_lent[:, E:]), 3)):
            stat = jnp.where(lane == 3 * head + t, part, stat)
        m_ref[rr, tail] = stat
        yield

    in_stages([(h, r) for h in range(PAIR) for r in range(2)], first, second)


def lent_heads(start, heads, offset, side, queries, asked, keys, values, pk, pv, y, b, after):
    rows = queries.shape[0]
    wide = PAIR * E
    pairs = heads // PAIR
    whole = pl.BlockSpec((rows, wide), lambda i: (0, start // PAIR + i))
    asked_at = pl.BlockSpec((rows, wide), lambda i: (0, offset // PAIR + i))
    part = pl.BlockSpec((rows, wide), lambda i: (0, i))
    later = pl.BlockSpec((rows, wide), lambda i: (0, pairs + i))
    fixed = lambda n: pl.BlockSpec((rows, n), lambda i: (0, 0))
    return pl.pallas_call(
        functools.partial(lent_kernel, heads),
        grid=(pairs,),
        in_specs=[SCALARS, whole, asked_at] + [whole] * 4 + [part, later] * 2 + [HBM],
        out_specs=[part, fixed(E), fixed((heads + 1) * E)],
        out_shape=[
            jax.ShapeDtypeStruct((rows, heads * E), jnp.float32),
            jax.ShapeDtypeStruct((rows, E), jnp.float32),
            jax.ShapeDtypeStruct((rows, (heads + 1) * E), jnp.bfloat16),
        ],
        compiler_params=params(60),
        cost_estimate=attention_cost(heads, rows),
        name="lent",
    )(side, queries, asked, keys, values, pk, pv, y, y, b, b, after)


def attention_cost(heads, rows):
    return pl.CostEstimate(
        flops=rows, bytes_accessed=rows, transcendentals=0
    )


def relayed_kernel(ok_ref, q_ref, ok, ov, zk, zv, ak, av, yk, yv, bk, bv, *rest):
    o_ref = rest[-1]
    rows = q_ref.shape[0]
    half = rows // 2
    row = lax.broadcasted_iota(jnp.int32, (half, half), 0)
    col = lax.broadcasted_iota(jnp.int32, (half, half), 1)
    causal, later = col <= row, col > row
    lo, hi = slice(0, half), slice(half, rows)

    def first(h, r, kept):
        cols = slice(h * E, (h + 1) * E)
        q = scaled(q_ref[(lo, hi)[r], cols])
        own, far = (ok, ov), (zk, zv)
        if r == 0:
            todo = [(own, lo, causal, None), (far, lo, later, 0), (far, hi, None, 0)]
        else:
            todo = [(own, lo, None, None), (own, hi, causal, None), (far, hi, later, 0)]
        for shard, flag in (((ak, av), 1), ((yk, yv), 2), ((bk, bv), 3)):
            todo += [(shard, part, None, flag) for part in (lo, hi)]
        kept["top"], kept["scores"] = None, []
        for (k_ref, v_ref), part, mask, flag in todo:
            s = score(q, k_ref[part, cols], mask)
            m = jnp.max(s, axis=1, keepdims=True)
            if flag is not None:
                m = jnp.where(ok_ref[flag] > 0, m, NEG)
            kept["top"] = m if kept["top"] is None else jnp.maximum(kept["top"], m)
            kept["scores"].append((s, v_ref, part, flag))
            yield

    def second(h, r, kept):
        top = kept["top"]
        acc = None
        cols = slice(h * E, (h + 1) * E)
        for s, v_ref, part, flag in kept["scores"]:
            limit = top if flag is None else jnp.where(ok_ref[flag] > 0, top, -NEG)
            a = weigh(s, limit, v_ref[part, cols])
            acc = a if acc is None else acc + a
            yield
        o_ref[(lo, hi)[r], cols] = (acc[:, :E] / acc[:, E:]).astype(o_ref.dtype)
        yield

    in_stages([(h, r) for h in range(PAIR) for r in range(2)], first, second)


def relayed_heads(start, offset, total, flags, queries, keys, values, z, a, y, b, result):
    rows, width = queries.shape
    wide = PAIR * E
    at = lambda n: pl.BlockSpec((rows, wide), lambda i: (0, n))
    own = at(start // PAIR)
    far = [at(offset // PAIR), at((total + offset) // PAIR)]
    args = [flags, queries, keys, values, z, z, a, a, y, y, b, b, result]
    return pl.pallas_call(
        relayed_kernel,
        grid=(1,),
        in_specs=[SCALARS] + [own] * 3 + far * 2 + [at(0), at(1)] * 2 + [HBM],
        out_specs=own,
        out_shape=jax.ShapeDtypeStruct((rows, width), jnp.bfloat16),
        input_output_aliases={len(args) - 1: 0},
        compiler_params=params(60),
        cost_estimate=attention_cost(PAIR, rows),
        name="relayed",
    )(*args)


def turn_kernel(count, column, own_ref, z_ref, _, *outs):
    wide = PAIR * E
    for j, out in enumerate(outs):
        for part in range(2):
            source = slice((part * count + j) * wide, (part * count + j + 1) * wide)
            out[:, part * wide : (part + 1) * wide] = jnp.where(
                column[0] == 0, own_ref[:, source], z_ref[:, source]
            )


def turn(count, column, own, z, after):
    rows = own.shape[0]
    by_tile = lambda n: pl.BlockSpec((rows // 2, n), lambda i: (i, 0))
    return pl.pallas_call(
        functools.partial(turn_kernel, count),
        grid=(2,),
        in_specs=[SCALARS, by_tile(own.shape[1]), by_tile(own.shape[1]), HBM],
        out_specs=[by_tile(2 * PAIR * E)] * count,
        out_shape=[jax.ShapeDtypeStruct((rows, 2 * PAIR * E), own.dtype)] * count,
        compiler_params=params(60),
        cost_estimate=pl.CostEstimate(flops=100, bytes_accessed=100, transcendentals=0),
        name="turn",
    )(column, own, z, after)


def join_kernel(ok_ref, mine_ref, l_ref, got_ref, stat_ref, *rest):
    o_ref = rest[-1]
    before = pl.program_id(0) * PAIR
    row = lax.broadcasted_iota(jnp.int32, (E, E), 0)
    col = lax.broadcasted_iota(jnp.int32, (E, E), 1)
    gather = jnp.where((row >= 3 * col) & (row < 3 * col + 3), 1.0, 0.0).astype(jnp.bfloat16)
    here = l_ref[...]
    there = jnp.where(ok_ref[0] > 0, contract(stat_ref[...], gather), NEG)
    top = jnp.maximum(here, there)
    here, there = jnp.exp2(here - top), jnp.exp2(there - top)
    share = split_bf16(here / (here + there), 2)
    for h in range(PAIR):
        cols = slice(h * E, (h + 1) * E)
        pick = jnp.where(row == before + h, 1.0, 0.0).astype(jnp.bfloat16)
        weight = sum(contract(part, pick) for part in share)
        back = got_ref[:, cols].astype(jnp.float32)
        o_ref[:, cols] = (back + weight * (mine_ref[:, cols] - back)).astype(o_ref.dtype)


def join(start, heads, flags, mine, l, got, width, result):
    rows = mine.shape[0]
    wide = PAIR * E
    part = pl.BlockSpec((rows, wide), lambda i: (0, i))
    args = [flags, mine, l, got, got]
    specs = [SCALARS, part, pl.BlockSpec((rows, E), lambda i: (0, 0)), part]
    specs.append(pl.BlockSpec((rows, E), lambda i: (0, heads)))
    aliases = {}
    if result is not None:
        aliases = {len(args): 0}
        args.append(result)
        specs.append(HBM)
    return pl.pallas_call(
        join_kernel,
        grid=(heads // PAIR,),
        in_specs=specs,
        out_specs=pl.BlockSpec((rows, wide), lambda i: (0, start // PAIR + i)),
        out_shape=jax.ShapeDtypeStruct((rows, width), jnp.bfloat16),
        input_output_aliases=aliases,
        compiler_params=params(60),
        cost_estimate=pl.CostEstimate(flops=rows, bytes_accessed=rows, transcendentals=0),
        name="join",
    )(*args)


def running_expo(expo_ref):
    size = expo_ref.shape[0]
    expo = expo_ref[...]
    high = (expo >> 8).astype(jnp.float32).astype(jnp.bfloat16)
    low = (expo & 255).astype(jnp.float32).astype(jnp.bfloat16)
    row = lax.broadcasted_iota(jnp.int32, (size, size), 0)
    col = lax.broadcasted_iota(jnp.int32, (size, size), 1)
    lower = jnp.where(row >= col, 1.0, 0.0).astype(jnp.bfloat16)
    upper = jnp.where(row <= col, 1.0, 0.0).astype(jnp.bfloat16)
    down = contract(lower, high) * 256.0 + contract(lower, low)
    across = contract(high, upper, ((0,), (0,))) * 256.0 + contract(low, upper, ((0,), (0,)))
    return down, across


def spread_matrix(heads, width):
    dim = width // heads
    head = lax.broadcasted_iota(jnp.int32, (heads, width), 0)
    col = lax.broadcasted_iota(jnp.int32, (heads, width), 1)
    inside = (col >= head * dim) & (col < head * dim + dim)
    return jnp.where(inside, 1.0, 0.0).astype(jnp.bfloat16)


def states_kernel(expo_ref, rate_ref, x_ref, b_ref, *refs):
    local_ref, both_ref = refs[-2:]
    heads, width, state = expo_ref.shape[1], x_ref.shape[1], b_ref.shape[1]

    @pl.when(pl.program_id(0) == 0)
    def _():
        both_ref[:state, :] = jnp.zeros((state, width), jnp.float32)
        both_ref[state:, :] = jnp.ones((8, width), jnp.float32)

    down, _ = running_expo(expo_ref)
    rate = rate_ref[...]
    end = down[-1:, :]
    spread = spread_matrix(heads, width)
    weights = split_contract(jnp.exp(rate * (down - end)), spread)
    decay = split_contract(jnp.broadcast_to(jnp.exp(-rate * end), (8, heads)), spread, 3)
    weighted = x_ref[...].astype(jnp.float32) * weights
    new = sum(contract(b_ref[...], part, ((0,), (0,))) for part in split_bf16(weighted, 2))
    before = both_ref[:state, :]
    local_ref[...] = before
    both_ref[:state, :] = before * decay[:1, :] + new
    both_ref[state:, :] = both_ref[state:, :] * decay


def intra_kernel(expo_ref, rate_ref, rates_ref, skip_ref, x_ref, b_ref, c_ref, local_ref, _, pre_ref, factor_ref, past):
    size, heads = expo_ref.shape
    width = x_ref.shape[1]
    dim = width // heads
    half = size // 2

    @pl.when(pl.program_id(0) == 0)
    def _():
        past[...] = jnp.zeros_like(past)

    down, across = running_expo(expo_ref)
    rate = rate_ref[...]
    factor_ref[...] = jnp.exp(-rate * (down + past[...]))
    past[...] = past[...] + down[-1:, :]
    c = c_ref[...]
    spread = spread_matrix(heads, width)
    within = split_contract(jnp.exp(-rate * down), spread)
    carried = sum(contract(c, part) for part in split_bf16(local_ref[...], 2))
    skip = split_contract(jnp.broadcast_to(skip_ref[...], (8, heads)), spread, 3)[:1, :]
    pre_ref[...] = carried * within + skip * x_ref[...].astype(jnp.float32)
    cross = contract(c, b_ref[...], ((1,), (1,)))
    row = lax.broadcasted_iota(jnp.int32, (half, half), 0)
    col = lax.broadcasted_iota(jnp.int32, (half, half), 1)
    seen = row >= col
    left = lax.broadcasted_iota(jnp.int32, (half, 2 * dim), 1) < dim
    for pair in range(heads // 2):
        columns = slice(pair * 2 * dim, (pair + 1) * 2 * dim)
        x = x_ref[:, columns]
        upper, lower = [], []
        for h in (2 * pair, 2 * pair + 1):
            r = rates_ref[h]
            here, there = down[:, h : h + 1], across[h : h + 1, :]
            gap = jnp.where(seen, (there[:, :half] - here[:half]) * r, NEG)
            inner = (cross[:half, :half] * jnp.exp(gap)).astype(jnp.bfloat16)
            upper.append(contract(inner, x[:half]))
            gap = (there[:, :half] - here[half:]) * r
            inner_left = (cross[half:, :half] * jnp.exp(gap)).astype(jnp.bfloat16)
            gap = jnp.where(seen, (there[:, half:] - here[half:]) * r, NEG)
            inner_right = (cross[half:, half:] * jnp.exp(gap)).astype(jnp.bfloat16)
            lower.append(contract(jnp.concatenate([inner_left, inner_right], axis=1), x))
        pre_ref[:half, columns] += jnp.where(left, upper[0], upper[1])
        pre_ref[half:, columns] += jnp.where(left, lower[0], lower[1])


def chip_kernel(core, both_ref, other_ref, *refs):
    chip_ref, rows_ref = refs[-2:]
    rows, width = both_ref.shape
    state = rows - 8
    wide = width // 2
    leads = core[0] == 0
    mine = jnp.where(leads, both_ref[:, :wide], both_ref[:, wide:])
    other = jnp.where(leads, other_ref[:, :wide], other_ref[:, wide:])
    first, second = jnp.where(leads, mine, other), jnp.where(leads, other, mine)
    total = first[:state] * second[state : state + 1] + second[:state]
    decay = first[state:] * second[state:]
    chip_ref[:state, :] = total
    chip_ref[state:, :] = decay
    rows_ref[:state, :] = total.astype(jnp.bfloat16)
    row = lax.broadcasted_iota(jnp.int32, (16, wide), 0)
    tail = jnp.zeros((16, wide), jnp.bfloat16)
    for t, part in enumerate(split_bf16(decay[:1, :], 3)):
        tail = jnp.where(row == t, part, tail)
    rows_ref[state:, :] = tail


def plane_kernel(column, chip_ref, got_ref, *refs):
    plane_ref, leaving_ref = refs[-2:]
    state = leaving_ref.shape[0]
    got = got_ref[...].astype(jnp.float32)
    got_total = got[:state]
    got_decay = got[state : state + 1] + got[state + 1 : state + 2] + got[state + 2 : state + 3]
    chip_total, chip_decay = chip_ref[:state, :], chip_ref[state : state + 1, :]
    total = jnp.where(
        column[0] == 0, chip_total * got_decay + got_total, got_total * chip_decay + chip_total
    )
    plane_ref[:state, :] = total
    plane_ref[state:, :] = chip_ref[state:, :] * got_decay
    leaving_ref[...] = total.astype(jnp.bfloat16)


def hop_kernel(plane_ref, entering_ref, came_ref, after_ref, leaving_ref):
    state = leaving_ref.shape[0]
    entering = entering_ref[...] + came_ref[...].astype(jnp.float32)
    after_ref[...] = entering
    leaving = entering * plane_ref[state : state + 1, :] + plane_ref[:state, :]
    leaving_ref[...] = leaving.astype(jnp.bfloat16)


def arrive_kernel(column, got_ref, entering_ref, came_ref, out_ref):
    state = came_ref.shape[0]
    entering = entering_ref[...] + came_ref[...].astype(jnp.float32)
    got = got_ref[...].astype(jnp.float32)
    got_decay = got[state : state + 1] + got[state + 1 : state + 2] + got[state + 2 : state + 3]
    out_ref[...] = jnp.where(column[0] == 0, entering, entering * got_decay + got[:state])


def final_kernel(core, pre_ref, factor_ref, c_ref, mine_ref, theirs_ref, other_ref, o_ref):
    size, width = pre_ref.shape
    heads = factor_ref.shape[1]
    state = mine_ref.shape[0]
    dim = width // heads
    wide = 2 * dim
    half = width // 2
    leads = core[0] == 0
    c = c_ref[...]
    row = lax.broadcasted_iota(jnp.int32, (wide, wide), 0) // dim
    col = lax.broadcasted_iota(jnp.int32, (wide, wide), 1) // dim
    same = jnp.where(row == col, 1.0, 0.0).astype(jnp.bfloat16)
    left = lax.broadcasted_iota(jnp.int32, (size, wide), 1) < dim
    for pair in range(heads // 2):
        columns = slice(pair * wide, (pair + 1) * wide)
        inner = slice(pair * wide % half, pair * wide % half + wide)
        mine, theirs = mine_ref[:, inner], theirs_ref[:, inner]
        first_half = pair * wide < half
        entering = jnp.where(leads, mine, theirs) if first_half else jnp.where(leads, theirs, mine)
        after_first = entering * other_ref[state : state + 1, columns] + other_ref[:state, columns]
        entering = jnp.where(leads, entering, after_first)
        carried = sum(contract(c, part) for part in split_bf16(entering, 2))
        factor = jnp.where(
            left, factor_ref[:, 2 * pair : 2 * pair + 1], factor_ref[:, 2 * pair + 1 : 2 * pair + 2]
        )
        mixed = pre_ref[:, columns] + carried * factor
        power = contract((mixed * mixed).astype(jnp.bfloat16), same)
        o_ref[:, columns] = (mixed * lax.rsqrt(power * (1.0 / dim) + EPS)).astype(o_ref.dtype)


def small(kernel, name, shapes, scalars, *args, after=()):
    late = list(after)
    return pl.pallas_call(
        kernel,
        in_specs=[SCALARS] * len(scalars) + [ON_CHIP] * len(args) + [HBM] * len(late),
        out_specs=[ON_CHIP] * len(shapes),
        out_shape=[jax.ShapeDtypeStruct(shape, kind) for shape, kind in shapes],
        compiler_params=params(16),
        cost_estimate=pl.CostEstimate(flops=100, bytes_accessed=100, transcendentals=0),
        name=name,
    )(*scalars, *args, *late)


def by_block(n):
    return pl.BlockSpec((Q, n), lambda b: (b, 0))


def once(r, n):
    return pl.BlockSpec((r, n), lambda b: (0, 0))


def recurrence_states(expo, rate, ssd_input, bmat, after):
    length, heads = expo.shape
    width, state = ssd_input.shape[1], bmat.shape[1]
    blocks = length // Q
    return pl.pallas_call(
        states_kernel,
        grid=(blocks,),
        in_specs=[by_block(heads), once(1, heads), by_block(width), by_block(state)] + [HBM] * len(after),
        out_specs=[pl.BlockSpec((state, width), lambda b: (b, 0)), once(state + 8, width)],
        out_shape=[
            jax.ShapeDtypeStruct((blocks * state, width), jnp.float32),
            jax.ShapeDtypeStruct((state + 8, width), jnp.float32),
        ],
        compiler_params=params(60),
        cost_estimate=pl.CostEstimate(
            flops=length, bytes_accessed=length, transcendentals=0
        ),
        name="states",
    )(expo, rate[None], ssd_input, bmat, *after)


def recurrence_intra(expo, rate, skip, ssd_input, bmat, cmat, local, after):
    length, heads = expo.shape
    width, state = ssd_input.shape[1], bmat.shape[1]
    blocks = length // Q
    return pl.pallas_call(
        intra_kernel,
        grid=(blocks,),
        in_specs=[
            by_block(heads),
            once(1, heads),
            SCALARS,
            once(1, heads),
            by_block(width),
            by_block(state),
            by_block(state),
            pl.BlockSpec((state, width), lambda b: (b, 0)),
            HBM,
        ],
        out_specs=[by_block(width), by_block(heads)],
        out_shape=[
            jax.ShapeDtypeStruct((length, width), jnp.float32),
            jax.ShapeDtypeStruct((length, heads), jnp.float32),
        ],
        scratch_shapes=[pltpu.VMEM((1, heads), jnp.float32)],
        compiler_params=params(60),
        cost_estimate=pl.CostEstimate(
            flops=length, bytes_accessed=length, transcendentals=0
        ),
        name="intra",
    )(expo, rate[None], rate, skip[None], ssd_input, bmat, cmat, local, after)


def recurrence_final(core, pre, factor, cmat, mine, theirs, other):
    length, width = pre.shape
    heads, state = factor.shape[1], cmat.shape[1]
    return pl.pallas_call(
        final_kernel,
        grid=(length // Q,),
        in_specs=[
            SCALARS,
            by_block(width),
            by_block(heads),
            by_block(state),
            once(*mine.shape),
            once(*theirs.shape),
            once(*other.shape),
        ],
        out_specs=by_block(width),
        out_shape=jax.ShapeDtypeStruct((length, width), jnp.bfloat16),
        compiler_params=params(60),
        cost_estimate=pl.CostEstimate(
            flops=length, bytes_accessed=length, transcendentals=0
        ),
        name="final",
    )(core, pre, factor, cmat, mine, theirs, other)


def on_device(queries, keys, values, ssd_input, bmat, cmat, expo, rate, skip):
    length, width = queries.shape
    devices = lax.axis_size("seq")
    here = lax.axis_index("seq")
    span = W // length
    assert span == 4 and devices % span == 0 and length % (2 * Q) == 0
    assert width == E * (sum(LENT) + sum(RELAYED))
    planes = devices // span
    core, column = here % 2, (here // 2) % 2
    core_1, column_1 = core[None].astype(jnp.int32), column[None].astype(jnp.int32)
    forward = [(i, i + span) for i in range(devices - span)]
    backward = [(j, i) for i, j in forward]
    across = [(i, i ^ 2) for i in range(devices)]
    partner = [(i, i ^ 1) for i in range(devices)]
    send = lambda array, route: lax.ppermute(array, "seq", route)

    starts = [sum(LENT[:i]) for i in range(len(LENT))]
    lent_total, relayed_total = sum(LENT), sum(RELAYED)
    columns = lambda array, s, n: array[:, s * E : (s + n) * E]
    packed = lambda s, n: jnp.concatenate([columns(keys, s, n), columns(values, s, n)], axis=1)

    by_y = [send(packed(s, n), across) for s, n in zip(starts, LENT)]
    asked_first = send(columns(queries, 0, LENT[0]), backward)
    asked_later = send(columns(queries, LENT[0], lent_total - LENT[0]), backward)
    to_z = packed(lent_total, relayed_total)
    by_z = send(to_z, forward)
    partner_k, partner_v = send(keys, partner), send(values, partner)
    by_b = [send(y, partner) for y in by_y]

    side = jnp.stack([core, column]).astype(jnp.int32)
    near = jnp.where(core == 0, 3, 1)
    distance = jnp.stack([jnp.int32(4), near, jnp.int32(2), 4 - near])
    flags = (here >= distance).astype(jnp.int32)

    def lent(i, after):
        asked, offset = (asked_first, 0) if i == 0 else (asked_later, starts[i] - LENT[0])
        return lent_heads(
            starts[i], LENT[i], offset, side, queries, asked, keys, values, partner_k, partner_v, by_y[i], by_b[i], after
        )

    local, both = recurrence_states(expo, rate, ssd_input, bmat, [by_y[0], asked_first])
    other = send(both, partner)
    partial = [lent(0, local)]
    pre, factor = recurrence_intra(expo, rate, skip, ssd_input, bmat, cmat, local, partial[0][1])
    state = bmat.shape[1]
    wide = ssd_input.shape[1] // 2
    full, brief = jnp.float32, jnp.bfloat16
    chip, rows = small(
        chip_kernel, "chip", [((state + 8, wide), full), ((state + 16, wide), brief)], [core_1], both, other, after=[factor, by_y[1]]
    )
    got = send(rows, across)
    partial.append(lent(1, chip))
    plane, leaving = small(
        plane_kernel, "plane", [((state + 8, wide), full), ((state, wide), brief)], [column_1], chip, got, after=[partial[1][1], by_y[2]]
    )
    by_a = send(jnp.where(core == 0, to_z, by_z), partner)
    turned = turn(len(RELAYED), column_1, to_z, by_z, partial[1][1])
    last_y = [send(part, across) for part in turned]
    last_b = [send(part, partner) for part in last_y]
    entering = jnp.zeros((state, wide), jnp.float32)
    for s in range(planes - 1):
        came = send(leaving, [(s * span + j, (s + 1) * span + j) for j in range(span)])
        if s == 0:
            partial.append(lent(2, plane))
        if s < planes - 2:
            entering, leaving = small(
                hop_kernel, "hop", [((state, wide), full), ((state, wide), brief)], [], plane, entering, came
            )
    (entering,) = small(arrive_kernel, "arrive", [((state, wide), full)], [column_1], got, entering, came)
    theirs = send(entering, partner)
    normed_recurrence_output = recurrence_final(core_1, pre, factor, cmat, entering, theirs, other)

    back = [send(message, forward) for _, _, message in partial]
    attn_out = None
    for i, (s, n) in enumerate(zip(starts[:-1], LENT)):
        attn_out = join(s, n, flags, partial[i][0], partial[i][1], back[i], width, attn_out)
    for i in range(len(RELAYED)):
        if i == len(RELAYED) - 1:
            attn_out = join(starts[-1], LENT[-1], flags, partial[-1][0], partial[-1][1], back[-1], width, attn_out)
        offset = sum(RELAYED[:i])
        attn_out = relayed_heads(
            lent_total + offset, offset, relayed_total, flags, queries, keys, values, by_z, by_a, last_y[i], last_b[i], attn_out
        )
    return (attn_out, normed_recurrence_output)


def solution(mesh):
    placed = P(("groups", "seq"), None)
    return jax.shard_map(
        on_device,
        mesh=mesh,
        in_specs=(placed,) * 7 + (P(), P()),
        out_specs=(placed, placed),
        check_vma=False,
    )
```

time: 215 us -> 168 us (0.78)
  the two profiles are of different devices: /device:TPU:13 before, /device:TPU:17 now
where the time goes in v2:
time: 168 us; the launch traced here: 165 us
  Pallas kernels  81.9 us (49%)
  starting transfers between devices  33.9 us (20%)
  waiting for transfers between devices  24.5 us (15%)
  local copies, waits for them, and re-layouts  15 us (9%)
  other arithmetic  8.92 us (5%)
    ppermute x27, starting transfers between devices, on_device(): send = lambda array, route: lax.ppermute(array, 'seq', route)  33.9 us
    pallas_call x3, Pallas kernels, lent_heads(): pl.pallas_call(functools.partial(lent_kernel, heads), grid=(pairs,), in_s...  26.5 us
    ppermute x27, waiting for transfers between devices, on_device(): send = lambda array, route: lax.ppermute(array, 'seq', route)  24.5 us
    pallas_call x3, Pallas kernels, relayed_heads(): pl.pallas_call(relayed_kernel, grid=(1,), in_specs=[SCALARS] + [own] * 3...  17 us
    pallas_call x1, Pallas kernels, recurrence_intra(): pl.pallas_call(intra_kernel, grid=(blocks,), in_specs=[by_block(heads), o...  10.4 us
    pallas_call x1, Pallas kernels, recurrence_final(): pl.pallas_call(final_kernel, grid=(length // Q,), in_specs=[SCALARS, by_b...  9.77 us
    pallas_call x3, Pallas kernels, join(): pl.pallas_call(join_kernel, grid=(heads // PAIR,), in_specs=specs, out_sp...  8.39 us
    slice x8, local copies, waits for them, and re-layouts, on_device(): columns = lambda array, s, n: array[:, s * E:(s + n) * E]  8.19 us
  transfers between devices with their start and end apart: 27, of which 5 were waited for; matrix products, arithmetic and copies ran while one was open for 11% of the time, Pallas kernels for 44%

profile of v2, /device:TPU:17, one launch (start us, length us, event | category | flops | bytes accessed | tf_op | source)
XLA Modules:
  0.0 165.3 jit_solution(18048447142506789579)
XLA Ops:
  1.5 1.0 slice.35
  2.4 1.0 slice.36
  3.5 1.3 collective-permute-start.7
  4.8 2.1 %fusion = (bf16[512,512]{1,0:T(8,128)(2,1)}, bf16[512,512]{1,0:T(8,128)(2,1)S(1)}) fusion(bf16[512,2048]{1,0:T(8,128)(2,1)} %ok.11), kind=kLoop, calls=%fused_computation.7 | loop fusion | bytes 2097152 | tf_op jit(solution)/shard_map/slice | solution.py:609
  6.8 0.9 fusion.1
  7.7 1.2 pad_maximum_fusion.1
  9.1 7.4 %collective-permute-done.7.refs_0_.yk.yv = bf16[512,512]{1,0:T(8,128)(2,1)S(1)} collective-permute-done((bf16[512,512]{1,0:T(8,128)(2,1)S(1)}, bf16[512,512]{1,0:T(8,128)(2,1)S(1)}, u32[]{:S(2)}, u32[]{:S(2)}) %collective-permute-start.7) | collective-permute-done | bytes 524320 | tf_op jit(solution)/shard_map/ppermute | solution.py:605
  16.5 2.2 %collective-permute-start.10 = (bf16[512,512]{1,0:T(8,128)(2,1)S(1)}, bf16[512,512]{1,0:T(8,128)(2,1)S(1)}, u32[]{:S(2)}, u32[]{:S(2)}) collective-permute-start(bf16[512,512]{1,0:T(8,128)(2,1)S(1)} %collective-permute-done.7.refs_0_.yk.yv), channel_id=1, source_target_pairs={{0,1},{1,0},{2,3},{3,2},{4,5},{5,4},{6,7},{7,6},{8,9},{9,8},{10,11... | collective-permute-start | bytes 1572872 | tf_op jit(solution)/shard_map/ppermute | solution.py:605
  18.8 1.0 slice.37
  19.8 2.1 %collective-permute-start.8 = (bf16[512,256]{1,0:T(8,128)(2,1)S(1)}, bf16[512,256]{1,0:T(8,128)(2,1)S(1)}, u32[]{:S(2)}, u32[]{:S(2)}) collective-permute-start(bf16[512,256]{1,0:T(8,128)(2,1)S(1)} %slice.37), channel_id=1, source_target_pairs={{4,0},{5,1},{6,2},{7,3},{8,4},{9,5},{10,6},{11,7},{12,8},{13,9},{1... | collective-permute-start | bytes 786440 | tf_op jit(solution)/shard_map/ppermute | solution.py:605
  21.8 1.2 slice.30
  23.1 1.3 pad_maximum_fusion.own_ref
  24.4 4.9 %collective-permute-done.8.refs_1_.n_ref = bf16[512,256]{1,0:T(8,128)(2,1)S(1)} collective-permute-done((bf16[512,256]{1,0:T(8,128)(2,1)S(1)}, bf16[512,256]{1,0:T(8,128)(2,1)S(1)}, u32[]{:S(2)}, u32[]{:S(2)}) %collective-permute-start.8) | collective-permute-done | bytes 262176 | tf_op jit(solution)/shard_map/ppermute | solution.py:605
  29.4 1.9 %collective-permute-start = (bf16[512,1536]{1,0:T(8,128)(2,1)}, bf16[512,1536]{1,0:T(8,128)(2,1)}, u32[]{:S(2)}, u32[]{:S(2)}) collective-permute-start(bf16[512,1536]{1,0:T(8,128)(2,1)} %pad_maximum_fusion.own_ref), channel_id=1, source_target_pairs={{0,4},{1,5},{2,6},{3,7},{4,8},{5,9},{6,10},{7,11},{8,12},{9,13},{1... | collective-permute-start | bytes 4718600 | tf_op jit(solution)/shard_map/ppermute | solution.py:605
  32.2 5.5 %states.1 = (f32[256,2048]{1,0:T(8,128)}, f32[136,2048]{1,0:T(8,128)}) custom-call(s32[512,32]{1,0:T(8,128)} %copy.16.expo_ref, f32[1,32]{1,0:T(1,128)} %bitcast.6, bf16[512,2048]{1,0:T(8,128)(2,1)} %x_ref.3, bf16[512,128]{1,0:T(8,128)(2,1)} %b_ref.3, bf16[512,512]{1,0:T(8,128)(2,1)} %copy-done.16, bf16[512,256]{1,0:T(8,128)(2,1)} %copy-done.23), custom_call_target="tpu_custom_call" | custom-call | flops 512 | bytes 512 | tf_op jit(solution)/shard_map/states/pallas_call | solution.py:517
  37.7 1.1 collective-permute-start.9
  38.8 2.3 %pad_maximum_fusion.2 = bf16[512,1024]{1,0:T(8,128)(2,1)} fusion(bf16[512,512]{1,0:T(8,128)(2,1)} %get-tuple-element.52, bf16[512,512]{1,0:T(8,128)(2,1)} %get-tuple-element.50), kind=kLoop, calls=%fused_computation.3 | loop fusion | flops 2097152 | bytes 2097152 | tf_op jit(solution)/shard_map/concatenate | solution.py:610
  41.1 1.3 collective-permute-start.13
  42.4 1.1 slice.32
  43.5 3.8 %collective-permute-start.2 = (bf16[512,1024]{1,0:T(8,128)(2,1)}, bf16[512,1024]{1,0:T(8,128)(2,1)}, u32[]{:S(2)}, u32[]{:S(2)}) collective-permute-start(bf16[512,1024]{1,0:T(8,128)(2,1)} %slice.32), channel_id=1, source_target_pairs={{4,0},{5,1},{6,2},{7,3},{8,4},{9,5},{10,6},{11,7},{12,8},{13,9},{1... | collective-permute-start | bytes 3145736 | tf_op jit(solution)/shard_map/ppermute | solution.py:605
  47.3 0.9 collective-permute-start.6
  48.8 6.3 %lent.3 = (f32[512,256]{1,0:T(8,128)}, f32[512,128]{1,0:T(8,128)}, bf16[512,384]{1,0:T(8,128)(2,1)}) custom-call(s32[2]{0:T(128)} %pad_add_fusion.side, bf16[512,2048]{1,0:T(8,128)(2,1)} %q_ref.11, bf16[512,256]{1,0:T(8,128)(2,1)} %copy-done.23, bf16[512,2048]{1,0:T(8,128)(2,1)} %ok.11, bf16[512,2048]{1,0:T(8,128)(2,1)} %ov.11, ...), custom_call_target="tpu_custom_call" | custom-call | flops 512 | bytes 512 | tf_op jit(solution)/shard_map/lent/pallas_call | solution.py:166
  55.1 10.4 %intra.1 = (f32[512,2048]{1,0:T(8,128)}, f32[512,32]{1,0:T(8,128)}) custom-call(s32[512,32]{1,0:T(8,128)} %copy.16.expo_ref, f32[1,32]{1,0:T(1,128)} %bitcast.7, f32[32]{0:T(128)} %rates_ref.1, f32[1,32]{1,0:T(1,128)} %bitcast.8, bf16[512,2048]{1,0:T(8,128)(2,1)} %x_ref.3, bf16[512,128]{1,0:T(8,128)(2,1)} %b_ref.3, bf16[512,128]{1,0:T(8,128)(2,1)} %c_ref.3, ...), custom_call_target="tpu_custom_call" | custom-call | flops 512 | bytes 512 | tf_op jit(solution)/shard_map/intra/pallas_call | solution.py:538
  65.5 1.6 copy-done.8
  67.1 0.9 copy-done.9
  68.1 0.9 chip.1
  70.3 10.1 %lent.4 = (f32[512,512]{1,0:T(8,128)}, f32[512,128]{1,0:T(8,128)}, bf16[512,640]{1,0:T(8,128)(2,1)}) custom-call(s32[2]{0:T(128)} %pad_add_fusion.side, bf16[512,2048]{1,0:T(8,128)(2,1)} %q_ref.11, bf16[512,1024]{1,0:T(8,128)(2,1)} %collective-permute-done.2.n_ref, bf16[512,2048]{1,0:T(8,128)(2,1)} %ok.11, bf16[512,2048]{1,0:T(8,128)(2,1)} %ov.11, ...), custom_call_target="tpu_custom_call" | custom-call | flops 512 | bytes 512 | tf_op jit(solution)/shard_map/lent/pallas_call | solution.py:166
  80.5 3.0 %turn.1 = (bf16[512,512]{1,0:T(8,128)(2,1)}, bf16[512,512]{1,0:T(8,128)(2,1)}, bf16[512,512]{1,0:T(8,128)(2,1)}) custom-call(s32[1]{0:T(128)} %bitcast.2.column, bf16[512,1536]{1,0:T(8,128)(2,1)} %pad_maximum_fusion.own_ref, bf16[512,1536]{1,0:T(8,128)(2,1)} %collective-permute-done.z_ref.zk.zv, f32[512,128]{1,0:T(8,128)} %get-tuple-element.31._.refs_0_.l_ref), custom_call_target="tpu_custom_call" | custom-call | flops 100 | bytes 100 | tf_op jit(solution)/shard_map/turn/pallas_call | solution.py:265
  83.5 1.2 collective-permute-start.19
  84.9 1.0 collective-permute-start.23
  86.0 2.9 %broadcast_select_fusion = bf16[512,1536]{1,0:T(8,128)(2,1)} fusion(bf16[512,1536]{1,0:T(8,128)(2,1)} %collective-permute-done.z_ref.zk.zv, pred[]{:T(512)S(6)} %eq.7, bf16[512,768]{1,0:T(8,128)(2,1)S(1)} %copy-done.15, bf16[512,768]{1,0:T(8,128)(2,1)S(1)} %copy-done.13), kind=kLoop, calls=%fused_computation.1 | loop fusion | flops 3932160 | bytes 4718593 | tf_op jit(solution)/shard_map/jit(_where)/select_n | solution.py:646
  88.9 2.4 %collective-permute-start.22 = (bf16[512,384]{1,0:T(8,128)(2,1)S(1)}, bf16[512,384]{1,0:T(8,128)(2,1)S(1)}, u32[]{:S(2)}, u32[]{:S(2)}) collective-permute-start(bf16[512,384]{1,0:T(8,128)(2,1)S(1)} %copy-done.27), channel_id=1, source_target_pairs={{0,4},{1,5},{2,6},{3,7},{4,8},{5,9},{6,10},{7,11},{8,12},{9,13},{1... | collective-permute-start | bytes 1179656 | tf_op jit(solution)/shard_map/ppermute | solution.py:605
  91.7 1.3 collective-permute-start.24
  93.0 8.7 %collective-permute-done.22.got_ref.stat_ref = bf16[512,384]{1,0:T(8,128)(2,1)S(1)} collective-permute-done((bf16[512,384]{1,0:T(8,128)(2,1)S(1)}, bf16[512,384]{1,0:T(8,128)(2,1)S(1)}, u32[]{:S(2)}, u32[]{:S(2)}) %collective-permute-start.22) | collective-permute-done | bytes 393248 | tf_op jit(solution)/shard_map/ppermute | solution.py:605
  102.4 1.9 %collective-permute-start.21 = (bf16[512,640]{1,0:T(8,128)(2,1)}, bf16[512,640]{1,0:T(8,128)(2,1)S(1)}, u32[]{:S(2)}, u32[]{:S(2)}) collective-permute-start(bf16[512,640]{1,0:T(8,128)(2,1)} %get-tuple-element.41), channel_id=1, source_target_pairs={{0,4},{1,5},{2,6},{3,7},{4,8},{5,9},{6,10},{7,11},{8,12},{9,13},{1... | collective-permute-start | bytes 1966088 | tf_op jit(solution)/shard_map/ppermute | solution.py:605
  104.3 3.1 %collective-permute-done.24.came_ref = bf16[128,1024]{1,0:T(8,128)(2,1)S(1)} collective-permute-done((bf16[128,1024]{1,0:T(8,128)(2,1)S(1)}, bf16[128,1024]{1,0:T(8,128)(2,1)S(1)}, u32[]{:S(2)}, u32[]{:S(2)}) %collective-permute-start.24) | collective-permute-done | bytes 262176 | tf_op jit(solution)/shard_map/ppermute | solution.py:605
  107.4 1.0 collective-permute-start.20
  108.6 1.9 %collective-permute-start.25 = (bf16[128,1024]{1,0:T(8,128)(2,1)S(1)}, bf16[128,1024]{1,0:T(8,128)(2,1)S(1)}, u32[]{:S(2)}, u32[]{:S(2)}) collective-permute-start(bf16[128,1024]{1,0:T(8,128)(2,1)S(1)} %get-tuple-element.49), channel_id=1, source_target_pairs={{8,12},{9,13},{10,14},{11,15},{24,28},{25,29},{26,30},{27,31}} | collective-permute-start | bytes 786440 | tf_op jit(solution)/shard_map/ppermute | solution.py:605
  110.5 10.2 %lent.5 = (f32[512,512]{1,0:T(8,128)}, f32[512,128]{1,0:T(8,128)}, bf16[512,640]{1,0:T(8,128)(2,1)}) custom-call(s32[2]{0:T(128)} %pad_add_fusion.side, bf16[512,2048]{1,0:T(8,128)(2,1)} %q_ref.11, bf16[512,1024]{1,0:T(8,128)(2,1)} %collective-permute-done.2.n_ref, bf16[512,2048]{1,0:T(8,128)(2,1)} %ok.11, bf16[512,2048]{1,0:T(8,128)(2,1)} %ov.11, ...), custom_call_target="tpu_custom_call" | custom-call | flops 512 | bytes 512 | tf_op jit(solution)/shard_map/lent/pallas_call | solution.py:166
  120.7 1.9 %collective-permute-start.16 = (bf16[512,640]{1,0:T(8,128)(2,1)}, bf16[512,640]{1,0:T(8,128)(2,1)S(1)}, u32[]{:S(2)}, u32[]{:S(2)}) collective-permute-start(bf16[512,640]{1,0:T(8,128)(2,1)} %get-tuple-element.37), channel_id=1, source_target_pairs={{0,4},{1,5},{2,6},{3,7},{4,8},{5,9},{6,10},{7,11},{8,12},{9,13},{1... | collective-permute-start | bytes 1966088 | tf_op jit(solution)/shard_map/ppermute | solution.py:605
  122.8 3.5 %collective-permute-start.18 = (bf16[512,512]{1,0:T(8,128)(2,1)S(1)}, bf16[512,512]{1,0:T(8,128)(2,1)}, u32[]{:S(2)}, u32[]{:S(2)}) collective-permute-start(bf16[512,512]{1,0:T(8,128)(2,1)S(1)} %collective-permute-done.17.yk.yv), channel_id=1, source_target_pairs={{0,1},{1,0},{2,3},{3,2},{4,5},{5,4},{6,7},{7,6},{8,9},{9,8},{10,11... | collective-permute-start | bytes 1572872 | tf_op jit(solution)/shard_map/ppermute | solution.py:605
  127.7 2.4 %join.3.rest_0_ = bf16[512,2048]{1,0:T(8,128)(2,1)} custom-call(s32[4]{0:T(128)} %compare_convert_fusion.ok_ref, f32[512,256]{1,0:T(8,128)} %get-tuple-element.42.mine_ref, f32[512,128]{1,0:T(8,128)} %get-tuple-element.28._.l_ref, bf16[512,384]{1,0:T(8,128)(2,1)} %copy-done.22, bf16[512,384]{1,0:T(8,128)(2,1)} %copy-done.22), custom_call_target="tpu_custom_call" | custom-call | flops 512 | bytes 512 | tf_op jit(solution)/shard_map/join/pallas_call | solution.py:308
  130.1 3.0 %join.4.rest_0_ = bf16[512,2048]{1,0:T(8,128)(2,1)} custom-call(s32[4]{0:T(128)} %compare_convert_fusion.ok_ref, f32[512,512]{1,0:T(8,128)} %get-tuple-element.40.mine_ref, f32[512,128]{1,0:T(8,128)} %get-tuple-element.31._.refs_0_.l_ref, bf16[512,640]{1,0:T(8,128)(2,1)} %copy-done.17, bf16[512,640]{1,0:T(8,128)(2,1)} %copy-done.17, ...), custom_call_target="tpu_custom_call", output_to_operand_aliasing={{}: (5, {})} | custom-call | flops 512 | bytes 512 | tf_op jit(solution)/shard_map/join/pallas_call | solution.py:308
  133.1 5.7 %relayed.3.rest_0_ = bf16[512,2048]{1,0:T(8,128)(2,1)} custom-call(s32[4]{0:T(128)} %compare_convert_fusion.ok_ref, bf16[512,2048]{1,0:T(8,128)(2,1)} %q_ref.11, bf16[512,2048]{1,0:T(8,128)(2,1)} %ok.11, bf16[512,2048]{1,0:T(8,128)(2,1)} %ov.11, bf16[512,1536]{1,0:T(8,128)(2,1)} %collective-permute-done.z_ref.zk.zv, ...), custom_call_target="tpu_custom_call", output_to_operand_aliasing={{}: (12, {})} | custom-call | flops 512 | bytes 512 | tf_op jit(solution)/shard_map/relayed/pallas_call | solution.py:239
  138.8 5.7 %relayed.4.rest_0_ = bf16[512,2048]{1,0:T(8,128)(2,1)} custom-call(s32[4]{0:T(128)} %compare_convert_fusion.ok_ref, bf16[512,2048]{1,0:T(8,128)(2,1)} %q_ref.11, bf16[512,2048]{1,0:T(8,128)(2,1)} %ok.11, bf16[512,2048]{1,0:T(8,128)(2,1)} %ov.11, bf16[512,1536]{1,0:T(8,128)(2,1)} %collective-permute-done.z_ref.zk.zv, ...), custom_call_target="tpu_custom_call", output_to_operand_aliasing={{}: (12, {})} | custom-call | flops 512 | bytes 512 | tf_op jit(solution)/shard_map/relayed/pallas_call | solution.py:239
  145.3 3.0 %join.5.rest_0_ = bf16[512,2048]{1,0:T(8,128)(2,1)} custom-call(s32[4]{0:T(128)} %compare_convert_fusion.ok_ref, f32[512,512]{1,0:T(8,128)} %get-tuple-element.35.mine_ref, f32[512,128]{1,0:T(8,128)} %get-tuple-element.36.l_ref, bf16[512,640]{1,0:T(8,128)(2,1)} %copy-done.18, bf16[512,640]{1,0:T(8,128)(2,1)} %copy-done.18, ...), custom_call_target="tpu_custom_call", output_to_operand_aliasing={{}: (5, {})} | custom-call | flops 512 | bytes 512 | tf_op jit(solution)/shard_map/join/pallas_call | solution.py:308
  149.0 5.7 %relayed.5 = bf16[512,2048]{1,0:T(8,128)(2,1)} custom-call(s32[4]{0:T(128)} %compare_convert_fusion.ok_ref, bf16[512,2048]{1,0:T(8,128)(2,1)} %q_ref.11, bf16[512,2048]{1,0:T(8,128)(2,1)} %ok.11, bf16[512,2048]{1,0:T(8,128)(2,1)} %ov.11, bf16[512,1536]{1,0:T(8,128)(2,1)} %collective-permute-done.z_ref.zk.zv, ...), custom_call_target="tpu_custom_call", output_to_operand_aliasing={{}: (12, {})} | custom-call | flops 512 | bytes 512 | tf_op jit(solution)/shard_map/relayed/pallas_call | solution.py:239
  155.5 9.8 %final.1 = bf16[512,2048]{1,0:T(8,128)(2,1)} custom-call(s32[1]{0:T(128)} %bitcast.3.core, f32[512,2048]{1,0:T(8,128)} %get-tuple-element.44.pre_ref, f32[512,32]{1,0:T(8,128)} %get-tuple-element.29.refs_0_.factor_ref, bf16[512,128]{1,0:T(8,128)(2,1)} %c_ref.3, f32[128,1024]{1,0:T(8,128)} %copy-done.7, f32[128,1024]{1,0:T(8,128)} %copy-done.24, ...), custom_call_target="tpu_custom_call" | custom-call | flops 512 | bytes 512 | tf_op jit(solution)/shard_map/final/pallas_call | solution.py:569
  (97 shorter events, 9.4 us)
Async XLA Ops:
  0.6 6.2 %copy-start.10 = (bf16[512,2048]{1,0:T(8,128)(2,1)S(1)}, bf16[512,2048]{1,0:T(8,128)(2,1)}, u32[]{:S(2)}) copy-start(bf16[512,2048]{1,0:T(8,128)(2,1)} %ov.11) | copy-start | bytes 6291460
  0.6 42.8 %collective-permute-start.3 = (bf16[512,2048]{1,0:T(8,128)(2,1)}, bf16[512,2048]{1,0:T(8,128)(2,1)}, u32[]{:S(2)}, u32[]{:S(2)}) collective-permute-start(bf16[512,2048]{1,0:T(8,128)(2,1)} %ok.11), channel_id=1, source_target_pairs={{0,1},{1,0},{2,3},{3,2},{4,5},{5,4},{6,7},{7,6},{8,9},{9,8},{10,11... | collective-permute-start | bytes 6291464 | tf_op jit(solution)/shard_map/ppermute | solution.py:605
  1.4 45.9 %collective-permute-start.4 = (bf16[512,2048]{1,0:T(8,128)(2,1)}, bf16[512,2048]{1,0:T(8,128)(2,1)}, u32[]{:S(2)}, u32[]{:S(2)}) collective-permute-start(bf16[512,2048]{1,0:T(8,128)(2,1)} %ov.11), channel_id=1, source_target_pairs={{0,1},{1,0},{2,3},{3,2},{4,5},{5,4},{6,7},{7,6},{8,9},{9,8},{10,11... | collective-permute-start | bytes 6291464 | tf_op jit(solution)/shard_map/ppermute | solution.py:605
  3.5 13.1 %collective-permute-start.7 = (bf16[512,512]{1,0:T(8,128)(2,1)S(1)}, bf16[512,512]{1,0:T(8,128)(2,1)S(1)}, u32[]{:S(2)}, u32[]{:S(2)}) collective-permute-start(bf16[512,512]{1,0:T(8,128)(2,1)S(1)} %pad_maximum_fusion.3), channel_id=1, source_target_pairs={{0,2},{1,3},{2,0},{3,1},{4,6},{5,7},{6,4},{7,5},{8,10},{9,11},{10,... | collective-permute-start | bytes 1572872 | tf_op jit(solution)/shard_map/ppermute | solution.py:605
  8.9 32.2 %collective-permute-start.5 = (bf16[512,1024]{1,0:T(8,128)(2,1)}, bf16[512,1024]{1,0:T(8,128)(2,1)S(1)}, u32[]{:S(2)}, u32[]{:S(2)}) collective-permute-start(bf16[512,1024]{1,0:T(8,128)(2,1)} %pad_maximum_fusion.1), channel_id=1, source_target_pairs={{0,2},{1,3},{2,0},{3,1},{4,6},{5,7},{6,4},{7,5},{8,10},{9,11},{10,... | collective-permute-start | bytes 3145736 | tf_op jit(solution)/shard_map/ppermute | solution.py:605
  16.5 7.9 %copy-start.16 = (bf16[512,512]{1,0:T(8,128)(2,1)}, bf16[512,512]{1,0:T(8,128)(2,1)S(1)}, u32[]{:S(2)}) copy-start(bf16[512,512]{1,0:T(8,128)(2,1)S(1)} %collective-permute-done.7.refs_0_.yk.yv) | copy-start | bytes 1572868
  16.5 21.1 %collective-permute-start.10 = (bf16[512,512]{1,0:T(8,128)(2,1)S(1)}, bf16[512,512]{1,0:T(8,128)(2,1)S(1)}, u32[]{:S(2)}, u32[]{:S(2)}) collective-permute-start(bf16[512,512]{1,0:T(8,128)(2,1)S(1)} %collective-permute-done.7.refs_0_.yk.yv), channel_id=1, source_target_pairs={{0,1},{1,0},{2,3},{3,2},{4,5},{5,4},{6,7},{7,6},{8,9},{9,8},{10,11... | collective-permute-start | bytes 1572872 | tf_op jit(solution)/shard_map/ppermute | solution.py:605
  19.8 9.6 %collective-permute-start.8 = (bf16[512,256]{1,0:T(8,128)(2,1)S(1)}, bf16[512,256]{1,0:T(8,128)(2,1)S(1)}, u32[]{:S(2)}, u32[]{:S(2)}) collective-permute-start(bf16[512,256]{1,0:T(8,128)(2,1)S(1)} %slice.37), channel_id=1, source_target_pairs={{4,0},{5,1},{6,2},{7,3},{8,4},{9,5},{10,6},{11,7},{12,8},{13,9},{1... | collective-permute-start | bytes 786440 | tf_op jit(solution)/shard_map/ppermute | solution.py:605
  23.0 8.3 %copy-start.25 = (s32[512,32]{0,1:T(8,128)S(1)}, s32[512,32]{0,1:T(8,128)}, u32[]{:S(2)}) copy-start(s32[512,32]{0,1:T(8,128)} %param.15) | copy-start | bytes 196612
  23.1 6.2 %copy-start.14 = (bf16[512,768]{1,0:T(8,128)(2,1)}, bf16[512,768]{1,0:T(8,128)(2,1)S(1)}, u32[]{:S(2)}) copy-start(bf16[512,768]{1,0:T(8,128)(2,1)S(1)} %slice.31) | copy-start | bytes 2359300
  29.4 2.8 %copy-start.23 = (bf16[512,256]{1,0:T(8,128)(2,1)}, bf16[512,256]{1,0:T(8,128)(2,1)S(1)}, u32[]{:S(2)}) copy-start(bf16[512,256]{1,0:T(8,128)(2,1)S(1)} %collective-permute-done.8.refs_1_.n_ref) | copy-start | bytes 786436
  29.4 51.1 %collective-permute-start = (bf16[512,1536]{1,0:T(8,128)(2,1)}, bf16[512,1536]{1,0:T(8,128)(2,1)}, u32[]{:S(2)}, u32[]{:S(2)}) collective-permute-start(bf16[512,1536]{1,0:T(8,128)(2,1)} %pad_maximum_fusion.own_ref), channel_id=1, source_target_pairs={{0,4},{1,5},{2,6},{3,7},{4,8},{5,9},{6,10},{7,11},{8,12},{9,13},{1... | collective-permute-start | bytes 4718600 | tf_op jit(solution)/shard_map/ppermute | solution.py:605
  37.7 4.7 %copy-start.11 = (bf16[512,2048]{1,0:T(8,128)(2,1)S(1)}, bf16[512,2048]{1,0:T(8,128)(2,1)}, u32[]{:S(2)}) copy-start(bf16[512,2048]{1,0:T(8,128)(2,1)} %q_ref.11) | copy-start | bytes 6291460
  37.7 3.4 %copy-start.20 = (bf16[512,512]{1,0:T(8,128)(2,1)}, bf16[512,512]{1,0:T(8,128)(2,1)S(1)}, u32[]{:S(2)}) copy-start(bf16[512,512]{1,0:T(8,128)(2,1)S(1)} %collective-permute-done.10.bk.bv) | copy-start | bytes 1572868
  37.7 27.8 %collective-permute-start.9 = (f32[136,2048]{1,0:T(8,128)}, f32[136,2048]{1,0:T(8,128)S(1)}, u32[]{:S(2)}, u32[]{:S(2)}) collective-permute-start(f32[136,2048]{1,0:T(8,128)} %get-tuple-element.26.both_ref), channel_id=1, source_target_pairs={{0,1},{1,0},{2,3},{3,2},{4,5},{5,4},{6,7},{7,6},{8,9},{9,8},{10,11... | collective-permute-start | bytes 3342344 | tf_op jit(solution)/shard_map/ppermute | solution.py:605
  41.1 24.4 %copy-start.1 = (bf16[512,1024]{1,0:T(8,128)(2,1)}, bf16[512,1024]{1,0:T(8,128)(2,1)S(1)}, u32[]{:S(2)}) copy-start(bf16[512,1024]{1,0:T(8,128)(2,1)S(1)} %collective-permute-done.5.refs_1_.yk.yv) | copy-start | bytes 3145732
  41.1 28.9 %collective-permute-start.13 = (bf16[512,1024]{1,0:T(8,128)(2,1)}, bf16[512,1024]{1,0:T(8,128)(2,1)S(1)}, u32[]{:S(2)}, u32[]{:S(2)}) collective-permute-start(bf16[512,1024]{1,0:T(8,128)(2,1)} %pad_maximum_fusion.2), channel_id=1, source_target_pairs={{0,2},{1,3},{2,0},{3,1},{4,6},{5,7},{6,4},{7,5},{8,10},{9,11},{10,... | collective-permute-start | bytes 3145736 | tf_op jit(solution)/shard_map/ppermute | solution.py:605
  43.5 26.9 %collective-permute-start.2 = (bf16[512,1024]{1,0:T(8,128)(2,1)}, bf16[512,1024]{1,0:T(8,128)(2,1)}, u32[]{:S(2)}, u32[]{:S(2)}) collective-permute-start(bf16[512,1024]{1,0:T(8,128)(2,1)} %slice.32), channel_id=1, source_target_pairs={{4,0},{5,1},{6,2},{7,3},{8,4},{9,5},{10,6},{11,7},{12,8},{13,9},{1... | collective-permute-start | bytes 3145736 | tf_op jit(solution)/shard_map/ppermute | solution.py:605
  47.3 23.0 %collective-permute-start.6 = (bf16[512,1024]{1,0:T(8,128)(2,1)S(1)}, bf16[512,1024]{1,0:T(8,128)(2,1)}, u32[]{:S(2)}, u32[]{:S(2)}) collective-permute-start(bf16[512,1024]{1,0:T(8,128)(2,1)S(1)} %collective-permute-done.5.refs_1_.yk.yv), channel_id=1, source_target_pairs={{0,1},{1,0},{2,3},{3,2},{4,5},{5,4},{6,7},{7,6},{8,9},{9,8},{10,11... | collective-permute-start | bytes 3145736 | tf_op jit(solution)/shard_map/ppermute | solution.py:605
  65.5 15.0 %copy-start.3 = (f32[136,2048]{1,0:T(8,128)}, f32[136,2048]{1,0:T(8,128)S(1)}, u32[]{:S(2)}) copy-start(f32[136,2048]{1,0:T(8,128)S(1)} %collective-permute-done.9.other_ref) | copy-start | bytes 3342340
  69.8 15.0 %collective-permute-start.15 = (bf16[144,1024]{1,0:T(8,128)(2,1)}, bf16[144,1024]{1,0:T(8,128)(2,1)S(1)}, u32[]{:S(2)}, u32[]{:S(2)}) collective-permute-start(bf16[144,1024]{1,0:T(8,128)(2,1)} %get-tuple-element.33), channel_id=1, source_target_pairs={{0,2},{1,3},{2,0},{3,1},{4,6},{5,7},{6,4},{7,5},{8,10},{9,11},{10,... | collective-permute-start | bytes 884744 | tf_op jit(solution)/shard_map/ppermute | solution.py:605
  70.0 14.7 %copy-start = (bf16[512,1024]{1,0:T(8,128)(2,1)}, bf16[512,1024]{1,0:T(8,128)(2,1)S(1)}, u32[]{:S(2)}) copy-start(bf16[512,1024]{1,0:T(8,128)(2,1)S(1)} %collective-permute-done.13.refs_1_.yk.yv) | copy-start | bytes 3145732
  70.0 21.7 %collective-permute-start.14 = (bf16[512,1024]{1,0:T(8,128)(2,1)S(1)}, bf16[512,1024]{1,0:T(8,128)(2,1)}, u32[]{:S(2)}, u32[]{:S(2)}) collective-permute-start(bf16[512,1024]{1,0:T(8,128)(2,1)S(1)} %collective-permute-done.13.refs_1_.yk.yv), channel_id=1, source_target_pairs={{0,1},{1,0},{2,3},{3,2},{4,5},{5,4},{6,7},{7,6},{8,9},{9,8},{10,11... | collective-permute-start | bytes 3145736 | tf_op jit(solution)/shard_map/ppermute | solution.py:605
  80.5 4.3 %copy-start.4 = (f32[512,128]{1,0:T(8,128)S(1)}, f32[512,128]{1,0:T(8,128)}, u32[]{:S(2)}) copy-start(f32[512,128]{1,0:T(8,128)} %get-tuple-element.31._.refs_0_.l_ref) | copy-start | bytes 786436
  80.5 4.3 %copy-start.6 = (f32[136,1024]{1,0:T(8,128)S(1)}, f32[136,1024]{1,0:T(8,128)}, u32[]{:S(2)}) copy-start(f32[136,1024]{1,0:T(8,128)} %copy-done.5) | copy-start | bytes 1671172
  80.5 5.5 %copy-start.13 = (bf16[512,768]{1,0:T(8,128)(2,1)S(1)}, bf16[512,768]{1,0:T(8,128)(2,1)}, u32[]{:S(2)}) copy-start(bf16[512,768]{1,0:T(8,128)(2,1)} %copy-done.12) | copy-start | bytes 2359300
  83.5 2.5 %copy-start.15 = (bf16[512,768]{1,0:T(8,128)(2,1)S(1)}, bf16[512,768]{1,0:T(8,128)(2,1)}, u32[]{:S(2)}) copy-start(bf16[512,768]{1,0:T(8,128)(2,1)} %copy-done.14) | copy-start | bytes 2359300
  83.5 18.9 %collective-permute-start.19 = (bf16[512,512]{1,0:T(8,128)(2,1)}, bf16[512,512]{1,0:T(8,128)(2,1)}, u32[]{:S(2)}, u32[]{:S(2)}) collective-permute-start(bf16[512,512]{1,0:T(8,128)(2,1)} %get-tuple-element.39), channel_id=1, source_target_pairs={{0,2},{1,3},{2,0},{3,1},{4,6},{5,7},{6,4},{7,5},{8,10},{9,11},{10,... | collective-permute-start | bytes 1572872 | tf_op jit(solution)/shard_map/ppermute | solution.py:605
  84.9 23.6 %copy-start.2 = (f32[136,1024]{1,0:T(8,128)}, f32[136,1024]{1,0:T(8,128)S(1)}, u32[]{:S(2)}) copy-start(f32[136,1024]{1,0:T(8,128)S(1)} %get-tuple-element.34._.plane_ref) | copy-start | bytes 1671172
  84.9 4.0 %copy-start.27 = (bf16[512,384]{1,0:T(8,128)(2,1)S(1)}, bf16[512,384]{1,0:T(8,128)(2,1)}, u32[]{:S(2)}) copy-start(bf16[512,384]{1,0:T(8,128)(2,1)} %get-tuple-element.43) | copy-start | bytes 1179652
  84.9 6.4 %copy-start.26 = (bf16[512,512]{1,0:T(8,128)(2,1)S(1)}, bf16[512,512]{1,0:T(8,128)(2,1)}, u32[]{:S(2)}) copy-start(bf16[512,512]{1,0:T(8,128)(2,1)} %get-tuple-element.38) | copy-start | bytes 1572868
  84.9 6.3 %collective-permute-start.23 = (bf16[128,1024]{1,0:T(8,128)(2,1)S(1)}, bf16[128,1024]{1,0:T(8,128)(2,1)S(1)}, u32[]{:S(2)}, u32[]{:S(2)}) collective-permute-start(bf16[128,1024]{1,0:T(8,128)(2,1)S(1)} %get-tuple-element.45), channel_id=1, source_target_pairs={{0,4},{1,5},{2,6},{3,7},{16,20},{17,21},{18,22},{19,23}} | collective-permute-start | bytes 786440 | tf_op jit(solution)/shard_map/ppermute | solution.py:605
  88.9 44.2 %collective-permute-start.1 = (bf16[512,1536]{1,0:T(8,128)(2,1)}, bf16[512,1536]{1,0:T(8,128)(2,1)}, u32[]{:S(2)}, u32[]{:S(2)}) collective-permute-start(bf16[512,1536]{1,0:T(8,128)(2,1)} %broadcast_select_fusion), channel_id=1, source_target_pairs={{0,1},{1,0},{2,3},{3,2},{4,5},{5,4},{6,7},{7,6},{8,9},{9,8},{10,11... | collective-permute-start | bytes 4718600 | tf_op jit(solution)/shard_map/ppermute | solution.py:605
  88.9 12.9 %collective-permute-start.22 = (bf16[512,384]{1,0:T(8,128)(2,1)S(1)}, bf16[512,384]{1,0:T(8,128)(2,1)S(1)}, u32[]{:S(2)}, u32[]{:S(2)}) collective-permute-start(bf16[512,384]{1,0:T(8,128)(2,1)S(1)} %copy-done.27), channel_id=1, source_target_pairs={{0,4},{1,5},{2,6},{3,7},{4,8},{5,9},{6,10},{7,11},{8,12},{9,13},{1... | collective-permute-start | bytes 1179656 | tf_op jit(solution)/shard_map/ppermute | solution.py:605
  91.3 17.3 %collective-permute-start.17 = (bf16[512,512]{1,0:T(8,128)(2,1)S(1)}, bf16[512,512]{1,0:T(8,128)(2,1)S(1)}, u32[]{:S(2)}, u32[]{:S(2)}) collective-permute-start(bf16[512,512]{1,0:T(8,128)(2,1)S(1)} %copy-done.26), channel_id=1, source_target_pairs={{0,2},{1,3},{2,0},{3,1},{4,6},{5,7},{6,4},{7,5},{8,10},{9,11},{10,... | collective-permute-start | bytes 1572872 | tf_op jit(solution)/shard_map/ppermute | solution.py:605
  91.7 15.7 %collective-permute-start.24 = (bf16[128,1024]{1,0:T(8,128)(2,1)S(1)}, bf16[128,1024]{1,0:T(8,128)(2,1)S(1)}, u32[]{:S(2)}, u32[]{:S(2)}) collective-permute-start(bf16[128,1024]{1,0:T(8,128)(2,1)S(1)} %get-tuple-element.47), channel_id=1, source_target_pairs={{4,8},{5,9},{6,10},{7,11},{20,24},{21,25},{22,26},{23,27}} | collective-permute-start | bytes 786440 | tf_op jit(solution)/shard_map/ppermute | solution.py:605
  101.8 6.8 %copy-start.22 = (bf16[512,384]{1,0:T(8,128)(2,1)}, bf16[512,384]{1,0:T(8,128)(2,1)S(1)}, u32[]{:S(2)}) copy-start(bf16[512,384]{1,0:T(8,128)(2,1)S(1)} %collective-permute-done.22.got_ref.stat_ref) | copy-start | bytes 1179652
  101.8 18.9 %collective-permute-start.11 = (bf16[512,512]{1,0:T(8,128)(2,1)}, bf16[512,512]{1,0:T(8,128)(2,1)}, u32[]{:S(2)}, u32[]{:S(2)}) collective-permute-start(bf16[512,512]{1,0:T(8,128)(2,1)} %get-tuple-element.32), channel_id=1, source_target_pairs={{0,2},{1,3},{2,0},{3,1},{4,6},{5,7},{6,4},{7,5},{8,10},{9,11},{10,... | collective-permute-start | bytes 1572872 | tf_op jit(solution)/shard_map/ppermute | solution.py:605
  102.4 24.1 %collective-permute-start.21 = (bf16[512,640]{1,0:T(8,128)(2,1)}, bf16[512,640]{1,0:T(8,128)(2,1)S(1)}, u32[]{:S(2)}, u32[]{:S(2)}) collective-permute-start(bf16[512,640]{1,0:T(8,128)(2,1)} %get-tuple-element.41), channel_id=1, source_target_pairs={{0,4},{1,5},{2,6},{3,7},{4,8},{5,9},{6,10},{7,11},{8,12},{9,13},{1... | collective-permute-start | bytes 1966088 | tf_op jit(solution)/shard_map/ppermute | solution.py:605
  107.4 19.2 %collective-permute-start.20 = (bf16[512,512]{1,0:T(8,128)(2,1)}, bf16[512,512]{1,0:T(8,128)(2,1)}, u32[]{:S(2)}, u32[]{:S(2)}) collective-permute-start(bf16[512,512]{1,0:T(8,128)(2,1)} %collective-permute-done.19.yk.yv), channel_id=1, source_target_pairs={{0,1},{1,0},{2,3},{3,2},{4,5},{5,4},{6,7},{7,6},{8,9},{9,8},{10,11... | collective-permute-start | bytes 1572872 | tf_op jit(solution)/shard_map/ppermute | solution.py:605
  108.6 14.3 %copy-start.19 = (bf16[512,512]{1,0:T(8,128)(2,1)}, bf16[512,512]{1,0:T(8,128)(2,1)S(1)}, u32[]{:S(2)}) copy-start(bf16[512,512]{1,0:T(8,128)(2,1)S(1)} %collective-permute-done.17.yk.yv) | copy-start | bytes 1572868
  108.6 14.3 %collective-permute-start.25 = (bf16[128,1024]{1,0:T(8,128)(2,1)S(1)}, bf16[128,1024]{1,0:T(8,128)(2,1)S(1)}, u32[]{:S(2)}, u32[]{:S(2)}) collective-permute-start(bf16[128,1024]{1,0:T(8,128)(2,1)S(1)} %get-tuple-element.49), channel_id=1, source_target_pairs={{8,12},{9,13},{10,14},{11,15},{24,28},{25,29},{26,30},{27,31}} | collective-permute-start | bytes 786440 | tf_op jit(solution)/shard_map/ppermute | solution.py:605
  120.7 23.7 %collective-permute-start.16 = (bf16[512,640]{1,0:T(8,128)(2,1)}, bf16[512,640]{1,0:T(8,128)(2,1)S(1)}, u32[]{:S(2)}, u32[]{:S(2)}) collective-permute-start(bf16[512,640]{1,0:T(8,128)(2,1)} %get-tuple-element.37), channel_id=1, source_target_pairs={{0,4},{1,5},{2,6},{3,7},{4,8},{5,9},{6,10},{7,11},{8,12},{9,13},{1... | collective-permute-start | bytes 1966088 | tf_op jit(solution)/shard_map/ppermute | solution.py:605
  122.8 15.9 %collective-permute-start.18 = (bf16[512,512]{1,0:T(8,128)(2,1)S(1)}, bf16[512,512]{1,0:T(8,128)(2,1)}, u32[]{:S(2)}, u32[]{:S(2)}) collective-permute-start(bf16[512,512]{1,0:T(8,128)(2,1)S(1)} %collective-permute-done.17.yk.yv), channel_id=1, source_target_pairs={{0,1},{1,0},{2,3},{3,2},{4,5},{5,4},{6,7},{7,6},{8,9},{9,8},{10,11... | collective-permute-start | bytes 1572872 | tf_op jit(solution)/shard_map/ppermute | solution.py:605
  126.4 6.7 %copy-start.7 = (f32[128,1024]{1,0:T(8,128)}, f32[128,1024]{1,0:T(8,128)S(1)}, u32[]{:S(2)}) copy-start(f32[128,1024]{1,0:T(8,128)S(1)} %arrive.1.mine_ref) | copy-start | bytes 1572868
  126.5 3.6 %copy-start.17 = (bf16[512,640]{1,0:T(8,128)(2,1)}, bf16[512,640]{1,0:T(8,128)(2,1)S(1)}, u32[]{:S(2)}) copy-start(bf16[512,640]{1,0:T(8,128)(2,1)S(1)} %collective-permute-done.21.got_ref.stat_ref) | copy-start | bytes 1966084
  126.5 21.8 %collective-permute-start.12 = (bf16[512,512]{1,0:T(8,128)(2,1)}, bf16[512,512]{1,0:T(8,128)(2,1)S(1)}, u32[]{:S(2)}, u32[]{:S(2)}) collective-permute-start(bf16[512,512]{1,0:T(8,128)(2,1)} %collective-permute-done.11.yk.yv), channel_id=1, source_target_pairs={{0,1},{1,0},{2,3},{3,2},{4,5},{5,4},{6,7},{7,6},{8,9},{9,8},{10,11... | collective-permute-start | bytes 1572872 | tf_op jit(solution)/shard_map/ppermute | solution.py:605
  126.6 28.2 %collective-permute-start.26 = (f32[128,1024]{1,0:T(8,128)S(1)}, f32[128,1024]{1,0:T(8,128)S(1)}, u32[]{:S(2)}, u32[]{:S(2)}) collective-permute-start(f32[128,1024]{1,0:T(8,128)S(1)} %arrive.1.mine_ref), channel_id=1, source_target_pairs={{0,1},{1,0},{2,3},{3,2},{4,5},{5,4},{6,7},{7,6},{8,9},{9,8},{10,11... | collective-permute-start | bytes 1572872 | tf_op jit(solution)/shard_map/ppermute | solution.py:605
  (7 other events, 7.3 us)

commit v3 on v2

--- a/solution.py
+++ b/solution.py
@@ -42,6 +42,22 @@
 
 def split_contract(a, b, terms=2):
     return sum(contract(part, b) for part in split_bf16(a, terms))
+
+
+def gate_kernel(array_ref, *refs):
+    pass
+
+
+def gate(array, *after):
+    return pl.pallas_call(
+        gate_kernel,
+        in_specs=[HBM] * (1 + len(after)),
+        out_specs=HBM,
+        out_shape=jax.ShapeDtypeStruct(array.shape, array.dtype),
+        input_output_aliases={0: 0},
+        cost_estimate=pl.CostEstimate(flops=1, bytes_accessed=1, transcendentals=0),
+        name="gate",
+    )(array, *after)
 
 
 def scaled(q):
@@ -180,9 +196,7 @@
 
 
 def attention_cost(heads, rows):
-    return pl.CostEstimate(
-        flops=rows, bytes_accessed=rows, transcendentals=0
-    )
+    return pl.CostEstimate(flops=int(heads * rows * 1), bytes_accessed=rows, transcendentals=0)
 
 
 def relayed_kernel(ok_ref, q_ref, ok, ov, zk, zv, ak, av, yk, yv, bk, bv, *rest):
@@ -293,13 +307,15 @@
         o_ref[:, cols] = (back + weight * (mine_ref[:, cols] - back)).astype(o_ref.dtype)
 
 
-def join(start, heads, flags, mine, l, got, width, result):
+def join(start, heads, flags, mine, l, got, width, after, result):
     rows = mine.shape[0]
     wide = PAIR * E
     part = pl.BlockSpec((rows, wide), lambda i: (0, i))
     args = [flags, mine, l, got, got]
     specs = [SCALARS, part, pl.BlockSpec((rows, E), lambda i: (0, 0)), part]
     specs.append(pl.BlockSpec((rows, E), lambda i: (0, heads)))
+    args.append(after)
+    specs.append(HBM)
     aliases = {}
     if result is not None:
         aliases = {len(args): 0}
@@ -319,7 +335,7 @@
 
 
 def running_expo(expo_ref):
-    size = expo_ref.shape[0]
+    size = expo_ref.shape[1]
     expo = expo_ref[...]
     high = (expo >> 8).astype(jnp.float32).astype(jnp.bfloat16)
     low = (expo & 255).astype(jnp.float32).astype(jnp.bfloat16)
@@ -327,8 +343,8 @@
     col = lax.broadcasted_iota(jnp.int32, (size, size), 1)
     lower = jnp.where(row >= col, 1.0, 0.0).astype(jnp.bfloat16)
     upper = jnp.where(row <= col, 1.0, 0.0).astype(jnp.bfloat16)
-    down = contract(lower, high) * 256.0 + contract(lower, low)
-    across = contract(high, upper, ((0,), (0,))) * 256.0 + contract(low, upper, ((0,), (0,)))
+    down = contract(lower, high, ((1,), (1,))) * 256.0 + contract(lower, low, ((1,), (1,)))
+    across = contract(high, upper) * 256.0 + contract(low, upper)
     return down, across
 
 
@@ -342,7 +358,7 @@
 
 def states_kernel(expo_ref, rate_ref, x_ref, b_ref, *refs):
     local_ref, both_ref = refs[-2:]
-    heads, width, state = expo_ref.shape[1], x_ref.shape[1], b_ref.shape[1]
+    heads, width, state = expo_ref.shape[0], x_ref.shape[1], b_ref.shape[1]
 
     @pl.when(pl.program_id(0) == 0)
     def _():
@@ -358,13 +374,17 @@
     weighted = x_ref[...].astype(jnp.float32) * weights
     new = sum(contract(b_ref[...], part, ((0,), (0,))) for part in split_bf16(weighted, 2))
     before = both_ref[:state, :]
-    local_ref[...] = before
+
+    @pl.when(pl.program_id(0) > 0)
+    def _():
+        local_ref[...] = before
+
     both_ref[:state, :] = before * decay[:1, :] + new
     both_ref[state:, :] = both_ref[state:, :] * decay
 
 
 def intra_kernel(expo_ref, rate_ref, rates_ref, skip_ref, x_ref, b_ref, c_ref, local_ref, _, pre_ref, factor_ref, past):
-    size, heads = expo_ref.shape
+    heads, size = expo_ref.shape
     width = x_ref.shape[1]
     dim = width // heads
     half = size // 2
@@ -379,10 +399,15 @@
     past[...] = past[...] + down[-1:, :]
     c = c_ref[...]
     spread = spread_matrix(heads, width)
-    within = split_contract(jnp.exp(-rate * down), spread)
-    carried = sum(contract(c, part) for part in split_bf16(local_ref[...], 2))
     skip = split_contract(jnp.broadcast_to(skip_ref[...], (8, heads)), spread, 3)[:1, :]
-    pre_ref[...] = carried * within + skip * x_ref[...].astype(jnp.float32)
+    pre_ref[...] = skip * x_ref[...].astype(jnp.float32)
+
+    @pl.when(pl.program_id(0) > 0)
+    def _():
+        within = split_contract(jnp.exp(-rate * down), spread)
+        carried = sum(contract(c, part) for part in split_bf16(local_ref[...], 2))
+        pre_ref[...] += carried * within
+
     cross = contract(c, b_ref[...], ((1,), (1,)))
     row = lax.broadcasted_iota(jnp.int32, (half, half), 0)
     col = lax.broadcasted_iota(jnp.int32, (half, half), 1)
@@ -511,42 +536,42 @@
 
 
 def recurrence_states(expo, rate, ssd_input, bmat, after):
-    length, heads = expo.shape
+    heads, length = expo.shape
     width, state = ssd_input.shape[1], bmat.shape[1]
     blocks = length // Q
     return pl.pallas_call(
         states_kernel,
         grid=(blocks,),
-        in_specs=[by_block(heads), once(1, heads), by_block(width), by_block(state)] + [HBM] * len(after),
-        out_specs=[pl.BlockSpec((state, width), lambda b: (b, 0)), once(state + 8, width)],
+        in_specs=[pl.BlockSpec((heads, Q), lambda b: (0, b)), once(1, heads), by_block(width), by_block(state)] + [HBM] * len(after),
+        out_specs=[pl.BlockSpec((state, width), lambda b: (jnp.maximum(b - 1, 0), 0)), once(state + 8, width)],
         out_shape=[
-            jax.ShapeDtypeStruct((blocks * state, width), jnp.float32),
+            jax.ShapeDtypeStruct(((blocks - 1) * state, width), jnp.float32),
             jax.ShapeDtypeStruct((state + 8, width), jnp.float32),
         ],
         compiler_params=params(60),
         cost_estimate=pl.CostEstimate(
-            flops=length, bytes_accessed=length, transcendentals=0
+            flops=int(length * 1), bytes_accessed=length, transcendentals=0
         ),
         name="states",
     )(expo, rate[None], ssd_input, bmat, *after)
 
 
 def recurrence_intra(expo, rate, skip, ssd_input, bmat, cmat, local, after):
-    length, heads = expo.shape
+    heads, length = expo.shape
     width, state = ssd_input.shape[1], bmat.shape[1]
     blocks = length // Q
     return pl.pallas_call(
         intra_kernel,
         grid=(blocks,),
         in_specs=[
-            by_block(heads),
+            pl.BlockSpec((heads, Q), lambda b: (0, b)),
             once(1, heads),
             SCALARS,
             once(1, heads),
             by_block(width),
             by_block(state),
             by_block(state),
-            pl.BlockSpec((state, width), lambda b: (b, 0)),
+            pl.BlockSpec((state, width), lambda b: (jnp.maximum(b - 1, 0), 0)),
             HBM,
         ],
         out_specs=[by_block(width), by_block(heads)],
@@ -557,7 +582,7 @@
         scratch_shapes=[pltpu.VMEM((1, heads), jnp.float32)],
         compiler_params=params(60),
         cost_estimate=pl.CostEstimate(
-            flops=length, bytes_accessed=length, transcendentals=0
+            flops=int(length * 1), bytes_accessed=length, transcendentals=0
         ),
         name="intra",
     )(expo, rate[None], rate, skip[None], ssd_input, bmat, cmat, local, after)
@@ -580,9 +605,9 @@
         ],
         out_specs=by_block(width),
         out_shape=jax.ShapeDtypeStruct((length, width), jnp.bfloat16),
-        compiler_params=params(60),
+        compiler_params=params(24),
         cost_estimate=pl.CostEstimate(
-            flops=length, bytes_accessed=length, transcendentals=0
+            flops=int(length * 1), bytes_accessed=length, transcendentals=0
         ),
         name="final",
     )(core, pre, factor, cmat, mine, theirs, other)
@@ -615,22 +640,22 @@
     to_z = packed(lent_total, relayed_total)
     by_z = send(to_z, forward)
     partner_k, partner_v = send(keys, partner), send(values, partner)
-    by_b = [send(y, partner) for y in by_y]
 
     side = jnp.stack([core, column]).astype(jnp.int32)
     near = jnp.where(core == 0, 3, 1)
     distance = jnp.stack([jnp.int32(4), near, jnp.int32(2), 4 - near])
     flags = (here >= distance).astype(jnp.int32)
 
-    def lent(i, after):
+    def lent(i, after, y):
         asked, offset = (asked_first, 0) if i == 0 else (asked_later, starts[i] - LENT[0])
         return lent_heads(
-            starts[i], LENT[i], offset, side, queries, asked, keys, values, partner_k, partner_v, by_y[i], by_b[i], after
+            starts[i], LENT[i], offset, side, queries, asked, keys, values, partner_k, partner_v, y, send(y, partner), after
         )
 
-    local, both = recurrence_states(expo, rate, ssd_input, bmat, [by_y[0], asked_first])
+    expo = expo.T
+    local, both = recurrence_states(expo, rate, ssd_input, bmat, [])
     other = send(both, partner)
-    partial = [lent(0, local)]
+    partial = [lent(0, local, by_y[0])]
     pre, factor = recurrence_intra(expo, rate, skip, ssd_input, bmat, cmat, local, partial[0][1])
     state = bmat.shape[1]
     wide = ssd_input.shape[1] // 2
@@ -639,19 +664,19 @@
         chip_kernel, "chip", [((state + 8, wide), full), ((state + 16, wide), brief)], [core_1], both, other, after=[factor, by_y[1]]
     )
     got = send(rows, across)
-    partial.append(lent(1, chip))
+    partial.append(lent(1, chip, by_y[1]))
     plane, leaving = small(
-        plane_kernel, "plane", [((state + 8, wide), full), ((state, wide), brief)], [column_1], chip, got, after=[partial[1][1], by_y[2]]
+        plane_kernel, "plane", [((state + 8, wide), full), ((state, wide), brief)], [column_1], chip, got, after=[partial[1][1]]
     )
     by_a = send(jnp.where(core == 0, to_z, by_z), partner)
-    turned = turn(len(RELAYED), column_1, to_z, by_z, partial[1][1])
+    turned = turn(len(RELAYED), column_1, to_z, by_z, factor)
     last_y = [send(part, across) for part in turned]
     last_b = [send(part, partner) for part in last_y]
     entering = jnp.zeros((state, wide), jnp.float32)
     for s in range(planes - 1):
         came = send(leaving, [(s * span + j, (s + 1) * span + j) for j in range(span)])
         if s == 0:
-            partial.append(lent(2, plane))
+            partial += [lent(i, plane, by_y[i]) for i in range(2, len(LENT))]
         if s < planes - 2:
             entering, leaving = small(
                 hop_kernel, "hop", [((state, wide), full), ((state, wide), brief)], [], plane, entering, came
@@ -663,10 +688,10 @@
     back = [send(message, forward) for _, _, message in partial]
     attn_out = None
     for i, (s, n) in enumerate(zip(starts[:-1], LENT)):
-        attn_out = join(s, n, flags, partial[i][0], partial[i][1], back[i], width, attn_out)
+        attn_out = join(s, n, flags, partial[i][0], partial[i][1], back[i], width, partial[-1][1], attn_out)
     for i in range(len(RELAYED)):
         if i == len(RELAYED) - 1:
-            attn_out = join(starts[-1], LENT[-1], flags, partial[-1][0], partial[-1][1], back[-1], width, attn_out)
+            attn_out = join(starts[-1], LENT[-1], flags, partial[-1][0], partial[-1][1], back[-1], width, bmat, attn_out)
         offset = sum(RELAYED[:i])
         attn_out = relayed_heads(
             lent_total + offset, offset, relayed_total, flags, queries, keys, values, by_z, by_a, last_y[i], last_b[i], attn_out

time: 168 us -> 163 us (0.970)
  local copies, waits for them, and re-layouts: 15 us -> 11.6 us
  Pallas kernels: 81.9 us -> 79 us
  waiting for transfers between devices: 24.5 us -> 27.4 us
    ppermute x27, waiting for transfers between devices: 24.5 us -> 27.4 us  [on_device(): send = lambda array, route: lax.ppermute(array, 'seq', route)]
    pallas_call x1, Pallas kernels: 9.77 us -> 7.41 us  [recurrence_final(): pl.pallas_call(final_kernel, grid=(length // Q,), in_specs=[SCALARS, by_b...]
    unnamed x57 -> x44, local copies, waits for them, and re-layouts: 6.8 us -> 4.94 us
  transfers between devices with their start and end apart: 27 -> 27, of which waited for: 5 -> 6; matrix products, arithmetic and copies ran while one was open for 11% -> 9% of each run, Pallas kernels for 44% -> 44%
where the time goes in v3:
time: 163 us; the launch traced here: 161 us
  Pallas kernels  79 us (48%)
  starting transfers between devices  34.3 us (21%)
  waiting for transfers between devices  27.4 us (17%)
  local copies, waits for them, and re-layouts  11.6 us (7%)
  other arithmetic  8.09 us (5%)
    ppermute x27, starting transfers between devices, on_device(): send = lambda array, route: lax.ppermute(array, 'seq', route)  34.3 us
    ppermute x27, waiting for transfers between devices, on_device(): send = lambda array, route: lax.ppermute(array, 'seq', route)  27.4 us
    pallas_call x3, Pallas kernels, lent_heads(): pl.pallas_call(functools.partial(lent_kernel, heads), grid=(pairs,), in_s...  26.5 us
    pallas_call x3, Pallas kernels, relayed_heads(): pl.pallas_call(relayed_kernel, grid=(1,), in_specs=[SCALARS] + [own] * 3...  17 us
    pallas_call x1, Pallas kernels, recurrence_intra(): pl.pallas_call(intra_kernel, grid=(blocks,), in_specs=[pl.BlockSpec((head...  9.6 us
    pallas_call x3, Pallas kernels, join(): pl.pallas_call(join_kernel, grid=(heads // PAIR,), in_specs=specs, out_sp...  8.41 us
    pallas_call x1, Pallas kernels, recurrence_final(): pl.pallas_call(final_kernel, grid=(length // Q,), in_specs=[SCALARS, by_b...  7.41 us
    slice x8, local copies, waits for them, and re-layouts, on_device(): columns = lambda array, s, n: array[:, s * E:(s + n) * E]  6.61 us
  transfers between devices with their start and end apart: 27, of which 6 were waited for; matrix products, arithmetic and copies ran while one was open for 9% of the time, Pallas kernels for 44%

profile of v3, /device:TPU:17, one launch (start us, length us, event | category | flops | bytes accessed | tf_op | source)
XLA Modules:
  0.0 161.4 jit_solution(11810328056382879045)
XLA Ops:
  1.5 1.0 slice.33
  2.4 1.0 slice.34
  3.5 1.3 collective-permute-start.5
  4.8 1.3 fusion
  6.1 1.1 pad_maximum_fusion.2
  7.5 9.0 %collective-permute-done.5.yk.yv = bf16[512,512]{1,0:T(8,128)(2,1)S(1)} collective-permute-done((bf16[512,512]{1,0:T(8,128)(2,1)S(1)}, bf16[512,512]{1,0:T(8,128)(2,1)S(1)}, u32[]{:S(2)}, u32[]{:S(2)}) %collective-permute-start.5) | collective-permute-done | bytes 524320 | tf_op jit(solution)/shard_map/ppermute | solution.py:630
  16.5 2.2 %collective-permute-start.6 = (bf16[512,512]{1,0:T(8,128)(2,1)S(1)}, bf16[512,512]{1,0:T(8,128)(2,1)S(1)}, u32[]{:S(2)}, u32[]{:S(2)}) collective-permute-start(bf16[512,512]{1,0:T(8,128)(2,1)S(1)} %collective-permute-done.5.yk.yv), channel_id=1, source_target_pairs={{0,1},{1,0},{2,3},{3,2},{4,5},{5,4},{6,7},{7,6},{8,9},{9,8},{10,11... | collective-permute-start | bytes 1572872 | tf_op jit(solution)/shard_map/ppermute | solution.py:630
  18.8 1.0 slice.32
  19.8 2.1 %collective-permute-start.2 = (bf16[512,256]{1,0:T(8,128)(2,1)S(1)}, bf16[512,256]{1,0:T(8,128)(2,1)S(1)}, u32[]{:S(2)}, u32[]{:S(2)}) collective-permute-start(bf16[512,256]{1,0:T(8,128)(2,1)S(1)} %slice.32), channel_id=1, source_target_pairs={{4,0},{5,1},{6,2},{7,3},{8,4},{9,5},{10,6},{11,7},{12,8},{13,9},{1... | collective-permute-start | bytes 786440 | tf_op jit(solution)/shard_map/ppermute | solution.py:630
  21.8 1.2 slice.30
  23.1 1.4 pad_maximum_fusion.own_ref
  24.5 4.8 %collective-permute-done.2.n_ref = bf16[512,256]{1,0:T(8,128)(2,1)S(1)} collective-permute-done((bf16[512,256]{1,0:T(8,128)(2,1)S(1)}, bf16[512,256]{1,0:T(8,128)(2,1)S(1)}, u32[]{:S(2)}, u32[]{:S(2)}) %collective-permute-start.2) | collective-permute-done | bytes 262176 | tf_op jit(solution)/shard_map/ppermute | solution.py:630
  29.4 1.9 %collective-permute-start = (bf16[512,1536]{1,0:T(8,128)(2,1)}, bf16[512,1536]{1,0:T(8,128)(2,1)}, u32[]{:S(2)}, u32[]{:S(2)}) collective-permute-start(bf16[512,1536]{1,0:T(8,128)(2,1)} %pad_maximum_fusion.own_ref), channel_id=1, source_target_pairs={{0,4},{1,5},{2,6},{3,7},{4,8},{5,9},{6,10},{7,11},{8,12},{9,13},{1... | collective-permute-start | bytes 4718600 | tf_op jit(solution)/shard_map/ppermute | solution.py:630
  31.3 5.8 %states.1 = (f32[128,2048]{1,0:T(8,128)}, f32[136,2048]{1,0:T(8,128)}) custom-call(s32[32,512]{1,0:T(8,128)} %bitcast.7, f32[1,32]{1,0:T(1,128)} %bitcast.9, bf16[512,2048]{1,0:T(8,128)(2,1)} %x_ref.3, bf16[512,128]{1,0:T(8,128)(2,1)} %rest_0_.1), custom_call_target="tpu_custom_call" | custom-call | flops 512 | bytes 512 | tf_op jit(solution)/shard_map/states/pallas_call | solution.py:542
  37.1 1.1 collective-permute-start.12
  38.2 1.1 pad_maximum_fusion.1
  39.4 1.3 collective-permute-start.10
  40.7 1.1 slice.35
  41.8 3.8 %collective-permute-start.9 = (bf16[512,1024]{1,0:T(8,128)(2,1)}, bf16[512,1024]{1,0:T(8,128)(2,1)}, u32[]{:S(2)}, u32[]{:S(2)}) collective-permute-start(bf16[512,1024]{1,0:T(8,128)(2,1)} %slice.35), channel_id=1, source_target_pairs={{4,0},{5,1},{6,2},{7,3},{8,4},{9,5},{10,6},{11,7},{12,8},{13,9},{1... | collective-permute-start | bytes 3145736 | tf_op jit(solution)/shard_map/ppermute | solution.py:630
  46.8 6.2 %lent.3 = (f32[512,256]{1,0:T(8,128)}, f32[512,128]{1,0:T(8,128)}, bf16[512,384]{1,0:T(8,128)(2,1)}) custom-call(s32[2]{0:T(128)} %pad_add_fusion.side, bf16[512,2048]{1,0:T(8,128)(2,1)} %q_ref.11, bf16[512,256]{1,0:T(8,128)(2,1)} %copy-done.19, bf16[512,2048]{1,0:T(8,128)(2,1)} %ok.11, bf16[512,2048]{1,0:T(8,128)(2,1)} %ov.11, ...), custom_call_target="tpu_custom_call" | custom-call | flops 1024 | bytes 512 | tf_op jit(solution)/shard_map/lent/pallas_call | solution.py:182
  53.1 9.6 %intra.1 = (f32[512,2048]{1,0:T(8,128)}, f32[512,32]{1,0:T(8,128)}) custom-call(s32[32,512]{1,0:T(8,128)} %bitcast.8, f32[1,32]{1,0:T(1,128)} %bitcast.10, f32[32]{0:T(128)} %rates_ref.1, f32[1,32]{1,0:T(1,128)} %bitcast.11, bf16[512,2048]{1,0:T(8,128)(2,1)} %x_ref.3, bf16[512,128]{1,0:T(8,128)(2,1)} %rest_0_.1, bf16[512,128]{1,0:T(8,128)(2,1)} %c_ref.3, ...), custom_call_target="tpu_custom_call" | custom-call | flops 512 | bytes 512 | tf_op jit(solution)/shard_map/intra/pallas_call | solution.py:563
  62.7 0.9 copy-done.3
  63.6 0.8 chip.1
  66.5 2.8 %turn.1 = (bf16[512,512]{1,0:T(8,128)(2,1)}, bf16[512,512]{1,0:T(8,128)(2,1)}, bf16[512,512]{1,0:T(8,128)(2,1)}) custom-call(s32[1]{0:T(128)} %bitcast.2.column, bf16[512,1536]{1,0:T(8,128)(2,1)} %pad_maximum_fusion.own_ref, bf16[512,1536]{1,0:T(8,128)(2,1)} %collective-permute-done.z_ref.zk.zv, f32[512,32]{1,0:T(8,128)} %get-tuple-element.28._.refs_0_.factor_ref), custom_call_target="tpu_custom_call" | custom-call | flops 100 | bytes 100 | tf_op jit(solution)/shard_map/turn/pallas_call | solution.py:279
  69.3 1.2 collective-permute-start.19
  70.6 10.2 %lent.4 = (f32[512,512]{1,0:T(8,128)}, f32[512,128]{1,0:T(8,128)}, bf16[512,640]{1,0:T(8,128)(2,1)}) custom-call(s32[2]{0:T(128)} %pad_add_fusion.side, bf16[512,2048]{1,0:T(8,128)(2,1)} %q_ref.11, bf16[512,1024]{1,0:T(8,128)(2,1)} %collective-permute-done.9.n_ref, bf16[512,2048]{1,0:T(8,128)(2,1)} %ok.11, bf16[512,2048]{1,0:T(8,128)(2,1)} %ov.11, ...), custom_call_target="tpu_custom_call" | custom-call | flops 2048 | bytes 512 | tf_op jit(solution)/shard_map/lent/pallas_call | solution.py:182
  80.8 0.9 copy-done.8
  81.9 1.0 collective-permute-start.23
  82.9 3.1 %broadcast_select_fusion = bf16[512,1536]{1,0:T(8,128)(2,1)} fusion(bf16[512,1536]{1,0:T(8,128)(2,1)} %collective-permute-done.z_ref.zk.zv, pred[]{:T(512)S(6)} %eq.7, bf16[512,768]{1,0:T(8,128)(2,1)} %copy-done.14, bf16[512,768]{1,0:T(8,128)(2,1)S(1)} %copy-done.13), kind=kLoop, calls=%fused_computation.1 | loop fusion | flops 3932160 | bytes 4718593 | tf_op jit(solution)/shard_map/jit(_where)/select_n | solution.py:671
  86.1 1.7 %collective-permute-start.1 = (bf16[512,1536]{1,0:T(8,128)(2,1)}, bf16[512,1536]{1,0:T(8,128)(2,1)}, u32[]{:S(2)}, u32[]{:S(2)}) collective-permute-start(bf16[512,1536]{1,0:T(8,128)(2,1)} %broadcast_select_fusion), channel_id=1, source_target_pairs={{0,1},{1,0},{2,3},{3,2},{4,5},{5,4},{6,7},{7,6},{8,9},{9,8},{10,11... | collective-permute-start | bytes 4718600 | tf_op jit(solution)/shard_map/ppermute | solution.py:630
  87.8 1.9 %collective-permute-start.22 = (bf16[512,384]{1,0:T(8,128)(2,1)S(1)}, bf16[512,384]{1,0:T(8,128)(2,1)S(1)}, u32[]{:S(2)}, u32[]{:S(2)}) collective-permute-start(bf16[512,384]{1,0:T(8,128)(2,1)S(1)} %copy-done.21), channel_id=1, source_target_pairs={{0,4},{1,5},{2,6},{3,7},{4,8},{5,9},{6,10},{7,11},{8,12},{9,13},{1... | collective-permute-start | bytes 1179656 | tf_op jit(solution)/shard_map/ppermute | solution.py:630
  90.2 1.3 collective-permute-start.24
  91.5 9.0 %collective-permute-done.22.got_ref.stat_ref = bf16[512,384]{1,0:T(8,128)(2,1)S(1)} collective-permute-done((bf16[512,384]{1,0:T(8,128)(2,1)S(1)}, bf16[512,384]{1,0:T(8,128)(2,1)S(1)}, u32[]{:S(2)}, u32[]{:S(2)}) %collective-permute-start.22) | collective-permute-done | bytes 393248 | tf_op jit(solution)/shard_map/ppermute | solution.py:630
  100.7 1.9 %collective-permute-start.21 = (bf16[512,640]{1,0:T(8,128)(2,1)}, bf16[512,640]{1,0:T(8,128)(2,1)S(1)}, u32[]{:S(2)}, u32[]{:S(2)}) collective-permute-start(bf16[512,640]{1,0:T(8,128)(2,1)} %get-tuple-element.41), channel_id=1, source_target_pairs={{0,4},{1,5},{2,6},{3,7},{4,8},{5,9},{6,10},{7,11},{8,12},{9,13},{1... | collective-permute-start | bytes 1966088 | tf_op jit(solution)/shard_map/ppermute | solution.py:630
  102.7 3.5 %collective-permute-done.24.came_ref = bf16[128,1024]{1,0:T(8,128)(2,1)S(1)} collective-permute-done((bf16[128,1024]{1,0:T(8,128)(2,1)S(1)}, bf16[128,1024]{1,0:T(8,128)(2,1)S(1)}, u32[]{:S(2)}, u32[]{:S(2)}) %collective-permute-start.24) | collective-permute-done | bytes 262176 | tf_op jit(solution)/shard_map/ppermute | solution.py:630
  106.1 1.1 collective-permute-start.20
  107.3 1.3 collective-permute-start.25
  108.6 10.1 %lent.5 = (f32[512,512]{1,0:T(8,128)}, f32[512,128]{1,0:T(8,128)}, bf16[512,640]{1,0:T(8,128)(2,1)}) custom-call(s32[2]{0:T(128)} %pad_add_fusion.side, bf16[512,2048]{1,0:T(8,128)(2,1)} %q_ref.11, bf16[512,1024]{1,0:T(8,128)(2,1)} %collective-permute-done.9.n_ref, bf16[512,2048]{1,0:T(8,128)(2,1)} %ok.11, bf16[512,2048]{1,0:T(8,128)(2,1)} %ov.11, ...), custom_call_target="tpu_custom_call" | custom-call | flops 2048 | bytes 512 | tf_op jit(solution)/shard_map/lent/pallas_call | solution.py:182
  118.8 1.9 %collective-permute-start.16 = (bf16[512,640]{1,0:T(8,128)(2,1)}, bf16[512,640]{1,0:T(8,128)(2,1)}, u32[]{:S(2)}, u32[]{:S(2)}) collective-permute-start(bf16[512,640]{1,0:T(8,128)(2,1)} %get-tuple-element.37), channel_id=1, source_target_pairs={{0,4},{1,5},{2,6},{3,7},{4,8},{5,9},{6,10},{7,11},{8,12},{9,13},{1... | collective-permute-start | bytes 1966088 | tf_op jit(solution)/shard_map/ppermute | solution.py:630
  121.4 3.6 %collective-permute-start.18 = (bf16[512,512]{1,0:T(8,128)(2,1)}, bf16[512,512]{1,0:T(8,128)(2,1)}, u32[]{:S(2)}, u32[]{:S(2)}) collective-permute-start(bf16[512,512]{1,0:T(8,128)(2,1)} %collective-permute-done.17.yk.yv), channel_id=1, source_target_pairs={{0,1},{1,0},{2,3},{3,2},{4,5},{5,4},{6,7},{7,6},{8,9},{9,8},{10,11... | collective-permute-start | bytes 1572872 | tf_op jit(solution)/shard_map/ppermute | solution.py:630
  126.3 2.4 %join.3.rest_1_ = bf16[512,2048]{1,0:T(8,128)(2,1)} custom-call(s32[4]{0:T(128)} %compare_convert_fusion.ok_ref, f32[512,256]{1,0:T(8,128)} %get-tuple-element.42.mine_ref, f32[512,128]{1,0:T(8,128)} %get-tuple-element.27._.l_ref, bf16[512,384]{1,0:T(8,128)(2,1)} %copy-done.18, bf16[512,384]{1,0:T(8,128)(2,1)} %copy-done.18, ...), custom_call_target="tpu_custom_call" | custom-call | flops 512 | bytes 512 | tf_op jit(solution)/shard_map/join/pallas_call | solution.py:324
  128.8 3.0 %join.4.rest_0_ = bf16[512,2048]{1,0:T(8,128)(2,1)} custom-call(s32[4]{0:T(128)} %compare_convert_fusion.ok_ref, f32[512,512]{1,0:T(8,128)} %get-tuple-element.40.mine_ref, f32[512,128]{1,0:T(8,128)} %get-tuple-element.33.refs_0_.l_ref, bf16[512,640]{1,0:T(8,128)(2,1)} %copy-done.15, bf16[512,640]{1,0:T(8,128)(2,1)} %copy-done.15, ...), custom_call_target="tpu_custom_call", output_to_operand_aliasing={{}: (6, {})} | custom-call | flops 512 | bytes 512 | tf_op jit(solution)/shard_map/join/pallas_call | solution.py:324
  131.8 5.7 %relayed.3.rest_0_ = bf16[512,2048]{1,0:T(8,128)(2,1)} custom-call(s32[4]{0:T(128)} %compare_convert_fusion.ok_ref, bf16[512,2048]{1,0:T(8,128)(2,1)} %q_ref.11, bf16[512,2048]{1,0:T(8,128)(2,1)} %ok.11, bf16[512,2048]{1,0:T(8,128)(2,1)} %ov.11, bf16[512,1536]{1,0:T(8,128)(2,1)} %collective-permute-done.z_ref.zk.zv, ...), custom_call_target="tpu_custom_call", output_to_operand_aliasing={{}: (12, {})} | custom-call | flops 1024 | bytes 512 | tf_op jit(solution)/shard_map/relayed/pallas_call | solution.py:253
  137.4 5.7 %relayed.4.rest_1_ = bf16[512,2048]{1,0:T(8,128)(2,1)} custom-call(s32[4]{0:T(128)} %compare_convert_fusion.ok_ref, bf16[512,2048]{1,0:T(8,128)(2,1)} %q_ref.11, bf16[512,2048]{1,0:T(8,128)(2,1)} %ok.11, bf16[512,2048]{1,0:T(8,128)(2,1)} %ov.11, bf16[512,1536]{1,0:T(8,128)(2,1)} %collective-permute-done.z_ref.zk.zv, ...), custom_call_target="tpu_custom_call", output_to_operand_aliasing={{}: (12, {})} | custom-call | flops 1024 | bytes 512 | tf_op jit(solution)/shard_map/relayed/pallas_call | solution.py:253
  143.1 3.0 %join.5.rest_0_ = bf16[512,2048]{1,0:T(8,128)(2,1)} custom-call(s32[4]{0:T(128)} %compare_convert_fusion.ok_ref, f32[512,512]{1,0:T(8,128)} %get-tuple-element.35.mine_ref, f32[512,128]{1,0:T(8,128)} %get-tuple-element.36.rest_0_.l_ref, bf16[512,640]{1,0:T(8,128)(2,1)} %collective-permute-done.16.got_ref.stat_ref, ...), custom_call_target="tpu_custom_call", output_to_operand_aliasing={{}: (6, {})} | custom-call | flops 512 | bytes 512 | tf_op jit(solution)/shard_map/join/pallas_call | solution.py:324
  146.1 5.7 %relayed.5 = bf16[512,2048]{1,0:T(8,128)(2,1)} custom-call(s32[4]{0:T(128)} %compare_convert_fusion.ok_ref, bf16[512,2048]{1,0:T(8,128)(2,1)} %q_ref.11, bf16[512,2048]{1,0:T(8,128)(2,1)} %ok.11, bf16[512,2048]{1,0:T(8,128)(2,1)} %ov.11, bf16[512,1536]{1,0:T(8,128)(2,1)} %collective-permute-done.z_ref.zk.zv, ...), custom_call_target="tpu_custom_call", output_to_operand_aliasing={{}: (12, {})} | custom-call | flops 1024 | bytes 512 | tf_op jit(solution)/shard_map/relayed/pallas_call | solution.py:253
  151.8 2.2 %copy-done.2 = f32[512,2048]{1,0:T(8,128)S(1)} copy-done((f32[512,2048]{1,0:T(8,128)S(1)}, f32[512,2048]{1,0:T(8,128)}, u32[]{:S(2)}) %copy-start.2) | copy-done | bytes 4194328
  154.0 7.4 %final.1 = bf16[512,2048]{1,0:T(8,128)(2,1)} custom-call(s32[1]{0:T(128)} %bitcast.6.core, f32[512,2048]{1,0:T(8,128)S(1)} %copy-done.2, f32[512,32]{1,0:T(8,128)S(1)} %copy-done.4, bf16[512,128]{1,0:T(8,128)(2,1)S(1)} %copy-done.9, f32[128,1024]{1,0:T(8,128)S(1)} %arrive.1.mine_ref, f32[128,1024]{1,0:T(8,128)S(1)} %collective-permute-done.26.theirs_ref, ...), custom_call_target="tpu_custom_call" | custom-call | flops 512 | bytes 512 | tf_op jit(solution)/shard_map/final/pallas_call | solution.py:594
  (84 shorter events, 7.5 us)
Async XLA Ops:
  0.6 5.4 %copy-start.10 = (bf16[512,2048]{1,0:T(8,128)(2,1)S(1)}, bf16[512,2048]{1,0:T(8,128)(2,1)}, u32[]{:S(2)}) copy-start(bf16[512,2048]{1,0:T(8,128)(2,1)} %ov.11) | copy-start | bytes 6291460
  0.6 41.1 %collective-permute-start.3 = (bf16[512,2048]{1,0:T(8,128)(2,1)}, bf16[512,2048]{1,0:T(8,128)(2,1)}, u32[]{:S(2)}, u32[]{:S(2)}) collective-permute-start(bf16[512,2048]{1,0:T(8,128)(2,1)} %ok.11), channel_id=1, source_target_pairs={{0,1},{1,0},{2,3},{3,2},{4,5},{5,4},{6,7},{7,6},{8,9},{9,8},{10,11... | collective-permute-start | bytes 6291464 | tf_op jit(solution)/shard_map/ppermute | solution.py:630
  1.4 44.2 %collective-permute-start.4 = (bf16[512,2048]{1,0:T(8,128)(2,1)}, bf16[512,2048]{1,0:T(8,128)(2,1)}, u32[]{:S(2)}, u32[]{:S(2)}) collective-permute-start(bf16[512,2048]{1,0:T(8,128)(2,1)} %ov.11), channel_id=1, source_target_pairs={{0,1},{1,0},{2,3},{3,2},{4,5},{5,4},{6,7},{7,6},{8,9},{9,8},{10,11... | collective-permute-start | bytes 6291464 | tf_op jit(solution)/shard_map/ppermute | solution.py:630
  3.5 13.1 %collective-permute-start.5 = (bf16[512,512]{1,0:T(8,128)(2,1)S(1)}, bf16[512,512]{1,0:T(8,128)(2,1)S(1)}, u32[]{:S(2)}, u32[]{:S(2)}) collective-permute-start(bf16[512,512]{1,0:T(8,128)(2,1)S(1)} %pad_maximum_fusion.3), channel_id=1, source_target_pairs={{0,2},{1,3},{2,0},{3,1},{4,6},{5,7},{6,4},{7,5},{8,10},{9,11},{10,... | collective-permute-start | bytes 1572872 | tf_op jit(solution)/shard_map/ppermute | solution.py:630
  7.3 32.1 %collective-permute-start.13 = (bf16[512,1024]{1,0:T(8,128)(2,1)}, bf16[512,1024]{1,0:T(8,128)(2,1)S(1)}, u32[]{:S(2)}, u32[]{:S(2)}) collective-permute-start(bf16[512,1024]{1,0:T(8,128)(2,1)} %pad_maximum_fusion.2), channel_id=1, source_target_pairs={{0,2},{1,3},{2,0},{3,1},{4,6},{5,7},{6,4},{7,5},{8,10},{9,11},{10,... | collective-permute-start | bytes 3145736 | tf_op jit(solution)/shard_map/ppermute | solution.py:630
  16.5 8.0 %copy-start.16 = (bf16[512,512]{1,0:T(8,128)(2,1)}, bf16[512,512]{1,0:T(8,128)(2,1)S(1)}, u32[]{:S(2)}) copy-start(bf16[512,512]{1,0:T(8,128)(2,1)S(1)} %collective-permute-done.5.yk.yv) | copy-start | bytes 1572868
  16.5 20.6 %collective-permute-start.6 = (bf16[512,512]{1,0:T(8,128)(2,1)S(1)}, bf16[512,512]{1,0:T(8,128)(2,1)S(1)}, u32[]{:S(2)}, u32[]{:S(2)}) collective-permute-start(bf16[512,512]{1,0:T(8,128)(2,1)S(1)} %collective-permute-done.5.yk.yv), channel_id=1, source_target_pairs={{0,1},{1,0},{2,3},{3,2},{4,5},{5,4},{6,7},{7,6},{8,9},{9,8},{10,11... | collective-permute-start | bytes 1572872 | tf_op jit(solution)/shard_map/ppermute | solution.py:630
  19.8 9.6 %collective-permute-start.2 = (bf16[512,256]{1,0:T(8,128)(2,1)S(1)}, bf16[512,256]{1,0:T(8,128)(2,1)S(1)}, u32[]{:S(2)}, u32[]{:S(2)}) collective-permute-start(bf16[512,256]{1,0:T(8,128)(2,1)S(1)} %slice.32), channel_id=1, source_target_pairs={{4,0},{5,1},{6,2},{7,3},{8,4},{9,5},{10,6},{11,7},{12,8},{13,9},{1... | collective-permute-start | bytes 786440 | tf_op jit(solution)/shard_map/ppermute | solution.py:630
  23.0 1.5 copy-start.12
  23.1 6.3 %copy-start.14 = (bf16[512,768]{1,0:T(8,128)(2,1)}, bf16[512,768]{1,0:T(8,128)(2,1)S(1)}, u32[]{:S(2)}) copy-start(bf16[512,768]{1,0:T(8,128)(2,1)S(1)} %slice.31) | copy-start | bytes 2359300
  29.4 10.0 %copy-start.19 = (bf16[512,256]{1,0:T(8,128)(2,1)}, bf16[512,256]{1,0:T(8,128)(2,1)S(1)}, u32[]{:S(2)}) copy-start(bf16[512,256]{1,0:T(8,128)(2,1)S(1)} %collective-permute-done.2.n_ref) | copy-start | bytes 786436
  29.4 37.1 %collective-permute-start = (bf16[512,1536]{1,0:T(8,128)(2,1)}, bf16[512,1536]{1,0:T(8,128)(2,1)}, u32[]{:S(2)}, u32[]{:S(2)}) collective-permute-start(bf16[512,1536]{1,0:T(8,128)(2,1)} %pad_maximum_fusion.own_ref), channel_id=1, source_target_pairs={{0,4},{1,5},{2,6},{3,7},{4,8},{5,9},{6,10},{7,11},{8,12},{9,13},{1... | collective-permute-start | bytes 4718600 | tf_op jit(solution)/shard_map/ppermute | solution.py:630
  37.1 3.5 %copy-start.11 = (bf16[512,2048]{1,0:T(8,128)(2,1)S(1)}, bf16[512,2048]{1,0:T(8,128)(2,1)}, u32[]{:S(2)}) copy-start(bf16[512,2048]{1,0:T(8,128)(2,1)} %q_ref.11) | copy-start | bytes 6291460
  37.1 4.6 %copy-start.17 = (bf16[512,512]{1,0:T(8,128)(2,1)}, bf16[512,512]{1,0:T(8,128)(2,1)S(1)}, u32[]{:S(2)}) copy-start(bf16[512,512]{1,0:T(8,128)(2,1)S(1)} %collective-permute-done.6.bk.bv) | copy-start | bytes 1572868
  37.1 25.5 %collective-permute-start.12 = (f32[136,2048]{1,0:T(8,128)}, f32[136,2048]{1,0:T(8,128)S(1)}, u32[]{:S(2)}, u32[]{:S(2)}) collective-permute-start(f32[136,2048]{1,0:T(8,128)} %get-tuple-element.30.both_ref), channel_id=1, source_target_pairs={{0,1},{1,0},{2,3},{3,2},{4,5},{5,4},{6,7},{7,6},{8,9},{9,8},{10,11... | collective-permute-start | bytes 3342344 | tf_op jit(solution)/shard_map/ppermute | solution.py:630
  39.4 23.3 %copy-start = (bf16[512,1024]{1,0:T(8,128)(2,1)}, bf16[512,1024]{1,0:T(8,128)(2,1)S(1)}, u32[]{:S(2)}) copy-start(bf16[512,1024]{1,0:T(8,128)(2,1)S(1)} %collective-permute-done.13.refs_1_.yk.yv) | copy-start | bytes 3145732
  39.4 26.5 %collective-permute-start.10 = (bf16[512,1024]{1,0:T(8,128)(2,1)}, bf16[512,1024]{1,0:T(8,128)(2,1)}, u32[]{:S(2)}, u32[]{:S(2)}) collective-permute-start(bf16[512,1024]{1,0:T(8,128)(2,1)} %pad_maximum_fusion.1), channel_id=1, source_target_pairs={{0,2},{1,3},{2,0},{3,1},{4,6},{5,7},{6,4},{7,5},{8,10},{9,11},{10,... | collective-permute-start | bytes 3145736 | tf_op jit(solution)/shard_map/ppermute | solution.py:630
  41.8 28.8 %collective-permute-start.9 = (bf16[512,1024]{1,0:T(8,128)(2,1)}, bf16[512,1024]{1,0:T(8,128)(2,1)}, u32[]{:S(2)}, u32[]{:S(2)}) collective-permute-start(bf16[512,1024]{1,0:T(8,128)(2,1)} %slice.35), channel_id=1, source_target_pairs={{4,0},{5,1},{6,2},{7,3},{8,4},{9,5},{10,6},{11,7},{12,8},{13,9},{1... | collective-permute-start | bytes 3145736 | tf_op jit(solution)/shard_map/ppermute | solution.py:630
  45.6 25.0 %collective-permute-start.15 = (bf16[512,1024]{1,0:T(8,128)(2,1)S(1)}, bf16[512,1024]{1,0:T(8,128)(2,1)}, u32[]{:S(2)}, u32[]{:S(2)}) collective-permute-start(bf16[512,1024]{1,0:T(8,128)(2,1)S(1)} %collective-permute-done.13.refs_1_.yk.yv), channel_id=1, source_target_pairs={{0,1},{1,0},{2,3},{3,2},{4,5},{5,4},{6,7},{7,6},{8,9},{9,8},{10,11... | collective-permute-start | bytes 3145736 | tf_op jit(solution)/shard_map/ppermute | solution.py:630
  53.1 9.6 %copy-start.7 = (f32[136,2048]{1,0:T(8,128)S(1)}, f32[136,2048]{1,0:T(8,128)}, u32[]{:S(2)}) copy-start(f32[136,2048]{1,0:T(8,128)} %get-tuple-element.30.both_ref) | copy-start | bytes 3342340
  62.7 1.0 copy-start.3
  65.3 15.5 %collective-permute-start.14 = (bf16[144,1024]{1,0:T(8,128)(2,1)}, bf16[144,1024]{1,0:T(8,128)(2,1)S(1)}, u32[]{:S(2)}, u32[]{:S(2)}) collective-permute-start(bf16[144,1024]{1,0:T(8,128)(2,1)} %get-tuple-element.32), channel_id=1, source_target_pairs={{0,2},{1,3},{2,0},{3,1},{4,6},{5,7},{6,4},{7,5},{8,10},{9,11},{10,... | collective-permute-start | bytes 884744 | tf_op jit(solution)/shard_map/ppermute | solution.py:630
  65.8 24.3 %collective-permute-start.11 = (bf16[512,1024]{1,0:T(8,128)(2,1)}, bf16[512,1024]{1,0:T(8,128)(2,1)}, u32[]{:S(2)}, u32[]{:S(2)}) collective-permute-start(bf16[512,1024]{1,0:T(8,128)(2,1)} %collective-permute-done.10.yk.yv), channel_id=1, source_target_pairs={{0,1},{1,0},{2,3},{3,2},{4,5},{5,4},{6,7},{7,6},{8,9},{9,8},{10,11... | collective-permute-start | bytes 3145736 | tf_op jit(solution)/shard_map/ppermute | solution.py:630
  69.3 31.4 %collective-permute-start.19 = (bf16[512,512]{1,0:T(8,128)(2,1)}, bf16[512,512]{1,0:T(8,128)(2,1)}, u32[]{:S(2)}, u32[]{:S(2)}) collective-permute-start(bf16[512,512]{1,0:T(8,128)(2,1)} %get-tuple-element.39), channel_id=1, source_target_pairs={{0,2},{1,3},{2,0},{3,1},{4,6},{5,7},{6,4},{7,5},{8,10},{9,11},{10,... | collective-permute-start | bytes 1572872 | tf_op jit(solution)/shard_map/ppermute | solution.py:630
  70.5 10.2 %copy-start.6 = (f32[136,1024]{1,0:T(8,128)S(1)}, f32[136,1024]{1,0:T(8,128)}, u32[]{:S(2)}) copy-start(f32[136,1024]{1,0:T(8,128)} %copy-done.5) | copy-start | bytes 1671172
  70.6 12.4 %copy-start.13 = (bf16[512,768]{1,0:T(8,128)(2,1)S(1)}, bf16[512,768]{1,0:T(8,128)(2,1)}, u32[]{:S(2)}) copy-start(bf16[512,768]{1,0:T(8,128)(2,1)} %copy-done.12) | copy-start | bytes 2359300
  80.8 1.0 copy-start.8
  81.8 25.4 %copy-start.1 = (f32[136,1024]{1,0:T(8,128)}, f32[136,1024]{1,0:T(8,128)S(1)}, u32[]{:S(2)}) copy-start(f32[136,1024]{1,0:T(8,128)S(1)} %get-tuple-element.34._.plane_ref) | copy-start | bytes 1671172
  81.9 5.9 %copy-start.21 = (bf16[512,384]{1,0:T(8,128)(2,1)S(1)}, bf16[512,384]{1,0:T(8,128)(2,1)}, u32[]{:S(2)}) copy-start(bf16[512,384]{1,0:T(8,128)(2,1)} %get-tuple-element.43) | copy-start | bytes 1179652
  81.9 7.8 %copy-start.20 = (bf16[512,512]{1,0:T(8,128)(2,1)S(1)}, bf16[512,512]{1,0:T(8,128)(2,1)}, u32[]{:S(2)}) copy-start(bf16[512,512]{1,0:T(8,128)(2,1)} %get-tuple-element.38) | copy-start | bytes 1572868
  81.9 7.8 %collective-permute-start.23 = (bf16[128,1024]{1,0:T(8,128)(2,1)S(1)}, bf16[128,1024]{1,0:T(8,128)(2,1)S(1)}, u32[]{:S(2)}, u32[]{:S(2)}) collective-permute-start(bf16[128,1024]{1,0:T(8,128)(2,1)S(1)} %get-tuple-element.45), channel_id=1, source_target_pairs={{0,4},{1,5},{2,6},{3,7},{16,20},{17,21},{18,22},{19,23}} | collective-permute-start | bytes 786440 | tf_op jit(solution)/shard_map/ppermute | solution.py:630
  86.1 45.7 %collective-permute-start.1 = (bf16[512,1536]{1,0:T(8,128)(2,1)}, bf16[512,1536]{1,0:T(8,128)(2,1)}, u32[]{:S(2)}, u32[]{:S(2)}) collective-permute-start(bf16[512,1536]{1,0:T(8,128)(2,1)} %broadcast_select_fusion), channel_id=1, source_target_pairs={{0,1},{1,0},{2,3},{3,2},{4,5},{5,4},{6,7},{7,6},{8,9},{9,8},{10,11... | collective-permute-start | bytes 4718600 | tf_op jit(solution)/shard_map/ppermute | solution.py:630
  87.8 12.7 %collective-permute-start.22 = (bf16[512,384]{1,0:T(8,128)(2,1)S(1)}, bf16[512,384]{1,0:T(8,128)(2,1)S(1)}, u32[]{:S(2)}, u32[]{:S(2)}) collective-permute-start(bf16[512,384]{1,0:T(8,128)(2,1)S(1)} %copy-done.21), channel_id=1, source_target_pairs={{0,4},{1,5},{2,6},{3,7},{4,8},{5,9},{6,10},{7,11},{8,12},{9,13},{1... | collective-permute-start | bytes 1179656 | tf_op jit(solution)/shard_map/ppermute | solution.py:630
  89.7 17.6 %collective-permute-start.17 = (bf16[512,512]{1,0:T(8,128)(2,1)S(1)}, bf16[512,512]{1,0:T(8,128)(2,1)}, u32[]{:S(2)}, u32[]{:S(2)}) collective-permute-start(bf16[512,512]{1,0:T(8,128)(2,1)S(1)} %copy-done.20), channel_id=1, source_target_pairs={{0,2},{1,3},{2,0},{3,1},{4,6},{5,7},{6,4},{7,5},{8,10},{9,11},{10,... | collective-permute-start | bytes 1572872 | tf_op jit(solution)/shard_map/ppermute | solution.py:630
  90.2 15.9 %collective-permute-start.24 = (bf16[128,1024]{1,0:T(8,128)(2,1)S(1)}, bf16[128,1024]{1,0:T(8,128)(2,1)S(1)}, u32[]{:S(2)}, u32[]{:S(2)}) collective-permute-start(bf16[128,1024]{1,0:T(8,128)(2,1)S(1)} %get-tuple-element.47), channel_id=1, source_target_pairs={{4,8},{5,9},{6,10},{7,11},{20,24},{21,25},{22,26},{23,27}} | collective-permute-start | bytes 786440 | tf_op jit(solution)/shard_map/ppermute | solution.py:630
  100.5 18.3 %copy-start.18 = (bf16[512,384]{1,0:T(8,128)(2,1)}, bf16[512,384]{1,0:T(8,128)(2,1)S(1)}, u32[]{:S(2)}) copy-start(bf16[512,384]{1,0:T(8,128)(2,1)S(1)} %collective-permute-done.22.got_ref.stat_ref) | copy-start | bytes 1179652
  100.5 18.3 %collective-permute-start.7 = (bf16[512,512]{1,0:T(8,128)(2,1)}, bf16[512,512]{1,0:T(8,128)(2,1)}, u32[]{:S(2)}, u32[]{:S(2)}) collective-permute-start(bf16[512,512]{1,0:T(8,128)(2,1)} %get-tuple-element.29), channel_id=1, source_target_pairs={{0,2},{1,3},{2,0},{3,1},{4,6},{5,7},{6,4},{7,5},{8,10},{9,11},{10,... | collective-permute-start | bytes 1572872 | tf_op jit(solution)/shard_map/ppermute | solution.py:630
  100.7 24.4 %collective-permute-start.21 = (bf16[512,640]{1,0:T(8,128)(2,1)}, bf16[512,640]{1,0:T(8,128)(2,1)S(1)}, u32[]{:S(2)}, u32[]{:S(2)}) collective-permute-start(bf16[512,640]{1,0:T(8,128)(2,1)} %get-tuple-element.41), channel_id=1, source_target_pairs={{0,4},{1,5},{2,6},{3,7},{4,8},{5,9},{6,10},{7,11},{8,12},{9,13},{1... | collective-permute-start | bytes 1966088 | tf_op jit(solution)/shard_map/ppermute | solution.py:630
  106.1 19.1 %collective-permute-start.20 = (bf16[512,512]{1,0:T(8,128)(2,1)}, bf16[512,512]{1,0:T(8,128)(2,1)}, u32[]{:S(2)}, u32[]{:S(2)}) collective-permute-start(bf16[512,512]{1,0:T(8,128)(2,1)} %collective-permute-done.19.yk.yv), channel_id=1, source_target_pairs={{0,1},{1,0},{2,3},{3,2},{4,5},{5,4},{6,7},{7,6},{8,9},{9,8},{10,11... | collective-permute-start | bytes 1572872 | tf_op jit(solution)/shard_map/ppermute | solution.py:630
  107.3 14.1 %collective-permute-start.25 = (bf16[128,1024]{1,0:T(8,128)(2,1)S(1)}, bf16[128,1024]{1,0:T(8,128)(2,1)S(1)}, u32[]{:S(2)}, u32[]{:S(2)}) collective-permute-start(bf16[128,1024]{1,0:T(8,128)(2,1)S(1)} %get-tuple-element.49), channel_id=1, source_target_pairs={{8,12},{9,13},{10,14},{11,15},{24,28},{25,29},{26,30},{27,31}} | collective-permute-start | bytes 786440 | tf_op jit(solution)/shard_map/ppermute | solution.py:630
  118.8 24.3 %collective-permute-start.16 = (bf16[512,640]{1,0:T(8,128)(2,1)}, bf16[512,640]{1,0:T(8,128)(2,1)}, u32[]{:S(2)}, u32[]{:S(2)}) collective-permute-start(bf16[512,640]{1,0:T(8,128)(2,1)} %get-tuple-element.37), channel_id=1, source_target_pairs={{0,4},{1,5},{2,6},{3,7},{4,8},{5,9},{6,10},{7,11},{8,12},{9,13},{1... | collective-permute-start | bytes 1966088 | tf_op jit(solution)/shard_map/ppermute | solution.py:630
  121.4 16.0 %collective-permute-start.18 = (bf16[512,512]{1,0:T(8,128)(2,1)}, bf16[512,512]{1,0:T(8,128)(2,1)}, u32[]{:S(2)}, u32[]{:S(2)}) collective-permute-start(bf16[512,512]{1,0:T(8,128)(2,1)} %collective-permute-done.17.yk.yv), channel_id=1, source_target_pairs={{0,1},{1,0},{2,3},{3,2},{4,5},{5,4},{6,7},{7,6},{8,9},{9,8},{10,11... | collective-permute-start | bytes 1572872 | tf_op jit(solution)/shard_map/ppermute | solution.py:630
  125.1 3.6 %copy-start.15 = (bf16[512,640]{1,0:T(8,128)(2,1)}, bf16[512,640]{1,0:T(8,128)(2,1)S(1)}, u32[]{:S(2)}) copy-start(bf16[512,640]{1,0:T(8,128)(2,1)S(1)} %collective-permute-done.21.got_ref.stat_ref) | copy-start | bytes 1966084
  125.1 21.0 %collective-permute-start.8 = (bf16[512,512]{1,0:T(8,128)(2,1)}, bf16[512,512]{1,0:T(8,128)(2,1)}, u32[]{:S(2)}, u32[]{:S(2)}) collective-permute-start(bf16[512,512]{1,0:T(8,128)(2,1)} %collective-permute-done.7.yk.yv), channel_id=1, source_target_pairs={{0,1},{1,0},{2,3},{3,2},{4,5},{5,4},{6,7},{7,6},{8,9},{9,8},{10,11... | collective-permute-start | bytes 1572872 | tf_op jit(solution)/shard_map/ppermute | solution.py:630
  125.2 26.6 %collective-permute-start.26 = (f32[128,1024]{1,0:T(8,128)S(1)}, f32[128,1024]{1,0:T(8,128)S(1)}, u32[]{:S(2)}, u32[]{:S(2)}) collective-permute-start(f32[128,1024]{1,0:T(8,128)S(1)} %arrive.1.mine_ref), channel_id=1, source_target_pairs={{0,1},{1,0},{2,3},{3,2},{4,5},{5,4},{6,7},{7,6},{8,9},{9,8},{10,11... | collective-permute-start | bytes 1572872 | tf_op jit(solution)/shard_map/ppermute | solution.py:630
  146.1 5.7 %copy-start.4 = (f32[512,32]{1,0:T(8,128)S(1)}, f32[512,32]{1,0:T(8,128)}, u32[]{:S(2)}) copy-start(f32[512,32]{1,0:T(8,128)} %get-tuple-element.28._.refs_0_.factor_ref) | copy-start | bytes 196612
  146.1 5.7 %copy-start.9 = (bf16[512,128]{1,0:T(8,128)(2,1)S(1)}, bf16[512,128]{1,0:T(8,128)(2,1)}, u32[]{:S(2)}) copy-start(bf16[512,128]{1,0:T(8,128)(2,1)} %c_ref.3) | copy-start | bytes 393220
  151.8 2.2 %copy-start.2 = (f32[512,2048]{1,0:T(8,128)S(1)}, f32[512,2048]{1,0:T(8,128)}, u32[]{:S(2)}) copy-start(f32[512,2048]{1,0:T(8,128)} %get-tuple-element.44.pre_ref) | copy-start | bytes 12582916
  (1 other events, 0.8 us)

commit v4 on v3

--- a/solution.py
+++ b/solution.py
@@ -418,15 +418,15 @@
         x = x_ref[:, columns]
         upper, lower = [], []
         for h in (2 * pair, 2 * pair + 1):
-            r = rates_ref[h]
+            r = rates_ref[h] * math.log2(math.e)
             here, there = down[:, h : h + 1], across[h : h + 1, :]
             gap = jnp.where(seen, (there[:, :half] - here[:half]) * r, NEG)
-            inner = (cross[:half, :half] * jnp.exp(gap)).astype(jnp.bfloat16)
+            inner = (cross[:half, :half] * jnp.exp2(gap)).astype(jnp.bfloat16)
             upper.append(contract(inner, x[:half]))
             gap = (there[:, :half] - here[half:]) * r
-            inner_left = (cross[half:, :half] * jnp.exp(gap)).astype(jnp.bfloat16)
+            inner_left = (cross[half:, :half] * jnp.exp2(gap)).astype(jnp.bfloat16)
             gap = jnp.where(seen, (there[:, half:] - here[half:]) * r, NEG)
-            inner_right = (cross[half:, half:] * jnp.exp(gap)).astype(jnp.bfloat16)
+            inner_right = (cross[half:, half:] * jnp.exp2(gap)).astype(jnp.bfloat16)
             lower.append(contract(jnp.concatenate([inner_left, inner_right], axis=1), x))
         pre_ref[:half, columns] += jnp.where(left, upper[0], upper[1])
         pre_ref[half:, columns] += jnp.where(left, lower[0], lower[1])
@@ -484,7 +484,7 @@
     out_ref[...] = jnp.where(column[0] == 0, entering, entering * got_decay + got[:state])
 
 
-def final_kernel(core, pre_ref, factor_ref, c_ref, mine_ref, theirs_ref, other_ref, o_ref):
+def final_kernel(core, pre_ref, factor_ref, c_ref, mine_ref, theirs_ref, other_ref, o_ref, high_ref, low_ref):
     size, width = pre_ref.shape
     heads = factor_ref.shape[1]
     state = mine_ref.shape[0]
@@ -492,6 +492,17 @@
     wide = 2 * dim
     half = width // 2
     leads = core[0] == 0
+
+    @pl.when(pl.program_id(0) == 0)
+    def _():
+        mine, theirs = mine_ref[...], theirs_ref[...]
+        for side, entering in enumerate((jnp.where(leads, mine, theirs), jnp.where(leads, theirs, mine))):
+            columns = slice(side * half, (side + 1) * half)
+            after_first = entering * other_ref[state : state + 1, columns] + other_ref[:state, columns]
+            high, low = split_bf16(jnp.where(leads, entering, after_first), 2)
+            high_ref[:, columns] = high
+            low_ref[:, columns] = low
+
     c = c_ref[...]
     row = lax.broadcasted_iota(jnp.int32, (wide, wide), 0) // dim
     col = lax.broadcasted_iota(jnp.int32, (wide, wide), 1) // dim
@@ -499,13 +510,7 @@
     left = lax.broadcasted_iota(jnp.int32, (size, wide), 1) < dim
     for pair in range(heads // 2):
         columns = slice(pair * wide, (pair + 1) * wide)
-        inner = slice(pair * wide % half, pair * wide % half + wide)
-        mine, theirs = mine_ref[:, inner], theirs_ref[:, inner]
-        first_half = pair * wide < half
-        entering = jnp.where(leads, mine, theirs) if first_half else jnp.where(leads, theirs, mine)
-        after_first = entering * other_ref[state : state + 1, columns] + other_ref[:state, columns]
-        entering = jnp.where(leads, entering, after_first)
-        carried = sum(contract(c, part) for part in split_bf16(entering, 2))
+        carried = contract(c, high_ref[:, columns]) + contract(c, low_ref[:, columns])
         factor = jnp.where(
             left, factor_ref[:, 2 * pair : 2 * pair + 1], factor_ref[:, 2 * pair + 1 : 2 * pair + 2]
         )
@@ -605,6 +610,7 @@
         ],
         out_specs=by_block(width),
         out_shape=jax.ShapeDtypeStruct((length, width), jnp.bfloat16),
+        scratch_shapes=[pltpu.VMEM((state, width), jnp.bfloat16)] * 2,
         compiler_params=params(24),
         cost_estimate=pl.CostEstimate(
             flops=int(length * 1), bytes_accessed=length, transcendentals=0

time: 163 us -> 163 us (level)
  no operation moved by 1% of the time
where the time goes in v4:
time: 163 us; the launch traced here: 161 us
  Pallas kernels  78.8 us (48%)
  starting transfers between devices  34.3 us (21%)
  waiting for transfers between devices  27.6 us (17%)
  local copies, waits for them, and re-layouts  11.6 us (7%)
  other arithmetic  8.09 us (5%)
    ppermute x27, starting transfers between devices, on_device(): send = lambda array, route: lax.ppermute(array, 'seq', route)  34.3 us
    ppermute x27, waiting for transfers between devices, on_device(): send = lambda array, route: lax.ppermute(array, 'seq', route)  27.6 us
    pallas_call x3, Pallas kernels, lent_heads(): pl.pallas_call(functools.partial(lent_kernel, heads), grid=(pairs,), in_s...  26.5 us
    pallas_call x3, Pallas kernels, relayed_heads(): pl.pallas_call(relayed_kernel, grid=(1,), in_specs=[SCALARS] + [own] * 3...  17 us
    pallas_call x1, Pallas kernels, recurrence_intra(): pl.pallas_call(intra_kernel, grid=(blocks,), in_specs=[pl.BlockSpec((head...  9.15 us
    pallas_call x3, Pallas kernels, join(): pl.pallas_call(join_kernel, grid=(heads // PAIR,), in_specs=specs, out_sp...  8.41 us
    pallas_call x1, Pallas kernels, recurrence_final(): pl.pallas_call(final_kernel, grid=(length // Q,), in_specs=[SCALARS, by_b...  7.69 us
    slice x8, local copies, waits for them, and re-layouts, on_device(): columns = lambda array, s, n: array[:, s * E:(s + n) * E]  6.61 us
  transfers between devices with their start and end apart: 27, of which 6 were waited for; matrix products, arithmetic and copies ran while one was open for 9% of the time, Pallas kernels for 44%

profile of v4, /device:TPU:17, one launch (start us, length us, event | category | flops | bytes accessed | tf_op | source)
XLA Modules:
  0.0 161.5 jit_solution(3931761719212752864)
XLA Ops:
  1.5 1.0 slice.33
  2.4 1.0 slice.34
  3.5 1.3 collective-permute-start.5
  4.8 1.3 fusion
  6.1 1.1 pad_maximum_fusion.2
  7.5 9.0 %collective-permute-done.5.yk.yv = bf16[512,512]{1,0:T(8,128)(2,1)S(1)} collective-permute-done((bf16[512,512]{1,0:T(8,128)(2,1)S(1)}, bf16[512,512]{1,0:T(8,128)(2,1)S(1)}, u32[]{:S(2)}, u32[]{:S(2)}) %collective-permute-start.5) | collective-permute-done | bytes 524320 | tf_op jit(solution)/shard_map/ppermute | solution.py:636
  16.5 2.2 %collective-permute-start.6 = (bf16[512,512]{1,0:T(8,128)(2,1)S(1)}, bf16[512,512]{1,0:T(8,128)(2,1)S(1)}, u32[]{:S(2)}, u32[]{:S(2)}) collective-permute-start(bf16[512,512]{1,0:T(8,128)(2,1)S(1)} %collective-permute-done.5.yk.yv), channel_id=1, source_target_pairs={{0,1},{1,0},{2,3},{3,2},{4,5},{5,4},{6,7},{7,6},{8,9},{9,8},{10,11... | collective-permute-start | bytes 1572872 | tf_op jit(solution)/shard_map/ppermute | solution.py:636
  18.8 1.0 slice.32
  19.8 2.1 %collective-permute-start.2 = (bf16[512,256]{1,0:T(8,128)(2,1)S(1)}, bf16[512,256]{1,0:T(8,128)(2,1)S(1)}, u32[]{:S(2)}, u32[]{:S(2)}) collective-permute-start(bf16[512,256]{1,0:T(8,128)(2,1)S(1)} %slice.32), channel_id=1, source_target_pairs={{4,0},{5,1},{6,2},{7,3},{8,4},{9,5},{10,6},{11,7},{12,8},{13,9},{1... | collective-permute-start | bytes 786440 | tf_op jit(solution)/shard_map/ppermute | solution.py:636
  21.8 1.2 slice.30
  23.1 1.4 pad_maximum_fusion.own_ref
  24.5 4.8 %collective-permute-done.2.n_ref = bf16[512,256]{1,0:T(8,128)(2,1)S(1)} collective-permute-done((bf16[512,256]{1,0:T(8,128)(2,1)S(1)}, bf16[512,256]{1,0:T(8,128)(2,1)S(1)}, u32[]{:S(2)}, u32[]{:S(2)}) %collective-permute-start.2) | collective-permute-done | bytes 262176 | tf_op jit(solution)/shard_map/ppermute | solution.py:636
  29.4 1.9 %collective-permute-start = (bf16[512,1536]{1,0:T(8,128)(2,1)}, bf16[512,1536]{1,0:T(8,128)(2,1)}, u32[]{:S(2)}, u32[]{:S(2)}) collective-permute-start(bf16[512,1536]{1,0:T(8,128)(2,1)} %pad_maximum_fusion.own_ref), channel_id=1, source_target_pairs={{0,4},{1,5},{2,6},{3,7},{4,8},{5,9},{6,10},{7,11},{8,12},{9,13},{1... | collective-permute-start | bytes 4718600 | tf_op jit(solution)/shard_map/ppermute | solution.py:636
  31.3 5.8 %states.1 = (f32[128,2048]{1,0:T(8,128)}, f32[136,2048]{1,0:T(8,128)}) custom-call(s32[32,512]{1,0:T(8,128)} %bitcast.7, f32[1,32]{1,0:T(1,128)} %bitcast.9, bf16[512,2048]{1,0:T(8,128)(2,1)} %x_ref.3, bf16[512,128]{1,0:T(8,128)(2,1)} %rest_0_.1), custom_call_target="tpu_custom_call" | custom-call | flops 512 | bytes 512 | tf_op jit(solution)/shard_map/states/pallas_call | solution.py:547
  37.1 1.1 collective-permute-start.12
  38.2 1.1 pad_maximum_fusion.1
  39.4 1.3 collective-permute-start.10
  40.7 1.1 slice.35
  41.8 3.8 %collective-permute-start.9 = (bf16[512,1024]{1,0:T(8,128)(2,1)}, bf16[512,1024]{1,0:T(8,128)(2,1)}, u32[]{:S(2)}, u32[]{:S(2)}) collective-permute-start(bf16[512,1024]{1,0:T(8,128)(2,1)} %slice.35), channel_id=1, source_target_pairs={{4,0},{5,1},{6,2},{7,3},{8,4},{9,5},{10,6},{11,7},{12,8},{13,9},{1... | collective-permute-start | bytes 3145736 | tf_op jit(solution)/shard_map/ppermute | solution.py:636
  46.8 6.2 %lent.3 = (f32[512,256]{1,0:T(8,128)}, f32[512,128]{1,0:T(8,128)}, bf16[512,384]{1,0:T(8,128)(2,1)}) custom-call(s32[2]{0:T(128)} %pad_add_fusion.side, bf16[512,2048]{1,0:T(8,128)(2,1)} %q_ref.11, bf16[512,256]{1,0:T(8,128)(2,1)} %copy-done.19, bf16[512,2048]{1,0:T(8,128)(2,1)} %ok.11, bf16[512,2048]{1,0:T(8,128)(2,1)} %ov.11, ...), custom_call_target="tpu_custom_call" | custom-call | flops 1024 | bytes 512 | tf_op jit(solution)/shard_map/lent/pallas_call | solution.py:182
  53.1 9.1 %intra.1 = (f32[512,2048]{1,0:T(8,128)}, f32[512,32]{1,0:T(8,128)}) custom-call(s32[32,512]{1,0:T(8,128)} %bitcast.8, f32[1,32]{1,0:T(1,128)} %bitcast.10, f32[32]{0:T(128)} %rates_ref.1, f32[1,32]{1,0:T(1,128)} %bitcast.11, bf16[512,2048]{1,0:T(8,128)(2,1)} %x_ref.3, bf16[512,128]{1,0:T(8,128)(2,1)} %rest_0_.1, bf16[512,128]{1,0:T(8,128)(2,1)} %c_ref.3, ...), custom_call_target="tpu_custom_call" | custom-call | flops 512 | bytes 512 | tf_op jit(solution)/shard_map/intra/pallas_call | solution.py:568
  62.2 0.9 copy-done.3
  63.2 0.8 chip.1
  66.5 2.8 %turn.1 = (bf16[512,512]{1,0:T(8,128)(2,1)}, bf16[512,512]{1,0:T(8,128)(2,1)}, bf16[512,512]{1,0:T(8,128)(2,1)}) custom-call(s32[1]{0:T(128)} %bitcast.2.column, bf16[512,1536]{1,0:T(8,128)(2,1)} %pad_maximum_fusion.own_ref, bf16[512,1536]{1,0:T(8,128)(2,1)} %collective-permute-done.z_ref.zk.zv, f32[512,32]{1,0:T(8,128)} %get-tuple-element.28._.refs_0_.factor_ref), custom_call_target="tpu_custom_call" | custom-call | flops 100 | bytes 100 | tf_op jit(solution)/shard_map/turn/pallas_call | solution.py:279
  69.3 1.2 collective-permute-start.19
  70.6 10.2 %lent.4 = (f32[512,512]{1,0:T(8,128)}, f32[512,128]{1,0:T(8,128)}, bf16[512,640]{1,0:T(8,128)(2,1)}) custom-call(s32[2]{0:T(128)} %pad_add_fusion.side, bf16[512,2048]{1,0:T(8,128)(2,1)} %q_ref.11, bf16[512,1024]{1,0:T(8,128)(2,1)} %collective-permute-done.9.n_ref, bf16[512,2048]{1,0:T(8,128)(2,1)} %ok.11, bf16[512,2048]{1,0:T(8,128)(2,1)} %ov.11, ...), custom_call_target="tpu_custom_call" | custom-call | flops 2048 | bytes 512 | tf_op jit(solution)/shard_map/lent/pallas_call | solution.py:182
  80.8 0.9 copy-done.8
  81.9 0.8 collective-permute-start.23
  82.7 3.1 %broadcast_select_fusion = bf16[512,1536]{1,0:T(8,128)(2,1)} fusion(bf16[512,1536]{1,0:T(8,128)(2,1)} %collective-permute-done.z_ref.zk.zv, pred[]{:T(512)S(6)} %eq.7, bf16[512,768]{1,0:T(8,128)(2,1)} %copy-done.14, bf16[512,768]{1,0:T(8,128)(2,1)S(1)} %copy-done.13), kind=kLoop, calls=%fused_computation.1 | loop fusion | flops 3932160 | bytes 4718593 | tf_op jit(solution)/shard_map/jit(_where)/select_n | solution.py:677
  85.8 1.7 %collective-permute-start.1 = (bf16[512,1536]{1,0:T(8,128)(2,1)}, bf16[512,1536]{1,0:T(8,128)(2,1)}, u32[]{:S(2)}, u32[]{:S(2)}) collective-permute-start(bf16[512,1536]{1,0:T(8,128)(2,1)} %broadcast_select_fusion), channel_id=1, source_target_pairs={{0,1},{1,0},{2,3},{3,2},{4,5},{5,4},{6,7},{7,6},{8,9},{9,8},{10,11... | collective-permute-start | bytes 4718600 | tf_op jit(solution)/shard_map/ppermute | solution.py:636
  87.6 2.1 %collective-permute-start.22 = (bf16[512,384]{1,0:T(8,128)(2,1)S(1)}, bf16[512,384]{1,0:T(8,128)(2,1)S(1)}, u32[]{:S(2)}, u32[]{:S(2)}) collective-permute-start(bf16[512,384]{1,0:T(8,128)(2,1)S(1)} %copy-done.21), channel_id=1, source_target_pairs={{0,4},{1,5},{2,6},{3,7},{4,8},{5,9},{6,10},{7,11},{8,12},{9,13},{1... | collective-permute-start | bytes 1179656 | tf_op jit(solution)/shard_map/ppermute | solution.py:636
  90.2 1.3 collective-permute-start.24
  91.5 8.8 %collective-permute-done.22.got_ref.stat_ref = bf16[512,384]{1,0:T(8,128)(2,1)S(1)} collective-permute-done((bf16[512,384]{1,0:T(8,128)(2,1)S(1)}, bf16[512,384]{1,0:T(8,128)(2,1)S(1)}, u32[]{:S(2)}, u32[]{:S(2)}) %collective-permute-start.22) | collective-permute-done | bytes 393248 | tf_op jit(solution)/shard_map/ppermute | solution.py:636
  100.5 1.9 %collective-permute-start.21 = (bf16[512,640]{1,0:T(8,128)(2,1)}, bf16[512,640]{1,0:T(8,128)(2,1)S(1)}, u32[]{:S(2)}, u32[]{:S(2)}) collective-permute-start(bf16[512,640]{1,0:T(8,128)(2,1)} %get-tuple-element.41), channel_id=1, source_target_pairs={{0,4},{1,5},{2,6},{3,7},{4,8},{5,9},{6,10},{7,11},{8,12},{9,13},{1... | collective-permute-start | bytes 1966088 | tf_op jit(solution)/shard_map/ppermute | solution.py:636
  102.4 3.5 %collective-permute-done.24.came_ref = bf16[128,1024]{1,0:T(8,128)(2,1)S(1)} collective-permute-done((bf16[128,1024]{1,0:T(8,128)(2,1)S(1)}, bf16[128,1024]{1,0:T(8,128)(2,1)S(1)}, u32[]{:S(2)}, u32[]{:S(2)}) %collective-permute-start.24) | collective-permute-done | bytes 262176 | tf_op jit(solution)/shard_map/ppermute | solution.py:636
  105.9 1.1 collective-permute-start.20
  107.1 1.3 collective-permute-start.25
  108.4 10.1 %lent.5 = (f32[512,512]{1,0:T(8,128)}, f32[512,128]{1,0:T(8,128)}, bf16[512,640]{1,0:T(8,128)(2,1)}) custom-call(s32[2]{0:T(128)} %pad_add_fusion.side, bf16[512,2048]{1,0:T(8,128)(2,1)} %q_ref.11, bf16[512,1024]{1,0:T(8,128)(2,1)} %collective-permute-done.9.n_ref, bf16[512,2048]{1,0:T(8,128)(2,1)} %ok.11, bf16[512,2048]{1,0:T(8,128)(2,1)} %ov.11, ...), custom_call_target="tpu_custom_call" | custom-call | flops 2048 | bytes 512 | tf_op jit(solution)/shard_map/lent/pallas_call | solution.py:182
  118.6 1.9 %collective-permute-start.16 = (bf16[512,640]{1,0:T(8,128)(2,1)}, bf16[512,640]{1,0:T(8,128)(2,1)}, u32[]{:S(2)}, u32[]{:S(2)}) collective-permute-start(bf16[512,640]{1,0:T(8,128)(2,1)} %get-tuple-element.37), channel_id=1, source_target_pairs={{0,4},{1,5},{2,6},{3,7},{4,8},{5,9},{6,10},{7,11},{8,12},{9,13},{1... | collective-permute-start | bytes 1966088 | tf_op jit(solution)/shard_map/ppermute | solution.py:636
  121.2 3.6 %collective-permute-start.18 = (bf16[512,512]{1,0:T(8,128)(2,1)}, bf16[512,512]{1,0:T(8,128)(2,1)}, u32[]{:S(2)}, u32[]{:S(2)}) collective-permute-start(bf16[512,512]{1,0:T(8,128)(2,1)} %collective-permute-done.17.yk.yv), channel_id=1, source_target_pairs={{0,1},{1,0},{2,3},{3,2},{4,5},{5,4},{6,7},{7,6},{8,9},{9,8},{10,11... | collective-permute-start | bytes 1572872 | tf_op jit(solution)/shard_map/ppermute | solution.py:636
  126.1 2.4 %join.3.rest_1_ = bf16[512,2048]{1,0:T(8,128)(2,1)} custom-call(s32[4]{0:T(128)} %compare_convert_fusion.ok_ref, f32[512,256]{1,0:T(8,128)} %get-tuple-element.42.mine_ref, f32[512,128]{1,0:T(8,128)} %get-tuple-element.27._.l_ref, bf16[512,384]{1,0:T(8,128)(2,1)} %copy-done.18, bf16[512,384]{1,0:T(8,128)(2,1)} %copy-done.18, ...), custom_call_target="tpu_custom_call" | custom-call | flops 512 | bytes 512 | tf_op jit(solution)/shard_map/join/pallas_call | solution.py:324
  128.5 3.0 %join.4.rest_0_ = bf16[512,2048]{1,0:T(8,128)(2,1)} custom-call(s32[4]{0:T(128)} %compare_convert_fusion.ok_ref, f32[512,512]{1,0:T(8,128)} %get-tuple-element.40.mine_ref, f32[512,128]{1,0:T(8,128)} %get-tuple-element.33.refs_0_.l_ref, bf16[512,640]{1,0:T(8,128)(2,1)} %copy-done.15, bf16[512,640]{1,0:T(8,128)(2,1)} %copy-done.15, ...), custom_call_target="tpu_custom_call", output_to_operand_aliasing={{}: (6, {})} | custom-call | flops 512 | bytes 512 | tf_op jit(solution)/shard_map/join/pallas_call | solution.py:324
  131.5 5.7 %relayed.3.rest_0_ = bf16[512,2048]{1,0:T(8,128)(2,1)} custom-call(s32[4]{0:T(128)} %compare_convert_fusion.ok_ref, bf16[512,2048]{1,0:T(8,128)(2,1)} %q_ref.11, bf16[512,2048]{1,0:T(8,128)(2,1)} %ok.11, bf16[512,2048]{1,0:T(8,128)(2,1)} %ov.11, bf16[512,1536]{1,0:T(8,128)(2,1)} %collective-permute-done.z_ref.zk.zv, ...), custom_call_target="tpu_custom_call", output_to_operand_aliasing={{}: (12, {})} | custom-call | flops 1024 | bytes 512 | tf_op jit(solution)/shard_map/relayed/pallas_call | solution.py:253
  137.2 5.7 %relayed.4.rest_1_ = bf16[512,2048]{1,0:T(8,128)(2,1)} custom-call(s32[4]{0:T(128)} %compare_convert_fusion.ok_ref, bf16[512,2048]{1,0:T(8,128)(2,1)} %q_ref.11, bf16[512,2048]{1,0:T(8,128)(2,1)} %ok.11, bf16[512,2048]{1,0:T(8,128)(2,1)} %ov.11, bf16[512,1536]{1,0:T(8,128)(2,1)} %collective-permute-done.z_ref.zk.zv, ...), custom_call_target="tpu_custom_call", output_to_operand_aliasing={{}: (12, {})} | custom-call | flops 1024 | bytes 512 | tf_op jit(solution)/shard_map/relayed/pallas_call | solution.py:253
  142.9 3.0 %join.5.rest_0_ = bf16[512,2048]{1,0:T(8,128)(2,1)} custom-call(s32[4]{0:T(128)} %compare_convert_fusion.ok_ref, f32[512,512]{1,0:T(8,128)} %get-tuple-element.35.mine_ref, f32[512,128]{1,0:T(8,128)} %get-tuple-element.36.rest_0_.l_ref, bf16[512,640]{1,0:T(8,128)(2,1)} %collective-permute-done.16.got_ref.stat_ref, ...), custom_call_target="tpu_custom_call", output_to_operand_aliasing={{}: (6, {})} | custom-call | flops 512 | bytes 512 | tf_op jit(solution)/shard_map/join/pallas_call | solution.py:324
  145.9 5.7 %relayed.5 = bf16[512,2048]{1,0:T(8,128)(2,1)} custom-call(s32[4]{0:T(128)} %compare_convert_fusion.ok_ref, bf16[512,2048]{1,0:T(8,128)(2,1)} %q_ref.11, bf16[512,2048]{1,0:T(8,128)(2,1)} %ok.11, bf16[512,2048]{1,0:T(8,128)(2,1)} %ov.11, bf16[512,1536]{1,0:T(8,128)(2,1)} %collective-permute-done.z_ref.zk.zv, ...), custom_call_target="tpu_custom_call", output_to_operand_aliasing={{}: (12, {})} | custom-call | flops 1024 | bytes 512 | tf_op jit(solution)/shard_map/relayed/pallas_call | solution.py:253
  151.6 2.2 %copy-done.2 = f32[512,2048]{1,0:T(8,128)S(1)} copy-done((f32[512,2048]{1,0:T(8,128)S(1)}, f32[512,2048]{1,0:T(8,128)}, u32[]{:S(2)}) %copy-start.2) | copy-done | bytes 4194328
  153.8 7.7 %final.1 = bf16[512,2048]{1,0:T(8,128)(2,1)} custom-call(s32[1]{0:T(128)} %bitcast.6.core, f32[512,2048]{1,0:T(8,128)S(1)} %copy-done.2, f32[512,32]{1,0:T(8,128)S(1)} %copy-done.4, bf16[512,128]{1,0:T(8,128)(2,1)S(1)} %copy-done.9, f32[128,1024]{1,0:T(8,128)S(1)} %arrive.1.mine_ref, f32[128,1024]{1,0:T(8,128)S(1)} %collective-permute-done.26.theirs_ref, ...), custom_call_target="tpu_custom_call" | custom-call | flops 512 | bytes 512 | tf_op jit(solution)/shard_map/final/pallas_call | solution.py:599
  (84 shorter events, 8.0 us)
Async XLA Ops:
  0.6 5.4 %copy-start.10 = (bf16[512,2048]{1,0:T(8,128)(2,1)S(1)}, bf16[512,2048]{1,0:T(8,128)(2,1)}, u32[]{:S(2)}) copy-start(bf16[512,2048]{1,0:T(8,128)(2,1)} %ov.11) | copy-start | bytes 6291460
  0.6 41.1 %collective-permute-start.3 = (bf16[512,2048]{1,0:T(8,128)(2,1)}, bf16[512,2048]{1,0:T(8,128)(2,1)}, u32[]{:S(2)}, u32[]{:S(2)}) collective-permute-start(bf16[512,2048]{1,0:T(8,128)(2,1)} %ok.11), channel_id=1, source_target_pairs={{0,1},{1,0},{2,3},{3,2},{4,5},{5,4},{6,7},{7,6},{8,9},{9,8},{10,11... | collective-permute-start | bytes 6291464 | tf_op jit(solution)/shard_map/ppermute | solution.py:636
  1.4 44.2 %collective-permute-start.4 = (bf16[512,2048]{1,0:T(8,128)(2,1)}, bf16[512,2048]{1,0:T(8,128)(2,1)}, u32[]{:S(2)}, u32[]{:S(2)}) collective-permute-start(bf16[512,2048]{1,0:T(8,128)(2,1)} %ov.11), channel_id=1, source_target_pairs={{0,1},{1,0},{2,3},{3,2},{4,5},{5,4},{6,7},{7,6},{8,9},{9,8},{10,11... | collective-permute-start | bytes 6291464 | tf_op jit(solution)/shard_map/ppermute | solution.py:636
  3.5 13.1 %collective-permute-start.5 = (bf16[512,512]{1,0:T(8,128)(2,1)S(1)}, bf16[512,512]{1,0:T(8,128)(2,1)S(1)}, u32[]{:S(2)}, u32[]{:S(2)}) collective-permute-start(bf16[512,512]{1,0:T(8,128)(2,1)S(1)} %pad_maximum_fusion.3), channel_id=1, source_target_pairs={{0,2},{1,3},{2,0},{3,1},{4,6},{5,7},{6,4},{7,5},{8,10},{9,11},{10,... | collective-permute-start | bytes 1572872 | tf_op jit(solution)/shard_map/ppermute | solution.py:636
  7.3 32.1 %collective-permute-start.13 = (bf16[512,1024]{1,0:T(8,128)(2,1)}, bf16[512,1024]{1,0:T(8,128)(2,1)S(1)}, u32[]{:S(2)}, u32[]{:S(2)}) collective-permute-start(bf16[512,1024]{1,0:T(8,128)(2,1)} %pad_maximum_fusion.2), channel_id=1, source_target_pairs={{0,2},{1,3},{2,0},{3,1},{4,6},{5,7},{6,4},{7,5},{8,10},{9,11},{10,... | collective-permute-start | bytes 3145736 | tf_op jit(solution)/shard_map/ppermute | solution.py:636
  16.5 8.0 %copy-start.16 = (bf16[512,512]{1,0:T(8,128)(2,1)}, bf16[512,512]{1,0:T(8,128)(2,1)S(1)}, u32[]{:S(2)}) copy-start(bf16[512,512]{1,0:T(8,128)(2,1)S(1)} %collective-permute-done.5.yk.yv) | copy-start | bytes 1572868
  16.5 20.6 %collective-permute-start.6 = (bf16[512,512]{1,0:T(8,128)(2,1)S(1)}, bf16[512,512]{1,0:T(8,128)(2,1)S(1)}, u32[]{:S(2)}, u32[]{:S(2)}) collective-permute-start(bf16[512,512]{1,0:T(8,128)(2,1)S(1)} %collective-permute-done.5.yk.yv), channel_id=1, source_target_pairs={{0,1},{1,0},{2,3},{3,2},{4,5},{5,4},{6,7},{7,6},{8,9},{9,8},{10,11... | collective-permute-start | bytes 1572872 | tf_op jit(solution)/shard_map/ppermute | solution.py:636
  19.8 9.6 %collective-permute-start.2 = (bf16[512,256]{1,0:T(8,128)(2,1)S(1)}, bf16[512,256]{1,0:T(8,128)(2,1)S(1)}, u32[]{:S(2)}, u32[]{:S(2)}) collective-permute-start(bf16[512,256]{1,0:T(8,128)(2,1)S(1)} %slice.32), channel_id=1, source_target_pairs={{4,0},{5,1},{6,2},{7,3},{8,4},{9,5},{10,6},{11,7},{12,8},{13,9},{1... | collective-permute-start | bytes 786440 | tf_op jit(solution)/shard_map/ppermute | solution.py:636
  23.0 1.5 copy-start.12
  23.1 6.3 %copy-start.14 = (bf16[512,768]{1,0:T(8,128)(2,1)}, bf16[512,768]{1,0:T(8,128)(2,1)S(1)}, u32[]{:S(2)}) copy-start(bf16[512,768]{1,0:T(8,128)(2,1)S(1)} %slice.31) | copy-start | bytes 2359300
  29.4 10.0 %copy-start.19 = (bf16[512,256]{1,0:T(8,128)(2,1)}, bf16[512,256]{1,0:T(8,128)(2,1)S(1)}, u32[]{:S(2)}) copy-start(bf16[512,256]{1,0:T(8,128)(2,1)S(1)} %collective-permute-done.2.n_ref) | copy-start | bytes 786436
  29.4 37.1 %collective-permute-start = (bf16[512,1536]{1,0:T(8,128)(2,1)}, bf16[512,1536]{1,0:T(8,128)(2,1)}, u32[]{:S(2)}, u32[]{:S(2)}) collective-permute-start(bf16[512,1536]{1,0:T(8,128)(2,1)} %pad_maximum_fusion.own_ref), channel_id=1, source_target_pairs={{0,4},{1,5},{2,6},{3,7},{4,8},{5,9},{6,10},{7,11},{8,12},{9,13},{1... | collective-permute-start | bytes 4718600 | tf_op jit(solution)/shard_map/ppermute | solution.py:636
  37.1 3.5 %copy-start.11 = (bf16[512,2048]{1,0:T(8,128)(2,1)S(1)}, bf16[512,2048]{1,0:T(8,128)(2,1)}, u32[]{:S(2)}) copy-start(bf16[512,2048]{1,0:T(8,128)(2,1)} %q_ref.11) | copy-start | bytes 6291460
  37.1 4.6 %copy-start.17 = (bf16[512,512]{1,0:T(8,128)(2,1)}, bf16[512,512]{1,0:T(8,128)(2,1)S(1)}, u32[]{:S(2)}) copy-start(bf16[512,512]{1,0:T(8,128)(2,1)S(1)} %collective-permute-done.6.bk.bv) | copy-start | bytes 1572868
  37.1 25.1 %collective-permute-start.12 = (f32[136,2048]{1,0:T(8,128)}, f32[136,2048]{1,0:T(8,128)S(1)}, u32[]{:S(2)}, u32[]{:S(2)}) collective-permute-start(f32[136,2048]{1,0:T(8,128)} %get-tuple-element.30.both_ref), channel_id=1, source_target_pairs={{0,1},{1,0},{2,3},{3,2},{4,5},{5,4},{6,7},{7,6},{8,9},{9,8},{10,11... | collective-permute-start | bytes 3342344 | tf_op jit(solution)/shard_map/ppermute | solution.py:636
  39.4 22.9 %copy-start = (bf16[512,1024]{1,0:T(8,128)(2,1)}, bf16[512,1024]{1,0:T(8,128)(2,1)S(1)}, u32[]{:S(2)}) copy-start(bf16[512,1024]{1,0:T(8,128)(2,1)S(1)} %collective-permute-done.13.refs_1_.yk.yv) | copy-start | bytes 3145732
  39.4 26.0 %collective-permute-start.10 = (bf16[512,1024]{1,0:T(8,128)(2,1)}, bf16[512,1024]{1,0:T(8,128)(2,1)}, u32[]{:S(2)}, u32[]{:S(2)}) collective-permute-start(bf16[512,1024]{1,0:T(8,128)(2,1)} %pad_maximum_fusion.1), channel_id=1, source_target_pairs={{0,2},{1,3},{2,0},{3,1},{4,6},{5,7},{6,4},{7,5},{8,10},{9,11},{10,... | collective-permute-start | bytes 3145736 | tf_op jit(solution)/shard_map/ppermute | solution.py:636
  41.8 28.8 %collective-permute-start.9 = (bf16[512,1024]{1,0:T(8,128)(2,1)}, bf16[512,1024]{1,0:T(8,128)(2,1)}, u32[]{:S(2)}, u32[]{:S(2)}) collective-permute-start(bf16[512,1024]{1,0:T(8,128)(2,1)} %slice.35), channel_id=1, source_target_pairs={{4,0},{5,1},{6,2},{7,3},{8,4},{9,5},{10,6},{11,7},{12,8},{13,9},{1... | collective-permute-start | bytes 3145736 | tf_op jit(solution)/shard_map/ppermute | solution.py:636
  45.6 25.0 %collective-permute-start.15 = (bf16[512,1024]{1,0:T(8,128)(2,1)S(1)}, bf16[512,1024]{1,0:T(8,128)(2,1)}, u32[]{:S(2)}, u32[]{:S(2)}) collective-permute-start(bf16[512,1024]{1,0:T(8,128)(2,1)S(1)} %collective-permute-done.13.refs_1_.yk.yv), channel_id=1, source_target_pairs={{0,1},{1,0},{2,3},{3,2},{4,5},{5,4},{6,7},{7,6},{8,9},{9,8},{10,11... | collective-permute-start | bytes 3145736 | tf_op jit(solution)/shard_map/ppermute | solution.py:636
  53.1 9.2 %copy-start.7 = (f32[136,2048]{1,0:T(8,128)S(1)}, f32[136,2048]{1,0:T(8,128)}, u32[]{:S(2)}) copy-start(f32[136,2048]{1,0:T(8,128)} %get-tuple-element.30.both_ref) | copy-start | bytes 3342340
  62.2 1.0 copy-start.3
  64.8 15.9 %collective-permute-start.14 = (bf16[144,1024]{1,0:T(8,128)(2,1)}, bf16[144,1024]{1,0:T(8,128)(2,1)S(1)}, u32[]{:S(2)}, u32[]{:S(2)}) collective-permute-start(bf16[144,1024]{1,0:T(8,128)(2,1)} %get-tuple-element.32), channel_id=1, source_target_pairs={{0,2},{1,3},{2,0},{3,1},{4,6},{5,7},{6,4},{7,5},{8,10},{9,11},{10,... | collective-permute-start | bytes 884744 | tf_op jit(solution)/shard_map/ppermute | solution.py:636
  65.4 24.8 %collective-permute-start.11 = (bf16[512,1024]{1,0:T(8,128)(2,1)}, bf16[512,1024]{1,0:T(8,128)(2,1)}, u32[]{:S(2)}, u32[]{:S(2)}) collective-permute-start(bf16[512,1024]{1,0:T(8,128)(2,1)} %collective-permute-done.10.yk.yv), channel_id=1, source_target_pairs={{0,1},{1,0},{2,3},{3,2},{4,5},{5,4},{6,7},{7,6},{8,9},{9,8},{10,11... | collective-permute-start | bytes 3145736 | tf_op jit(solution)/shard_map/ppermute | solution.py:636
  69.3 31.2 %collective-permute-start.19 = (bf16[512,512]{1,0:T(8,128)(2,1)}, bf16[512,512]{1,0:T(8,128)(2,1)}, u32[]{:S(2)}, u32[]{:S(2)}) collective-permute-start(bf16[512,512]{1,0:T(8,128)(2,1)} %get-tuple-element.39), channel_id=1, source_target_pairs={{0,2},{1,3},{2,0},{3,1},{4,6},{5,7},{6,4},{7,5},{8,10},{9,11},{10,... | collective-permute-start | bytes 1572872 | tf_op jit(solution)/shard_map/ppermute | solution.py:636
  70.5 10.2 %copy-start.6 = (f32[136,1024]{1,0:T(8,128)S(1)}, f32[136,1024]{1,0:T(8,128)}, u32[]{:S(2)}) copy-start(f32[136,1024]{1,0:T(8,128)} %copy-done.5) | copy-start | bytes 1671172
  70.6 12.1 %copy-start.13 = (bf16[512,768]{1,0:T(8,128)(2,1)S(1)}, bf16[512,768]{1,0:T(8,128)(2,1)}, u32[]{:S(2)}) copy-start(bf16[512,768]{1,0:T(8,128)(2,1)} %copy-done.12) | copy-start | bytes 2359300
  80.8 1.0 copy-start.8
  81.8 25.1 %copy-start.1 = (f32[136,1024]{1,0:T(8,128)}, f32[136,1024]{1,0:T(8,128)S(1)}, u32[]{:S(2)}) copy-start(f32[136,1024]{1,0:T(8,128)S(1)} %get-tuple-element.34._.plane_ref) | copy-start | bytes 1671172
  81.9 5.7 %copy-start.21 = (bf16[512,384]{1,0:T(8,128)(2,1)S(1)}, bf16[512,384]{1,0:T(8,128)(2,1)}, u32[]{:S(2)}) copy-start(bf16[512,384]{1,0:T(8,128)(2,1)} %get-tuple-element.43) | copy-start | bytes 1179652
  81.9 7.8 %copy-start.20 = (bf16[512,512]{1,0:T(8,128)(2,1)S(1)}, bf16[512,512]{1,0:T(8,128)(2,1)}, u32[]{:S(2)}) copy-start(bf16[512,512]{1,0:T(8,128)(2,1)} %get-tuple-element.38) | copy-start | bytes 1572868
  81.9 7.8 %collective-permute-start.23 = (bf16[128,1024]{1,0:T(8,128)(2,1)S(1)}, bf16[128,1024]{1,0:T(8,128)(2,1)S(1)}, u32[]{:S(2)}, u32[]{:S(2)}) collective-permute-start(bf16[128,1024]{1,0:T(8,128)(2,1)S(1)} %get-tuple-element.45), channel_id=1, source_target_pairs={{0,4},{1,5},{2,6},{3,7},{16,20},{17,21},{18,22},{19,23}} | collective-permute-start | bytes 786440 | tf_op jit(solution)/shard_map/ppermute | solution.py:636
  85.8 45.7 %collective-permute-start.1 = (bf16[512,1536]{1,0:T(8,128)(2,1)}, bf16[512,1536]{1,0:T(8,128)(2,1)}, u32[]{:S(2)}, u32[]{:S(2)}) collective-permute-start(bf16[512,1536]{1,0:T(8,128)(2,1)} %broadcast_select_fusion), channel_id=1, source_target_pairs={{0,1},{1,0},{2,3},{3,2},{4,5},{5,4},{6,7},{7,6},{8,9},{9,8},{10,11... | collective-permute-start | bytes 4718600 | tf_op jit(solution)/shard_map/ppermute | solution.py:636
  87.6 12.7 %collective-permute-start.22 = (bf16[512,384]{1,0:T(8,128)(2,1)S(1)}, bf16[512,384]{1,0:T(8,128)(2,1)S(1)}, u32[]{:S(2)}, u32[]{:S(2)}) collective-permute-start(bf16[512,384]{1,0:T(8,128)(2,1)S(1)} %copy-done.21), channel_id=1, source_target_pairs={{0,4},{1,5},{2,6},{3,7},{4,8},{5,9},{6,10},{7,11},{8,12},{9,13},{1... | collective-permute-start | bytes 1179656 | tf_op jit(solution)/shard_map/ppermute | solution.py:636
  89.7 17.4 %collective-permute-start.17 = (bf16[512,512]{1,0:T(8,128)(2,1)S(1)}, bf16[512,512]{1,0:T(8,128)(2,1)}, u32[]{:S(2)}, u32[]{:S(2)}) collective-permute-start(bf16[512,512]{1,0:T(8,128)(2,1)S(1)} %copy-done.20), channel_id=1, source_target_pairs={{0,2},{1,3},{2,0},{3,1},{4,6},{5,7},{6,4},{7,5},{8,10},{9,11},{10,... | collective-permute-start | bytes 1572872 | tf_op jit(solution)/shard_map/ppermute | solution.py:636
  90.2 15.7 %collective-permute-start.24 = (bf16[128,1024]{1,0:T(8,128)(2,1)S(1)}, bf16[128,1024]{1,0:T(8,128)(2,1)S(1)}, u32[]{:S(2)}, u32[]{:S(2)}) collective-permute-start(bf16[128,1024]{1,0:T(8,128)(2,1)S(1)} %get-tuple-element.47), channel_id=1, source_target_pairs={{4,8},{5,9},{6,10},{7,11},{20,24},{21,25},{22,26},{23,27}} | collective-permute-start | bytes 786440 | tf_op jit(solution)/shard_map/ppermute | solution.py:636
  100.3 18.2 %copy-start.18 = (bf16[512,384]{1,0:T(8,128)(2,1)}, bf16[512,384]{1,0:T(8,128)(2,1)S(1)}, u32[]{:S(2)}) copy-start(bf16[512,384]{1,0:T(8,128)(2,1)S(1)} %collective-permute-done.22.got_ref.stat_ref) | copy-start | bytes 1179652
  100.3 18.3 %collective-permute-start.7 = (bf16[512,512]{1,0:T(8,128)(2,1)}, bf16[512,512]{1,0:T(8,128)(2,1)}, u32[]{:S(2)}, u32[]{:S(2)}) collective-permute-start(bf16[512,512]{1,0:T(8,128)(2,1)} %get-tuple-element.29), channel_id=1, source_target_pairs={{0,2},{1,3},{2,0},{3,1},{4,6},{5,7},{6,4},{7,5},{8,10},{9,11},{10,... | collective-permute-start | bytes 1572872 | tf_op jit(solution)/shard_map/ppermute | solution.py:636
  100.5 24.4 %collective-permute-start.21 = (bf16[512,640]{1,0:T(8,128)(2,1)}, bf16[512,640]{1,0:T(8,128)(2,1)S(1)}, u32[]{:S(2)}, u32[]{:S(2)}) collective-permute-start(bf16[512,640]{1,0:T(8,128)(2,1)} %get-tuple-element.41), channel_id=1, source_target_pairs={{0,4},{1,5},{2,6},{3,7},{4,8},{5,9},{6,10},{7,11},{8,12},{9,13},{1... | collective-permute-start | bytes 1966088 | tf_op jit(solution)/shard_map/ppermute | solution.py:636
  105.9 19.1 %collective-permute-start.20 = (bf16[512,512]{1,0:T(8,128)(2,1)}, bf16[512,512]{1,0:T(8,128)(2,1)}, u32[]{:S(2)}, u32[]{:S(2)}) collective-permute-start(bf16[512,512]{1,0:T(8,128)(2,1)} %collective-permute-done.19.yk.yv), channel_id=1, source_target_pairs={{0,1},{1,0},{2,3},{3,2},{4,5},{5,4},{6,7},{7,6},{8,9},{9,8},{10,11... | collective-permute-start | bytes 1572872 | tf_op jit(solution)/shard_map/ppermute | solution.py:636
  107.1 14.1 %collective-permute-start.25 = (bf16[128,1024]{1,0:T(8,128)(2,1)S(1)}, bf16[128,1024]{1,0:T(8,128)(2,1)S(1)}, u32[]{:S(2)}, u32[]{:S(2)}) collective-permute-start(bf16[128,1024]{1,0:T(8,128)(2,1)S(1)} %get-tuple-element.49), channel_id=1, source_target_pairs={{8,12},{9,13},{10,14},{11,15},{24,28},{25,29},{26,30},{27,31}} | collective-permute-start | bytes 786440 | tf_op jit(solution)/shard_map/ppermute | solution.py:636
  118.6 24.3 %collective-permute-start.16 = (bf16[512,640]{1,0:T(8,128)(2,1)}, bf16[512,640]{1,0:T(8,128)(2,1)}, u32[]{:S(2)}, u32[]{:S(2)}) collective-permute-start(bf16[512,640]{1,0:T(8,128)(2,1)} %get-tuple-element.37), channel_id=1, source_target_pairs={{0,4},{1,5},{2,6},{3,7},{4,8},{5,9},{6,10},{7,11},{8,12},{9,13},{1... | collective-permute-start | bytes 1966088 | tf_op jit(solution)/shard_map/ppermute | solution.py:636
  121.2 16.0 %collective-permute-start.18 = (bf16[512,512]{1,0:T(8,128)(2,1)}, bf16[512,512]{1,0:T(8,128)(2,1)}, u32[]{:S(2)}, u32[]{:S(2)}) collective-permute-start(bf16[512,512]{1,0:T(8,128)(2,1)} %collective-permute-done.17.yk.yv), channel_id=1, source_target_pairs={{0,1},{1,0},{2,3},{3,2},{4,5},{5,4},{6,7},{7,6},{8,9},{9,8},{10,11... | collective-permute-start | bytes 1572872 | tf_op jit(solution)/shard_map/ppermute | solution.py:636
  124.9 3.6 %copy-start.15 = (bf16[512,640]{1,0:T(8,128)(2,1)}, bf16[512,640]{1,0:T(8,128)(2,1)S(1)}, u32[]{:S(2)}) copy-start(bf16[512,640]{1,0:T(8,128)(2,1)S(1)} %collective-permute-done.21.got_ref.stat_ref) | copy-start | bytes 1966084
  124.9 21.0 %collective-permute-start.8 = (bf16[512,512]{1,0:T(8,128)(2,1)}, bf16[512,512]{1,0:T(8,128)(2,1)}, u32[]{:S(2)}, u32[]{:S(2)}) collective-permute-start(bf16[512,512]{1,0:T(8,128)(2,1)} %collective-permute-done.7.yk.yv), channel_id=1, source_target_pairs={{0,1},{1,0},{2,3},{3,2},{4,5},{5,4},{6,7},{7,6},{8,9},{9,8},{10,11... | collective-permute-start | bytes 1572872 | tf_op jit(solution)/shard_map/ppermute | solution.py:636
  125.0 26.6 %collective-permute-start.26 = (f32[128,1024]{1,0:T(8,128)S(1)}, f32[128,1024]{1,0:T(8,128)S(1)}, u32[]{:S(2)}, u32[]{:S(2)}) collective-permute-start(f32[128,1024]{1,0:T(8,128)S(1)} %arrive.1.mine_ref), channel_id=1, source_target_pairs={{0,1},{1,0},{2,3},{3,2},{4,5},{5,4},{6,7},{7,6},{8,9},{9,8},{10,11... | collective-permute-start | bytes 1572872 | tf_op jit(solution)/shard_map/ppermute | solution.py:636
  145.9 5.7 %copy-start.4 = (f32[512,32]{1,0:T(8,128)S(1)}, f32[512,32]{1,0:T(8,128)}, u32[]{:S(2)}) copy-start(f32[512,32]{1,0:T(8,128)} %get-tuple-element.28._.refs_0_.factor_ref) | copy-start | bytes 196612
  145.9 5.7 %copy-start.9 = (bf16[512,128]{1,0:T(8,128)(2,1)S(1)}, bf16[512,128]{1,0:T(8,128)(2,1)}, u32[]{:S(2)}) copy-start(bf16[512,128]{1,0:T(8,128)(2,1)} %c_ref.3) | copy-start | bytes 393220
  151.6 2.2 %copy-start.2 = (f32[512,2048]{1,0:T(8,128)S(1)}, f32[512,2048]{1,0:T(8,128)}, u32[]{:S(2)}) copy-start(f32[512,2048]{1,0:T(8,128)} %get-tuple-element.44.pre_ref) | copy-start | bytes 12582916
  (1 other events, 0.8 us)
